TPU v7x, 128 devices: a whole 4x4x4 slice. The times are simulated.
128 devices in a mesh: fsdp: 32 (over x, z, core), rep: 4 (over y).
Axes of the slice: x: 4, y: 4, z: 4, core: 2. Of those that a mesh axis runs over, the one named last changes fastest.
Arguments:
- grads: bfloat16 [64, 1024, 1024], P(None, 'fsdp', 'rep'), may hold values from -1.7 to 1.7
- owner_slot: int32 [64], replicated, may hold values from 0 to 63, each once
- gram_left: float32 [64, 1024, 1024], P('fsdp', 'rep'), may hold values from -1.2 to 1.2
- gram_right: float32 [64, 1024, 1024], P('fsdp', 'rep'), may hold values from -1.2 to 1.2
- root_left: bfloat16 [64, 1024, 1024], P('fsdp', 'rep'), may hold values from -0.6 to 2.6
- root_right: bfloat16 [64, 1024, 1024], P('fsdp'), may hold values from -0.6 to 2.6
- moment: float32 [64, 1024, 1024], P('fsdp', 'rep'), may hold values from -0.18 to 0.18
- second: float32 [64, 1024, 1024], P('fsdp', 'rep'), may hold values from 0.0001 to 0.01
Outputs:
- updates: bfloat16 [64, 1024, 1024], P(None, 'fsdp', 'rep')
- gram_left_new: float32 [64, 1024, 1024], P('fsdp', 'rep')
- gram_right_new: float32 [64, 1024, 1024], P('fsdp', 'rep')
- moment_new: float32 [64, 1024, 1024], P('fsdp', 'rep')
- second_new: float32 [64, 1024, 1024], P('fsdp', 'rep')
Inputs may be any that keep to these rules, and one draw needn't show every extreme that they name: `owner_slot`: each slot is named by exactly one block.
All inputs are finite; a program needn't handle non-finite values.
Results may differ from a plain program's by a relative error of at most 0.0049.
Values may be sent and summed in bfloat16 or wider, within the bound.
No kernel may reach another device: no remote copies, remote signals or barrier semaphores. Data moves between devices by JAX's collectives and lax.ppermute only.
A program may use at most 128 MiB of HBM per device.

v0:
```python
import jax
import jax.numpy as jnp
from jax import lax
from jax.sharding import PartitionSpec as P


def per_device(grads, owner_slot, gram_left, gram_right, root_left, root_right, moment, second):
    owners = lax.axis_size("fsdp")
    replicas = lax.axis_size("rep")
    blocks = owner_slot.shape[0]
    per_owner = blocks // owners
    block_size = root_right.shape[1]
    quarter = block_size // replicas
    slot_ids = jnp.arange(blocks, dtype=jnp.int32)
    matches = owner_slot[:, None] == slot_ids[None, :]
    block_of_slot = jnp.sum(jnp.where(matches, slot_ids[:, None], 0), axis=0)
    ordered = grads[block_of_slot]
    row_part = ordered.shape[1]
    col_part = ordered.shape[2]
    copies = jnp.broadcast_to(
        ordered.reshape(owners, 1, per_owner, row_part, col_part),
        (owners, replicas, per_owner, row_part, col_part),
    ).reshape(owners * replicas * per_owner, row_part, col_part)
    arrived = lax.all_to_all(copies, ("fsdp", "rep"), split_axis=0, concat_axis=1, tiled=True)
    arrived = arrived.reshape(per_owner, owners, replicas, row_part, col_part)
    whole_grad = jnp.transpose(arrived, (0, 1, 3, 2, 4)).reshape(per_owner, block_size, block_size)
    rep_index = lax.axis_index("rep")
    first_row = rep_index * quarter
    grad_rows = lax.dynamic_slice_in_dim(whole_grad, first_row, quarter, 1)
    grad_cols = lax.dynamic_slice_in_dim(whole_grad, first_row, quarter, 2)
    left_new = 0.95 * gram_left + 0.05 * jnp.einsum(
        "nik,njk->nij", grad_rows, whole_grad, preferred_element_type=jnp.float32
    )
    right_new = 0.95 * gram_right + 0.05 * jnp.einsum(
        "nki,nkj->nij", grad_cols, whole_grad, preferred_element_type=jnp.float32
    )
    product = jnp.einsum(
        "nik,nkj->nij", whole_grad, root_right, preferred_element_type=jnp.float32
    ).astype(jnp.bfloat16)
    precond = jnp.einsum("nik,nkj->nij", root_left, product, preferred_element_type=jnp.float32)
    grad_float = grad_rows.astype(jnp.float32)
    moment_new = 0.9 * moment + 0.1 * grad_float
    second_new = 0.95 * second + 0.05 * grad_float * grad_float
    adam_dir = moment_new / (jnp.sqrt(second_new) + 1e-08)
    adam_sq = jnp.sum(adam_dir * adam_dir, axis=(1, 2))
    pre_sq = jnp.sum(precond * precond, axis=(1, 2))
    adam_all, pre_all = lax.psum((adam_sq, pre_sq), "rep")
    cells = float(block_size * block_size)
    ratio = jnp.sqrt(adam_all / cells + 1e-06) / jnp.sqrt(pre_all / cells + 1e-06)
    grafted = (precond * ratio[:, None, None]).astype(jnp.bfloat16)
    homed = lax.all_to_all(
        lax.all_to_all(grafted, "rep", split_axis=2, concat_axis=1, tiled=True),
        "fsdp",
        split_axis=1,
        concat_axis=0,
        tiled=True,
    )
    updates = homed[owner_slot]
    return (updates, left_new, right_new, moment_new, second_new)


def solution(mesh):
    return jax.shard_map(
        per_device,
        mesh=mesh,
        in_specs=(
            P(None, "fsdp", "rep"),
            P(),
            P("fsdp", "rep", None),
            P("fsdp", "rep", None),
            P("fsdp", "rep", None),
            P("fsdp", None, None),
            P("fsdp", "rep", None),
            P("fsdp", "rep", None),
        ),
        out_specs=(
            P(None, "fsdp", "rep"),
            P("fsdp", "rep", None),
            P("fsdp", "rep", None),
            P("fsdp", "rep", None),
            P("fsdp", "rep", None),
        ),
        check_vma=False,
    )
```

profile of v0, /device:TPU:1, one launch (start us, length us, event | category | flops | bytes accessed | tf_op | source)
XLA Modules:
  0.0 162.9 jit_solution(14528776825637400498)
XLA Ops:
  0.6 0.0 copy-start
  0.6 0.8 select_reduce_fusion
  1.5 1.8 %gather_fusion = bf16[64,32,256]{2,1,0:T(8,128)(2,1)S(1)} fusion(bf16[64,32,256]{2,1,0:T(8,128)(2,1)} %param.8, s32[1024]{0:T(1024)S(1)} %pad_clamp_fusion.1), kind=kCustom, calls=%fused_computation | custom fusion | bytes 2097408 | tf_op jit(solution)/shard_map/gather | solution.py:17
  3.3 2.5 %broadcast_in_dim.30 = bf16[32,4,2,32,256]{4,3,2,1,0:T(8,128)(2,1)} broadcast(bf16[32,2,32,256]{3,2,1,0:T(8,128)(2,1)S(1)} %bitcast.29), dimensions={0,2,3,4} | broadcast | bytes 5242880 | tf_op jit(solution)/shard_map/broadcast_in_dim | solution.py:20
  5.9 12.0 %all-to-all-start = ((bf16[256,32,256]{2,1,0:T(8,128)(2,1)}), bf16[256,32,256]{2,1,0:T(8,128)(2,1)}, u32[]{:S(2)}, u32[]{:S(2)}) async-start(bf16[256,32,256]{2,1,0:T(8,128)(2,1)} %bitcast.28), calls=%async_computation | async-start | bytes 8388608 | tf_op jit(solution)/shard_map/all_to_all | solution.py:24
  17.8 53.1 %all-to-all-done = bf16[256,32,256]{2,1,0:T(8,128)(2,1)} async-done(((bf16[256,32,256]{2,1,0:T(8,128)(2,1)}), bf16[256,32,256]{2,1,0:T(8,128)(2,1)}, u32[]{:S(2)}, u32[]{:S(2)}) %all-to-all-start) | async-done | bytes 4194336 | tf_op jit(solution)/shard_map/all_to_all | solution.py:24
  70.9 12.5 %copy.41 = bf16[2,32,32,4,256]{4,3,2,1,0:T(4,128)(2,1)} copy(bf16[2,32,32,4,256]{4,2,0,3,1:T(8,128)(2,1)} %bitcast.8) | data formatting | bytes 8388608 | tf_op jit(solution)/shard_map/transpose | solution.py:26
  83.4 7.7 %reshape.39 = bf16[2,1024,1024]{2,1,0:T(8,128)(2,1)} reshape(bf16[2,32,32,4,256]{4,3,2,1,0:T(4,128)(2,1)} %copy.41) | data formatting | bytes 8388608 | tf_op jit(solution)/shard_map/reshape | solution.py:26
  91.1 0.0 copy-done
  91.1 11.0 %multiply_reduce_fusion = (f32[2]{0:T(128)S(1)}, f32[2,1024,256]{2,1,0:T(8,128)}) fusion(bf16[2,256,1024]{2,1,0:T(8,128)(2,1)S(1)} %copy-done, bf16[2,1024,1024]{2,1,0:T(8,128)(2,1)} %reshape.39, bf16[2,1024,1024]{2,1,0:T(8,128)(2,1)} %param.13), kind=kOutput, calls=%fused_computation.11 | convolution fusion | flops 5371854848 | bytes 11534344 | tf_op jit(solution)/shard_map/nik,nkj->nij/dot_general | solution.py:40
  102.1 0.0 copy-done.2
  102.1 5.3 %multiply_reduce_fusion.1 = (f32[2]{0:T(128)S(1)}, f32[2,256,1024]{2,1,0:T(8,128)}, f32[2,256,1024]{2,1,0:T(8,128)}) fusion(bf16[2,1024,1024]{2,1,0:T(8,128)(2,1)} %reshape.39, s32[]{:T(128)S(6)} %select_n.23, f32[2,256,1024]{2,1,0:T(8,128)S(1)} %copy-done.2, f32[2,256,1024]{2,1,0:T(8,128)} %param.14), kind=kLoop, calls=%fused_computation.12 | loop fusion | flops 6291454 | bytes 9437196 | tf_op jit(solution)/shard_map/reduce_sum | solution.py:45
  107.4 6.4 %all-reduce = (f32[2]{0:T(128)S(1)}, f32[2]{0:T(128)S(1)}) all-reduce(f32[2]{0:T(128)S(1)} %get-tuple-element.10, f32[2]{0:T(128)S(1)} %get-tuple-element.7), channel_id=1, replica_groups=mesh['fsdp'=32,'rep'=4] {'rep'}, use_global_device_ids=true, to_apply=%region_4.5 | all-reduce | flops 4 | bytes 32 | tf_op jit(solution)/shard_map/psum | solution.py:47
  113.8 1.8 %fusion.6 = bf16[2,256,1024]{1,2,0:T(8,128)(2,1)S(1)} fusion(f32[2,1024,256]{2,1,0:T(8,128)} %get-tuple-element.11, f32[2]{0:T(128)S(1)} %rsqrt_multiply_fusion), kind=kLoop, calls=%fused_computation.14 | loop fusion | flops 1048576 | bytes 3145736 | tf_op jit(solution)/shard_map/convert_element_type | solution.py:50
  115.6 0.0 copy-start.4
  115.6 2.0 %copy.43 = bf16[2,256,1024]{1,0,2:T(2,128)(2,1)} copy(bf16[2,256,1024]{1,2,0:T(8,128)(2,1)S(1)} %fusion.6) | data formatting | bytes 2097152 | tf_op jit(solution)/shard_map/convert_element_type | solution.py:50
  117.7 3.5 %all-to-all-start.1 = ((bf16[2,256,1024]{1,0,2:T(2,128)(2,1)}), bf16[2,256,1024]{1,0,2:T(2,128)(2,1)S(1)}, u32[]{:S(2)}, u32[]{:S(2)}) async-start(bf16[2,256,1024]{1,0,2:T(2,128)(2,1)} %copy.43), calls=%async_computation.1 | async-start | bytes 2097152 | tf_op jit(solution)/shard_map/all_to_all | solution.py:52
  121.2 0.0 copy-done.4
  121.2 11.6 %all-to-all-done.1 = bf16[2,256,1024]{1,0,2:T(2,128)(2,1)S(1)} async-done(((bf16[2,256,1024]{1,0,2:T(2,128)(2,1)}), bf16[2,256,1024]{1,0,2:T(2,128)(2,1)S(1)}, u32[]{:S(2)}, u32[]{:S(2)}) %all-to-all-start.1) | async-done | bytes 1048608 | tf_op jit(solution)/shard_map/all_to_all | solution.py:52
  132.8 0.1 copy.44
  133.0 0.5 copy.45
  133.5 2.0 %copy.46 = bf16[2,1024,256]{2,0,1:T(2,128)(2,1)} copy(bf16[2,1024,256]{2,1,0:T(8,128)(2,1)S(1)} %bitcast.32) | data formatting | bytes 2097152 | tf_op jit(solution)/shard_map/all_to_all | solution.py:52
  135.6 8.6 %all-to-all-start.2 = ((bf16[2,1024,256]{2,0,1:T(2,128)(2,1)}), bf16[2,1024,256]{2,0,1:T(2,128)(2,1)S(1)}, u32[]{:S(2)}, u32[]{:S(2)}) async-start(bf16[2,1024,256]{2,0,1:T(2,128)(2,1)} %copy.46), calls=%async_computation.2 | async-start | bytes 2097152 | tf_op jit(solution)/shard_map/all_to_all | solution.py:51
  144.2 0.0 copy-start.1
  144.2 0.0 copy-start.3
  144.2 6.1 %multiply_add_fusion = f32[2,256,1024]{2,1,0:T(8,128)} fusion(f32[2,256,1024]{2,1,0:T(8,128)} %param.11, bf16[2,1024,1024]{2,1,0:T(8,128)(2,1)} %reshape.39, s32[]{:T(128)S(6)} %select_n.23), kind=kOutput, calls=%fused_computation.8 | convolution fusion | flops 1075314688 | bytes 9437188 | tf_op jit(solution)/shard_map/nki,nkj->nij/dot_general | solution.py:34
  150.4 0.0 copy-done.1
  150.4 2.8 %multiply_add_fusion.1 = f32[2,256,1024]{2,1,0:T(8,128)} fusion(f32[2,256,1024]{2,1,0:T(8,128)S(1)} %copy-done.3, bf16[2,1024,1024]{2,1,0:T(8,128)(2,1)S(1)} %copy-done.1, s32[]{:T(128)S(6)} %select_n.23), kind=kOutput, calls=%fused_computation.9 | convolution fusion | flops 1075314688 | bytes 9437188 | tf_op jit(solution)/shard_map/nik,njk->nij/dot_general | solution.py:31
  153.1 8.0 %all-to-all-done.2 = bf16[2,1024,256]{2,0,1:T(2,128)(2,1)S(1)} async-done(((bf16[2,1024,256]{2,0,1:T(2,128)(2,1)}), bf16[2,1024,256]{2,0,1:T(2,128)(2,1)S(1)}, u32[]{:S(2)}, u32[]{:S(2)}) %all-to-all-start.2) | async-done | bytes 1048608 | tf_op jit(solution)/shard_map/all_to_all | solution.py:51
  161.1 0.1 copy.47
  161.3 0.1 copy.48
  161.4 1.6 gather_fusion.1
  (7 shorter events, 0.0 us)
Async XLA Ops:
  0.6 90.5 %copy-start = (bf16[2,256,1024]{2,1,0:T(8,128)(2,1)S(1)}, bf16[2,256,1024]{2,1,0:T(8,128)(2,1)}, u32[]{:S(2)}) copy-start(bf16[2,256,1024]{2,1,0:T(8,128)(2,1)} %param.12) | copy-start | bytes 3145732
  5.9 65.1 %all-to-all-start = ((bf16[256,32,256]{2,1,0:T(8,128)(2,1)}), bf16[256,32,256]{2,1,0:T(8,128)(2,1)}, u32[]{:S(2)}, u32[]{:S(2)}) async-start(bf16[256,32,256]{2,1,0:T(8,128)(2,1)} %bitcast.28), calls=%async_computation | async-start | bytes 8388608 | tf_op jit(solution)/shard_map/all_to_all | solution.py:24
  91.1 11.0 %copy-start.2 = (f32[2,256,1024]{2,1,0:T(8,128)S(1)}, f32[2,256,1024]{2,1,0:T(8,128)}, u32[]{:S(2)}) copy-start(f32[2,256,1024]{2,1,0:T(8,128)} %param.15) | copy-start | bytes 6291460
  115.6 5.6 %copy-start.4 = (s32[64]{0:T(128)S(1)}, s32[64]{0:T(128)}, u32[]{:S(2)}) copy-start(s32[64]{0:T(128)} %param.9) | copy-start | bytes 772
  117.7 15.2 %all-to-all-start.1 = ((bf16[2,256,1024]{1,0,2:T(2,128)(2,1)}), bf16[2,256,1024]{1,0,2:T(2,128)(2,1)S(1)}, u32[]{:S(2)}, u32[]{:S(2)}) async-start(bf16[2,256,1024]{1,0,2:T(2,128)(2,1)} %copy.43), calls=%async_computation.1 | async-start | bytes 2097152 | tf_op jit(solution)/shard_map/all_to_all | solution.py:52
  135.6 25.6 %all-to-all-start.2 = ((bf16[2,1024,256]{2,0,1:T(2,128)(2,1)}), bf16[2,1024,256]{2,0,1:T(2,128)(2,1)S(1)}, u32[]{:S(2)}, u32[]{:S(2)}) async-start(bf16[2,1024,256]{2,0,1:T(2,128)(2,1)} %copy.46), calls=%async_computation.2 | async-start | bytes 2097152 | tf_op jit(solution)/shard_map/all_to_all | solution.py:51
  144.2 6.1 %copy-start.1 = (bf16[2,1024,1024]{2,1,0:T(8,128)(2,1)S(1)}, bf16[2,1024,1024]{2,1,0:T(8,128)(2,1)}, u32[]{:S(2)}) copy-start(bf16[2,1024,1024]{2,1,0:T(8,128)(2,1)} %reshape.39) | copy-start | bytes 12582916
  144.2 6.1 %copy-start.3 = (f32[2,256,1024]{2,1,0:T(8,128)S(1)}, f32[2,256,1024]{2,1,0:T(8,128)}, u32[]{:S(2)}) copy-start(f32[2,256,1024]{2,1,0:T(8,128)} %param.10) | copy-start | bytes 6291460
where the time goes:
time: 164 us; the launch traced here: 163 us
  waiting for transfers between devices  72.8 us (44%)
  local copies, waits for them, and re-layouts  31.1 us (19%)
  starting transfers between devices  24.1 us (15%)
  matrix products  19.8 us (12%)
  other arithmetic  7.97 us (5%)
  blocking collectives  6.36 us (4%)
    all_to_all x1, waiting for transfers between devices, per_device(): lax.all_to_all(copies, ('fsdp', 'rep'), split_axis=0, concat_axis=1, tile...  53.1 us
    transpose x1, local copies, waits for them, and re-layouts, per_device(): jnp.transpose(arrived, (0, 1, 3, 2, 4))  12.5 us
    all_to_all x1, starting transfers between devices, per_device(): lax.all_to_all(copies, ('fsdp', 'rep'), split_axis=0, concat_axis=1, tile...  12 us
    all_to_all x1, waiting for transfers between devices, per_device(): lax.all_to_all(grafted, 'rep', split_axis=2, concat_axis=1, tiled=True)  11.6 us
    dot_general x1, matrix products, per_device(): jnp.einsum('nik,nkj->nij', root_left, product, preferred_element_type=jnp...  11 us
    all_to_all x1, starting transfers between devices, per_device(): lax.all_to_all(lax.all_to_all(grafted, 'rep', split_axis=2, concat_axis=1...  8.63 us
    all_to_all x1, waiting for transfers between devices, per_device(): lax.all_to_all(lax.all_to_all(grafted, 'rep', split_axis=2, concat_axis=1...  8.01 us
    reshape x1, local copies, waits for them, and re-layouts, per_device(): jnp.transpose(arrived, (0, 1, 3, 2, 4))  7.71 us
  transfers between devices with their start and end apart: 3, of which 3 were waited for; matrix products, arithmetic and copies ran while one was open for 5% of the time, Pallas kernels for 0%

commit v1 on v0

v1 whole, which is shorter than its diff:
```python
import functools

import jax
import jax.numpy as jnp
from jax import lax
from jax.experimental import pallas as pl
from jax.experimental.pallas import tpu as pltpu
from jax.sharding import PartitionSpec as P

VMEM_LIMIT = 48 * 1024 * 1024
QUARTERS = 4
PAD = 16
NT = (((1,), (1,)), ((), ()))
TN = (((0,), (0,)), ((), ()))


def params():
    return pltpu.CompilerParams(vmem_limit_bytes=VMEM_LIMIT)


def any_spec():
    return pl.BlockSpec(memory_space=pl.ANY)


def vmem_spec():
    return pl.BlockSpec(memory_space=pltpu.VMEM)


def smem_spec():
    return pl.BlockSpec(memory_space=pltpu.SMEM)


def dot(a, b, dims=(((1,), (0,)), ((), ()))):
    return lax.dot_general(a, b, dims, preferred_element_type=jnp.float32)


def scatter_kernel(slot_ref, grads_ref, even_ref, odd_ref, sem):
    blocks = grads_ref.shape[0]

    def body(b, _):
        slot = slot_ref[b]
        owner = slot // 2

        @pl.when(slot % 2 == 0)
        def _():
            pltpu.make_async_copy(grads_ref.at[b], even_ref.at[owner], sem).start()

        @pl.when(slot % 2 == 1)
        def _():
            pltpu.make_async_copy(grads_ref.at[b], odd_ref.at[owner], sem).start()

        return 0

    lax.fori_loop(0, blocks, body, 0, unroll=8)
    pltpu.make_async_copy(even_ref, even_ref, sem).wait()
    pltpu.make_async_copy(odd_ref, odd_ref, sem).wait()


def scatter(owner_slot, grads):
    blocks, rows, cols = grads.shape
    half = jax.ShapeDtypeStruct((blocks // 2, rows, cols), grads.dtype)
    return pl.pallas_call(
        scatter_kernel,
        out_shape=(half, half),
        in_specs=[smem_spec(), any_spec()],
        out_specs=(any_spec(), any_spec()),
        scratch_shapes=[pltpu.SemaphoreType.DMA],
        compiler_params=params(),
        cost_estimate=pl.CostEstimate(flops=0, bytes_accessed=2 * grads.size * 2, transcendentals=0),
        name="scatter_blocks",
    )(owner_slot, grads)


def gather_kernel(slot_ref, even_ref, odd_ref, out_ref, sem):
    blocks = out_ref.shape[0]

    def body(b, _):
        slot = slot_ref[b]
        owner = slot // 2

        @pl.when(slot % 2 == 0)
        def _():
            pltpu.make_async_copy(even_ref.at[owner], out_ref.at[b], sem).start()

        @pl.when(slot % 2 == 1)
        def _():
            pltpu.make_async_copy(odd_ref.at[owner], out_ref.at[b], sem).start()

        return 0

    lax.fori_loop(0, blocks, body, 0, unroll=8)
    pltpu.make_async_copy(out_ref, out_ref, sem).wait()


def gather(owner_slot, even, odd):
    owners, rows, cols = even.shape
    return pl.pallas_call(
        gather_kernel,
        out_shape=jax.ShapeDtypeStruct((2 * owners, rows, cols), even.dtype),
        in_specs=[smem_spec(), any_spec(), any_spec()],
        out_specs=any_spec(),
        scratch_shapes=[pltpu.SemaphoreType.DMA],
        compiler_params=params(),
        cost_estimate=pl.CostEstimate(flops=0, bytes_accessed=4 * even.size * 2, transcendentals=0),
        name="gather_blocks",
    )(owner_slot, even, odd)


def adam_kernel(rep_ref, g0_ref, g1_ref, g2_ref, g3_ref, mom_ref, sec_ref, *rest):
    mom_out, sec_out, sum_ref = rest[-3:]
    rep = rep_ref[0]
    part = g0_ref.shape[1]
    rows = mom_ref.shape[1]
    total = jnp.zeros((8, part), jnp.float32)
    for j, ref in enumerate((g0_ref, g1_ref, g2_ref, g3_ref)):
        cols = pl.ds(pl.multiple_of(lax.rem(rep + j, QUARTERS) * part, part), part)
        grad = ref[pl.ds(pl.multiple_of(rep * rows, rows), rows), :].astype(jnp.float32)
        first = 0.9 * mom_ref[0, :, cols] + 0.1 * grad
        second = 0.95 * sec_ref[0, :, cols] + 0.05 * grad * grad
        mom_out[0, :, cols] = first
        sec_out[0, :, cols] = second
        way = first / (jnp.sqrt(second) + 1e-08)
        total += jnp.sum((way * way).reshape(rows // 8, 8, part), axis=0)
    sum_ref[...] = total


def adam(k, rep, quarters, moment, second, earlier):
    rows, size = moment.shape[1:]
    part = quarters[0].shape[1]
    out = jax.ShapeDtypeStruct(moment.shape, jnp.float32)
    state = pl.BlockSpec((1, rows, size), lambda i: (k, 0, 0))
    return pl.pallas_call(
        adam_kernel,
        grid=(1,),
        out_shape=(out, out, jax.ShapeDtypeStruct((8, part), jnp.float32)),
        in_specs=[smem_spec()] + [vmem_spec()] * 4 + [state, state] + [any_spec()] * len(earlier),
        out_specs=(state, state, vmem_spec()),
        input_output_aliases={7 + i: i for i in range(len(earlier))},
        compiler_params=params(),
        cost_estimate=pl.CostEstimate(flops=rows * size * 14, bytes_accessed=rows * size * 18, transcendentals=rows * size * 2),
        name="adam_rows",
    )(rep, *quarters, moment, second, *earlier)


def precond_kernel(rep_ref, g0_ref, g1_ref, g2_ref, g3_ref, left_ref, right_ref, adam_ref, out0, out1, out2, out3, acc):
    rep = rep_ref[0]
    part = g0_ref.shape[1]
    rows = left_ref.shape[1]
    left = left_ref[0]
    for j, ref in enumerate((g0_ref, g1_ref, g2_ref, g3_ref)):
        mixed = dot(left, ref[...]).astype(jnp.bfloat16)
        depth = pl.ds(pl.multiple_of(lax.rem(rep + j, QUARTERS) * part, part), part)
        term = dot(mixed, right_ref[0, depth, :])
        if j == 0:
            acc[...] = term
        else:
            acc[...] += term
    whole = acc[...]
    pre_sq = jnp.sum(whole * whole)
    adam_sq = jnp.sum(adam_ref[...])
    pad_row = lax.broadcasted_iota(jnp.int32, (PAD, part), 0)
    pad = jnp.zeros((PAD, part), jnp.float32)
    for first, value in ((0, adam_sq), (3, pre_sq)):
        rest = jnp.full((PAD, part), value, jnp.float32)
        for i in range(3):
            high = rest.astype(jnp.bfloat16).astype(jnp.float32)
            pad = jnp.where(pad_row == first + i, high, pad)
            rest = rest - high
    pad = pad.astype(jnp.bfloat16)
    for j, ref in enumerate((out0, out1, out2, out3)):
        cols = pl.ds(pl.multiple_of(lax.rem(rep + j, QUARTERS) * part, part), part)
        ref[:rows, :] = acc[:, cols].astype(jnp.bfloat16)
        ref[rows:, :] = pad


def precond(k, rep, quarters, root_left, root_right, adam_sq):
    rows, size = root_left.shape[1:]
    part = quarters[0].shape[1]
    piece = jax.ShapeDtypeStruct((rows + PAD, part), jnp.bfloat16)
    return pl.pallas_call(
        precond_kernel,
        grid=(1,),
        out_shape=(piece,) * 4,
        in_specs=[smem_spec()]
        + [vmem_spec()] * 4
        + [
            pl.BlockSpec((1, rows, size), lambda i: (k, 0, 0)),
            pl.BlockSpec((1, size, size), lambda i: (k, 0, 0)),
            vmem_spec(),
        ],
        out_specs=(vmem_spec(),) * 4,
        scratch_shapes=[pltpu.VMEM((rows, size), jnp.float32)],
        compiler_params=params(),
        cost_estimate=pl.CostEstimate(flops=4 * rows * size * size, bytes_accessed=5 * size * size, transcendentals=0),
        name="precond_rows",
    )(rep, *quarters, root_left, root_right, adam_sq)


def gram_kernel(rep_ref, g0_ref, g1_ref, g2_ref, g3_ref, left_ref, right_ref, *rest):
    left_out, right_out = rest[-2:]
    rep = rep_ref[0]
    part = g0_ref.shape[1]
    rows = left_ref.shape[1]
    own = pl.ds(pl.multiple_of(rep * rows, rows), rows)
    for j, ref in enumerate((g0_ref, g1_ref, g2_ref, g3_ref)):
        cols = pl.ds(pl.multiple_of(lax.rem(rep + j, QUARTERS) * part, part), part)
        term = 0.05 * dot(ref[own, :], ref[...], NT)
        if j == 0:
            left_out[0] = 0.95 * left_ref[0] + term
        else:
            left_out[0] += term
        right_out[0, :, cols] = 0.95 * right_ref[0, :, cols] + 0.05 * dot(g0_ref[...], ref[...], TN)


def gram(k, rep, quarters, gram_left, gram_right, earlier):
    rows, size = gram_left.shape[1:]
    out = jax.ShapeDtypeStruct(gram_left.shape, jnp.float32)
    state = pl.BlockSpec((1, rows, size), lambda i: (k, 0, 0))
    return pl.pallas_call(
        gram_kernel,
        grid=(1,),
        out_shape=(out, out),
        in_specs=[smem_spec()] + [vmem_spec()] * 4 + [state, state] + [any_spec()] * len(earlier),
        out_specs=(state, state),
        input_output_aliases={7 + i: i for i in range(len(earlier))},
        compiler_params=params(),
        cost_estimate=pl.CostEstimate(flops=4 * rows * size * size, bytes_accessed=6 * size * size, transcendentals=0),
        name="gram_rows",
    )(rep, *quarters, gram_left, gram_right, *earlier)


def scale_kernel(cells, rep_ref, p0_ref, p1_ref, p2_ref, p3_ref, out_ref):
    rep = rep_ref[0]
    rows = p0_ref.shape[0] - PAD
    sums = jnp.zeros((PAD, p0_ref.shape[1]), jnp.float32)
    pieces = (p0_ref, p1_ref, p2_ref, p3_ref)
    for ref in pieces:
        sums += ref[rows:, :].astype(jnp.float32)
    adam_all = sums[0:1] + sums[1:2] + sums[2:3]
    pre_all = sums[3:4] + sums[4:5] + sums[5:6]
    ratio = jnp.sqrt(adam_all / cells + 1e-06) / jnp.sqrt(pre_all / cells + 1e-06)
    for j, ref in enumerate(pieces):
        where = pl.ds(pl.multiple_of(lax.rem(rep + j, QUARTERS) * rows, rows), rows)
        out_ref[where, :] = (ref[:rows, :].astype(jnp.float32) * ratio).astype(jnp.bfloat16)


def scale(rep, pieces, size):
    rows = pieces[0].shape[0] - PAD
    part = pieces[0].shape[1]
    return pl.pallas_call(
        functools.partial(scale_kernel, float(size * size)),
        out_shape=jax.ShapeDtypeStruct((QUARTERS * rows, part), jnp.bfloat16),
        in_specs=[smem_spec()] + [vmem_spec()] * 4,
        out_specs=vmem_spec(),
        compiler_params=params(),
        cost_estimate=pl.CostEstimate(flops=2 * size * part, bytes_accessed=4 * size * part, transcendentals=0),
        name="scale_rows",
    )(rep, *pieces)


def shift(x, step):
    return lax.ppermute(x, "rep", [(i, (i + step) % QUARTERS) for i in range(QUARTERS)])


def swap(x):
    return lax.all_to_all(x, "fsdp", split_axis=0, concat_axis=0, tiled=True)


def per_device(grads, owner_slot, gram_left, gram_right, root_left, root_right, moment, second):
    row_part, col_part = grads.shape[1:]
    size = root_right.shape[1]
    rep = lax.axis_index("rep").astype(jnp.int32).reshape(1)
    sent = scatter(owner_slot, grads)
    own = [swap(x).reshape(size, col_part) for x in sent]
    before = [shift(x, 1) for x in own]
    after = [shift(x, -1) for x in own]
    across = [shift(before[0], 1), shift(after[1], -1)]
    homed, state, grams = [], (), ()
    for k in range(2):
        quarters = (own[k], after[k], across[k], before[k])
        *state, adam_sq = adam(k, rep, quarters, moment, second, state)
        pieces = precond(k, rep, quarters, root_left, root_right, adam_sq)
        arrived = [pieces[0]] + [shift(pieces[QUARTERS - j], -j) for j in range(1, QUARTERS)]
        grams = gram(k, rep, quarters, gram_left, gram_right, grams)
        scaled = scale(rep, arrived, size)
        homed.append(swap(scaled.reshape(-1, row_part, col_part)))
    updates = gather(owner_slot, *homed)
    return (updates, *grams, *state)


def solution(mesh):
    return jax.shard_map(
        per_device,
        mesh=mesh,
        in_specs=(
            P(None, "fsdp", "rep"),
            P(),
            P("fsdp", "rep", None),
            P("fsdp", "rep", None),
            P("fsdp", "rep", None),
            P("fsdp", None, None),
            P("fsdp", "rep", None),
            P("fsdp", "rep", None),
        ),
        out_specs=(
            P(None, "fsdp", "rep"),
            P("fsdp", "rep", None),
            P("fsdp", "rep", None),
            P("fsdp", "rep", None),
            P("fsdp", "rep", None),
        ),
        check_vma=False,
    )
```

time: 164 us -> 175 us (1.067)
  Pallas kernels: 0 us -> 61.8 us
  local copies, waits for them, and re-layouts: 31.1 us -> 2.84 us
  matrix products: 19.8 us -> 0 us
  waiting for transfers between devices: 72.8 us -> 56.3 us
  blocking collectives: 6.36 us -> 20.9 us
  other arithmetic: 7.97 us -> 0 us
  starting transfers between devices: 24.1 us -> 31.4 us
    pallas_call x0 -> x10, Pallas kernels: none -> 61.8 us  [the longest x1 33.4 us: gather(): pl.pallas_call(gather_kernel, out_shape=jax.ShapeDtypeStruct((2 * owners,...]
    all_to_all x3, waiting for transfers between devices: 72.8 us -> 13.1 us  [swap(): return lax.all_to_all(x, 'fsdp', split_axis=0, concat_axis=0, tiled=True)]
    ppermute x0 -> x12, waiting for transfers between devices: none -> 43.2 us  [shift(): lax.ppermute(x, 'rep', [(i, (i + step) % QUARTERS) for i in range(QUARTER...]
    all_to_all x0 -> x1, blocking collectives: none -> 20.9 us  [swap(): return lax.all_to_all(x, 'fsdp', split_axis=0, concat_axis=0, tiled=True)]
    dot_general x3 -> x0, matrix products: 19.8 us -> none  [the longest x1 11 us: per_device(): jnp.einsum('nik,nkj->nij', root_left, product, preferred_element_type=jnp...]
    ppermute x0 -> x12, starting transfers between devices: none -> 15 us  [shift(): lax.ppermute(x, 'rep', [(i, (i + step) % QUARTERS) for i in range(QUARTER...]
    transpose x1 -> x0, local copies, waits for them, and re-layouts: 12.5 us -> none  [per_device(): jnp.transpose(arrived, (0, 1, 3, 2, 4))]
    reshape x1 -> x0, local copies, waits for them, and re-layouts: 7.71 us -> none  [per_device(): jnp.transpose(arrived, (0, 1, 3, 2, 4))]
  transfers between devices with their start and end apart: 3 -> 15, of which waited for: 3 -> 12; matrix products, arithmetic and copies ran while one was open for 5% -> 0% of each run, Pallas kernels for 0% -> 10%
where the time goes in v1:
time: 175 us; the launch traced here: 174 us
  Pallas kernels  61.8 us (35%)
  waiting for transfers between devices  56.3 us (32%)
  starting transfers between devices  31.4 us (18%)
  blocking collectives  20.9 us (12%)
  local copies, waits for them, and re-layouts  2.84 us (2%)
    ppermute x12, waiting for transfers between devices, shift(): lax.ppermute(x, 'rep', [(i, (i + step) % QUARTERS) for i in range(QUARTER...  43.2 us
    pallas_call x1, Pallas kernels, gather(): pl.pallas_call(gather_kernel, out_shape=jax.ShapeDtypeStruct((2 * owners,...  33.4 us
    all_to_all x1, blocking collectives, swap(): return lax.all_to_all(x, 'fsdp', split_axis=0, concat_axis=0, tiled=True)  20.9 us
    all_to_all x3, starting transfers between devices, swap(): return lax.all_to_all(x, 'fsdp', split_axis=0, concat_axis=0, tiled=True)  16.4 us
    ppermute x12, starting transfers between devices, shift(): lax.ppermute(x, 'rep', [(i, (i + step) % QUARTERS) for i in range(QUARTER...  15 us
    all_to_all x3, waiting for transfers between devices, swap(): return lax.all_to_all(x, 'fsdp', split_axis=0, concat_axis=0, tiled=True)  13.1 us
    pallas_call x2, Pallas kernels, gram(): pl.pallas_call(gram_kernel, grid=(1,), out_shape=(out, out), in_specs=[sm...  8.72 us
    pallas_call x2, Pallas kernels, precond(): pl.pallas_call(precond_kernel, grid=(1,), out_shape=(piece,) * 4, in_spec...  8.18 us
  transfers between devices with their start and end apart: 15, of which 12 were waited for; matrix products, arithmetic and copies ran while one was open for 0% of the time, Pallas kernels for 10%

profile of v1, /device:TPU:1, one launch (start us, length us, event | category | flops | bytes accessed | tf_op | source)
XLA Modules:
  0.0 174.1 jit_solution(11770925048473784152)
XLA Ops:
  0.7 1.4 copy-done.5
  2.7 3.1 %scatter_blocks.1 = (bf16[32,32,256]{2,1,0:T(8,128)(2,1)S(1)}, bf16[32,32,256]{2,1,0:T(8,128)(2,1)S(1)}) custom-call(s32[64]{0:T(128)S(1)} %copy-done.7, bf16[64,32,256]{2,1,0:T(8,128)(2,1)S(1)} %copy-done.5), custom_call_target="tpu_custom_call" | custom-call | bytes 2097152 | tf_op jit(solution)/shard_map/scatter_blocks/pallas_call | solution.py:62
  5.8 20.9 %all_to_all.20 = bf16[32,32,256]{2,1,0:T(8,128)(2,1)S(1)} all-to-all(bf16[32,32,256]{2,1,0:T(8,128)(2,1)S(1)} %get-tuple-element.25), channel_id=1, replica_groups=mesh['fsdp'=32,'rep'=4] {'fsdp'}, dimensions={0} | all-to-all | bytes 1048576 | tf_op jit(solution)/shard_map/all_to_all | solution.py:266
  26.6 3.7 %all-to-all-start.2 = ((bf16[32,32,256]{2,1,0:T(8,128)(2,1)}), bf16[32,32,256]{2,1,0:T(8,128)(2,1)S(1)}, u32[]{:S(2)}, u32[]{:S(2)}) async-start(bf16[32,32,256]{2,1,0:T(8,128)(2,1)} %copy-done.6), calls=%async_computation.2 | async-start | bytes 1048576 | tf_op jit(solution)/shard_map/all_to_all | solution.py:266
  30.3 1.4 collective-permute-start.1
  31.7 10.2 %all-to-all-done.2 = bf16[32,32,256]{2,1,0:T(8,128)(2,1)S(1)} async-done(((bf16[32,32,256]{2,1,0:T(8,128)(2,1)}), bf16[32,32,256]{2,1,0:T(8,128)(2,1)S(1)}, u32[]{:S(2)}, u32[]{:S(2)}) %all-to-all-start.2) | async-done | bytes 524320 | tf_op jit(solution)/shard_map/all_to_all | solution.py:266
  41.9 2.7 %collective-permute-start.6 = (bf16[1024,256]{1,0:T(8,128)(2,1)S(1)}, bf16[1024,256]{1,0:T(8,128)(2,1)}, u32[]{:S(2)}, u32[]{:S(2)}) collective-permute-start(bf16[1024,256]{1,0:T(8,128)(2,1)S(1)} %bitcast.10), channel_id=1, source_target_pairs={{0,3},{1,0},{2,1},{3,2},{4,7},{5,4},{6,5},{7,6},{8,11},{9,8},{10,9... | collective-permute-start | bytes 1572872 | tf_op jit(solution)/shard_map/ppermute | solution.py:262
  45.2 0.9 collective-permute-start.2
  46.4 9.7 %collective-permute-done.6.g1_ref = bf16[1024,256]{1,0:T(8,128)(2,1)} collective-permute-done((bf16[1024,256]{1,0:T(8,128)(2,1)S(1)}, bf16[1024,256]{1,0:T(8,128)(2,1)}, u32[]{:S(2)}, u32[]{:S(2)}) %collective-permute-start.6) | collective-permute-done | bytes 524320 | tf_op jit(solution)/shard_map/ppermute | solution.py:262
  56.1 3.5 %collective-permute-start.7 = (bf16[1024,256]{1,0:T(8,128)(2,1)}, bf16[1024,256]{1,0:T(8,128)(2,1)}, u32[]{:S(2)}, u32[]{:S(2)}) collective-permute-start(bf16[1024,256]{1,0:T(8,128)(2,1)} %collective-permute-done.6.g1_ref), channel_id=1, source_target_pairs={{0,3},{1,0},{2,1},{3,2},{4,7},{5,4},{6,5},{7,6},{8,11},{9,8},{10,9... | collective-permute-start | bytes 1572872 | tf_op jit(solution)/shard_map/ppermute | solution.py:262
  59.6 7.7 %collective-permute-done.g1_ref = bf16[1024,256]{1,0:T(8,128)(2,1)} collective-permute-done((bf16[1024,256]{1,0:T(8,128)(2,1)S(1)}, bf16[1024,256]{1,0:T(8,128)(2,1)}, u32[]{:S(2)}, u32[]{:S(2)}) %collective-permute-start) | collective-permute-done | bytes 524320 | tf_op jit(solution)/shard_map/ppermute | solution.py:262
  67.3 3.6 %adam_rows.2 = (f32[2,256,1024]{2,1,0:T(8,128)}, f32[2,256,1024]{2,1,0:T(8,128)}, f32[8,256]{1,0:T(8,128)S(1)}) custom-call(s32[1]{0:T(128)} %bitcast.rep_ref, bf16[1024,256]{1,0:T(8,128)(2,1)S(1)} %bitcast.7, bf16[1024,256]{1,0:T(8,128)(2,1)} %collective-permute-done.g1_ref, bf16[1024,256]{1,0:T(8,128)(2,1)} %collective-permute-done.2.g2_ref, ...), custom_call_target="tpu_custom_call" | custom-call | flops 3670016 | bytes 4718592 | tf_op jit(solution)/shard_map/adam_rows/pallas_call | solution.py:132
  71.0 7.7 %collective-permute-done.7.g2_ref = bf16[1024,256]{1,0:T(8,128)(2,1)} collective-permute-done((bf16[1024,256]{1,0:T(8,128)(2,1)}, bf16[1024,256]{1,0:T(8,128)(2,1)}, u32[]{:S(2)}, u32[]{:S(2)}) %collective-permute-start.7) | collective-permute-done | bytes 524320 | tf_op jit(solution)/shard_map/ppermute | solution.py:262
  78.7 3.7 %adam_rows.3 = (f32[2,256,1024]{2,1,0:T(8,128)}, f32[2,256,1024]{2,1,0:T(8,128)}, f32[8,256]{1,0:T(8,128)S(1)}) custom-call(s32[1]{0:T(128)} %bitcast.rep_ref, bf16[1024,256]{1,0:T(8,128)(2,1)S(1)} %bitcast.12, bf16[1024,256]{1,0:T(8,128)(2,1)} %collective-permute-done.6.g1_ref, ...), custom_call_target="tpu_custom_call", output_to_operand_aliasing={{0}: (7, {}), {1}: (8, {})} | custom-call | flops 3670016 | bytes 4718592 | tf_op jit(solution)/shard_map/adam_rows/pallas_call | solution.py:132
  82.4 4.1 %precond_rows.3 = (bf16[272,256]{1,0:T(8,128)(2,1)S(1)}, bf16[272,256]{1,0:T(8,128)(2,1)S(1)}, bf16[272,256]{1,0:T(8,128)(2,1)S(1)}, bf16[272,256]{1,0:T(8,128)(2,1)S(1)}) custom-call(s32[1]{0:T(128)} %bitcast.rep_ref, bf16[1024,256]{1,0:T(8,128)(2,1)S(1)} %bitcast.13, bf16[1024,256]{1,0:T(8,128)(2,1)} %collective-permute-done.6.g1_ref, ...), custom_call_target="tpu_custom_call" | custom-call | flops 1073741824 | bytes 5242880 | tf_op jit(solution)/shard_map/precond_rows/pallas_call | solution.py:180
  86.5 3.5 %collective-permute-start.9 = (bf16[272,256]{1,0:T(8,128)(2,1)S(1)}, bf16[272,256]{1,0:T(8,128)(2,1)S(1)}, u32[]{:S(2)}, u32[]{:S(2)}) collective-permute-start(bf16[272,256]{1,0:T(8,128)(2,1)S(1)} %get-tuple-element.36), channel_id=1, source_target_pairs={{0,3},{1,0},{2,1},{3,2},{4,7},{5,4},{6,5},{7,6},{8,11},{9,8},{10,9... | collective-permute-start | bytes 417800 | tf_op jit(solution)/shard_map/ppermute | solution.py:262
  90.7 4.8 %collective-permute-done.9.p1_ref = bf16[272,256]{1,0:T(8,128)(2,1)S(1)} collective-permute-done((bf16[272,256]{1,0:T(8,128)(2,1)S(1)}, bf16[272,256]{1,0:T(8,128)(2,1)S(1)}, u32[]{:S(2)}, u32[]{:S(2)}) %collective-permute-start.9) | collective-permute-done | bytes 139296 | tf_op jit(solution)/shard_map/ppermute | solution.py:262
  95.8 3.6 %collective-permute-done.11.p3_ref = bf16[272,256]{1,0:T(8,128)(2,1)S(1)} collective-permute-done((bf16[272,256]{1,0:T(8,128)(2,1)S(1)}, bf16[272,256]{1,0:T(8,128)(2,1)S(1)}, u32[]{:S(2)}, u32[]{:S(2)}) %collective-permute-start.11) | collective-permute-done | bytes 139296 | tf_op jit(solution)/shard_map/ppermute | solution.py:262
  99.4 0.9 scale_rows.3
  100.3 5.0 %all-to-all-start.3 = ((bf16[32,32,256]{2,1,0:T(8,128)(2,1)}), bf16[32,32,256]{2,1,0:T(8,128)(2,1)}, u32[]{:S(2)}, u32[]{:S(2)}) async-start(bf16[32,32,256]{2,1,0:T(8,128)(2,1)} %bitcast.4), calls=%async_computation.3 | async-start | bytes 1048576 | tf_op jit(solution)/shard_map/all_to_all | solution.py:266
  105.4 4.1 %precond_rows.2 = (bf16[272,256]{1,0:T(8,128)(2,1)S(1)}, bf16[272,256]{1,0:T(8,128)(2,1)S(1)}, bf16[272,256]{1,0:T(8,128)(2,1)S(1)}, bf16[272,256]{1,0:T(8,128)(2,1)S(1)}) custom-call(s32[1]{0:T(128)} %bitcast.rep_ref, bf16[1024,256]{1,0:T(8,128)(2,1)S(1)} %bitcast.8, bf16[1024,256]{1,0:T(8,128)(2,1)} %collective-permute-done.g1_ref, ...), custom_call_target="tpu_custom_call" | custom-call | flops 1073741824 | bytes 5242880 | tf_op jit(solution)/shard_map/precond_rows/pallas_call | solution.py:180
  109.5 0.7 collective-permute-start.3
  110.2 0.8 collective-permute-start.5
  111.0 3.5 %collective-permute-done.3.p1_ref = bf16[272,256]{1,0:T(8,128)(2,1)S(1)} collective-permute-done((bf16[272,256]{1,0:T(8,128)(2,1)S(1)}, bf16[272,256]{1,0:T(8,128)(2,1)S(1)}, u32[]{:S(2)}, u32[]{:S(2)}) %collective-permute-start.3) | collective-permute-done | bytes 139296 | tf_op jit(solution)/shard_map/ppermute | solution.py:262
  114.5 1.8 %collective-permute-done.4.p2_ref = bf16[272,256]{1,0:T(8,128)(2,1)S(1)} collective-permute-done((bf16[272,256]{1,0:T(8,128)(2,1)S(1)}, bf16[272,256]{1,0:T(8,128)(2,1)S(1)}, u32[]{:S(2)}, u32[]{:S(2)}) %collective-permute-start.4) | collective-permute-done | bytes 139296 | tf_op jit(solution)/shard_map/ppermute | solution.py:262
  116.3 4.0 %collective-permute-done.5.p3_ref = bf16[272,256]{1,0:T(8,128)(2,1)S(1)} collective-permute-done((bf16[272,256]{1,0:T(8,128)(2,1)S(1)}, bf16[272,256]{1,0:T(8,128)(2,1)S(1)}, u32[]{:S(2)}, u32[]{:S(2)}) %collective-permute-start.5) | collective-permute-done | bytes 139296 | tf_op jit(solution)/shard_map/ppermute | solution.py:262
  120.4 0.8 copy-done.4
  121.2 7.7 %all-to-all-start.1 = ((bf16[32,32,256]{2,1,0:T(8,128)(2,1)}), bf16[32,32,256]{2,1,0:T(8,128)(2,1)}, u32[]{:S(2)}, u32[]{:S(2)}) async-start(bf16[32,32,256]{2,1,0:T(8,128)(2,1)} %bitcast.15), calls=%async_computation.1 | async-start | bytes 1048576 | tf_op jit(solution)/shard_map/all_to_all | solution.py:266
  128.9 4.4 %gram_rows.2 = (f32[2,256,1024]{2,1,0:T(8,128)}, f32[2,256,1024]{2,1,0:T(8,128)}) custom-call(s32[1]{0:T(128)} %bitcast.rep_ref, bf16[1024,256]{1,0:T(8,128)(2,1)S(1)} %bitcast.9, bf16[1024,256]{1,0:T(8,128)(2,1)} %collective-permute-done.g1_ref, bf16[1024,256]{1,0:T(8,128)(2,1)} %collective-permute-done.2.g2_ref, ...), custom_call_target="tpu_custom_call" | custom-call | flops 1073741824 | bytes 6291456 | tf_op jit(solution)/shard_map/gram_rows/pallas_call | solution.py:219
  133.3 4.4 %gram_rows.3 = (f32[2,256,1024]{2,1,0:T(8,128)}, f32[2,256,1024]{2,1,0:T(8,128)}) custom-call(s32[1]{0:T(128)} %bitcast.rep_ref, bf16[1024,256]{1,0:T(8,128)(2,1)S(1)} %bitcast.14, bf16[1024,256]{1,0:T(8,128)(2,1)} %collective-permute-done.6.g1_ref, bf16[1024,256]{1,0:T(8,128)(2,1)} %collective-permute-done.7.g2_ref, ...), custom_call_target="tpu_custom_call", output_to_operand_aliasing={{0}: (7, {}), {1}: (8, {})} | custom-call | flops 1073741824 | bytes 6291456 | tf_op jit(solution)/shard_map/gram_rows/pallas_call | solution.py:219
  137.6 2.9 %all-to-all-done.1.even_ref = bf16[32,32,256]{2,1,0:T(8,128)(2,1)} async-done(((bf16[32,32,256]{2,1,0:T(8,128)(2,1)}), bf16[32,32,256]{2,1,0:T(8,128)(2,1)}, u32[]{:S(2)}, u32[]{:S(2)}) %all-to-all-start.1) | async-done | bytes 524320 | tf_op jit(solution)/shard_map/all_to_all | solution.py:266
  140.6 33.4 %gather_blocks.1 = bf16[64,32,256]{2,1,0:T(8,128)(2,1)} custom-call(s32[64]{0:T(128)S(1)} %copy-done.8, bf16[32,32,256]{2,1,0:T(8,128)(2,1)} %all-to-all-done.1.even_ref, bf16[32,32,256]{2,1,0:T(8,128)(2,1)} %all-to-all-done.3.odd_ref), custom_call_target="tpu_custom_call" | custom-call | bytes 2097152 | tf_op jit(solution)/shard_map/gather_blocks/pallas_call | solution.py:97
  (27 shorter events, 2.7 us)
Async XLA Ops:
  0.6 66.7 %copy-start = (f32[2,256,1024]{2,1,0:T(8,128)S(1)}, f32[2,256,1024]{2,1,0:T(8,128)}, u32[]{:S(2)}) copy-start(f32[2,256,1024]{2,1,0:T(8,128)} %mom_ref.3) | copy-start | bytes 6291460
  0.6 1.4 copy-start.5
  2.0 0.7 copy-start.7
  5.8 20.9 %copy-start.6 = (bf16[32,32,256]{2,1,0:T(8,128)(2,1)}, bf16[32,32,256]{2,1,0:T(8,128)(2,1)S(1)}, u32[]{:S(2)}) copy-start(bf16[32,32,256]{2,1,0:T(8,128)(2,1)S(1)} %get-tuple-element.31) | copy-start | bytes 1572868
  26.6 15.3 %all-to-all-start.2 = ((bf16[32,32,256]{2,1,0:T(8,128)(2,1)}), bf16[32,32,256]{2,1,0:T(8,128)(2,1)S(1)}, u32[]{:S(2)}, u32[]{:S(2)}) async-start(bf16[32,32,256]{2,1,0:T(8,128)(2,1)} %copy-done.6), calls=%async_computation.2 | async-start | bytes 1048576 | tf_op jit(solution)/shard_map/all_to_all | solution.py:266
  30.3 14.9 %collective-permute-start.1 = (bf16[1024,256]{1,0:T(8,128)(2,1)S(1)}, bf16[1024,256]{1,0:T(8,128)(2,1)}, u32[]{:S(2)}, u32[]{:S(2)}) collective-permute-start(bf16[1024,256]{1,0:T(8,128)(2,1)S(1)} %bitcast.5), channel_id=1, source_target_pairs={{0,1},{1,2},{2,3},{3,0},{4,5},{5,6},{6,7},{7,4},{8,9},{9,10},{10,1... | collective-permute-start | bytes 1572872 | tf_op jit(solution)/shard_map/ppermute | solution.py:262
  41.9 14.2 %collective-permute-start.6 = (bf16[1024,256]{1,0:T(8,128)(2,1)S(1)}, bf16[1024,256]{1,0:T(8,128)(2,1)}, u32[]{:S(2)}, u32[]{:S(2)}) collective-permute-start(bf16[1024,256]{1,0:T(8,128)(2,1)S(1)} %bitcast.10), channel_id=1, source_target_pairs={{0,3},{1,0},{2,1},{3,2},{4,7},{5,4},{6,5},{7,6},{8,11},{9,8},{10,9... | collective-permute-start | bytes 1572872 | tf_op jit(solution)/shard_map/ppermute | solution.py:262
  44.6 22.7 %collective-permute-start = (bf16[1024,256]{1,0:T(8,128)(2,1)S(1)}, bf16[1024,256]{1,0:T(8,128)(2,1)}, u32[]{:S(2)}, u32[]{:S(2)}) collective-permute-start(bf16[1024,256]{1,0:T(8,128)(2,1)S(1)} %bitcast.6), channel_id=1, source_target_pairs={{0,3},{1,0},{2,1},{3,2},{4,7},{5,4},{6,5},{7,6},{8,11},{9,8},{10,9... | collective-permute-start | bytes 1572872 | tf_op jit(solution)/shard_map/ppermute | solution.py:262
  45.2 22.2 %collective-permute-start.2 = (bf16[1024,256]{1,0:T(8,128)(2,1)}, bf16[1024,256]{1,0:T(8,128)(2,1)}, u32[]{:S(2)}, u32[]{:S(2)}) collective-permute-start(bf16[1024,256]{1,0:T(8,128)(2,1)} %collective-permute-done.1.g3_ref), channel_id=1, source_target_pairs={{0,1},{1,2},{2,3},{3,0},{4,5},{5,6},{6,7},{7,4},{8,9},{9,10},{10,1... | collective-permute-start | bytes 1572872 | tf_op jit(solution)/shard_map/ppermute | solution.py:262
  46.1 24.9 %collective-permute-start.8 = (bf16[1024,256]{1,0:T(8,128)(2,1)S(1)}, bf16[1024,256]{1,0:T(8,128)(2,1)}, u32[]{:S(2)}, u32[]{:S(2)}) collective-permute-start(bf16[1024,256]{1,0:T(8,128)(2,1)S(1)} %bitcast.11), channel_id=1, source_target_pairs={{0,1},{1,2},{2,3},{3,0},{4,5},{5,6},{6,7},{7,4},{8,9},{9,10},{10,1... | collective-permute-start | bytes 1572872 | tf_op jit(solution)/shard_map/ppermute | solution.py:262
  56.1 22.6 %collective-permute-start.7 = (bf16[1024,256]{1,0:T(8,128)(2,1)}, bf16[1024,256]{1,0:T(8,128)(2,1)}, u32[]{:S(2)}, u32[]{:S(2)}) collective-permute-start(bf16[1024,256]{1,0:T(8,128)(2,1)} %collective-permute-done.6.g1_ref), channel_id=1, source_target_pairs={{0,3},{1,0},{2,1},{3,2},{4,7},{5,4},{6,5},{7,6},{8,11},{9,8},{10,9... | collective-permute-start | bytes 1572872 | tf_op jit(solution)/shard_map/ppermute | solution.py:262
  78.7 3.7 %copy-start.2 = (bf16[2,256,1024]{2,1,0:T(8,128)(2,1)S(1)}, bf16[2,256,1024]{2,1,0:T(8,128)(2,1)}, u32[]{:S(2)}) copy-start(bf16[2,256,1024]{2,1,0:T(8,128)(2,1)} %left_ref.5) | copy-start | bytes 3145732
  86.5 18.9 %copy-start.3 = (bf16[2,256,1024]{2,1,0:T(8,128)(2,1)S(1)}, bf16[2,256,1024]{2,1,0:T(8,128)(2,1)}, u32[]{:S(2)}) copy-start(bf16[2,256,1024]{2,1,0:T(8,128)(2,1)} %left_ref.5) | copy-start | bytes 3145732
  86.5 9.0 %collective-permute-start.9 = (bf16[272,256]{1,0:T(8,128)(2,1)S(1)}, bf16[272,256]{1,0:T(8,128)(2,1)S(1)}, u32[]{:S(2)}, u32[]{:S(2)}) collective-permute-start(bf16[272,256]{1,0:T(8,128)(2,1)S(1)} %get-tuple-element.36), channel_id=1, source_target_pairs={{0,3},{1,0},{2,1},{3,2},{4,7},{5,4},{6,5},{7,6},{8,11},{9,8},{10,9... | collective-permute-start | bytes 417800 | tf_op jit(solution)/shard_map/ppermute | solution.py:262
  90.0 5.8 %collective-permute-start.10 = (bf16[272,256]{1,0:T(8,128)(2,1)S(1)}, bf16[272,256]{1,0:T(8,128)(2,1)S(1)}, u32[]{:S(2)}, u32[]{:S(2)}) collective-permute-start(bf16[272,256]{1,0:T(8,128)(2,1)S(1)} %get-tuple-element.37), channel_id=1, source_target_pairs={{0,2},{1,3},{2,0},{3,1},{4,6},{5,7},{6,4},{7,5},{8,10},{9,11},{10,... | collective-permute-start | bytes 417800 | tf_op jit(solution)/shard_map/ppermute | solution.py:262
  90.0 9.4 %collective-permute-start.11 = (bf16[272,256]{1,0:T(8,128)(2,1)S(1)}, bf16[272,256]{1,0:T(8,128)(2,1)S(1)}, u32[]{:S(2)}, u32[]{:S(2)}) collective-permute-start(bf16[272,256]{1,0:T(8,128)(2,1)S(1)} %get-tuple-element.38), channel_id=1, source_target_pairs={{0,1},{1,2},{2,3},{3,0},{4,5},{5,6},{6,7},{7,4},{8,9},{9,10},{10,1... | collective-permute-start | bytes 417800 | tf_op jit(solution)/shard_map/ppermute | solution.py:262
  100.3 20.8 %all-to-all-start.3 = ((bf16[32,32,256]{2,1,0:T(8,128)(2,1)}), bf16[32,32,256]{2,1,0:T(8,128)(2,1)}, u32[]{:S(2)}, u32[]{:S(2)}) async-start(bf16[32,32,256]{2,1,0:T(8,128)(2,1)} %bitcast.4), calls=%async_computation.3 | async-start | bytes 1048576 | tf_op jit(solution)/shard_map/all_to_all | solution.py:266
  109.5 19.4 %copy-start.1 = (f32[2,256,1024]{2,1,0:T(8,128)S(1)}, f32[2,256,1024]{2,1,0:T(8,128)}, u32[]{:S(2)}) copy-start(f32[2,256,1024]{2,1,0:T(8,128)} %left_ref.7) | copy-start | bytes 6291460
  109.5 5.0 %collective-permute-start.3 = (bf16[272,256]{1,0:T(8,128)(2,1)S(1)}, bf16[272,256]{1,0:T(8,128)(2,1)S(1)}, u32[]{:S(2)}, u32[]{:S(2)}) collective-permute-start(bf16[272,256]{1,0:T(8,128)(2,1)S(1)} %get-tuple-element.28), channel_id=1, source_target_pairs={{0,3},{1,0},{2,1},{3,2},{4,7},{5,4},{6,5},{7,6},{8,11},{9,8},{10,9... | collective-permute-start | bytes 417800 | tf_op jit(solution)/shard_map/ppermute | solution.py:262
  110.2 6.1 %collective-permute-start.4 = (bf16[272,256]{1,0:T(8,128)(2,1)S(1)}, bf16[272,256]{1,0:T(8,128)(2,1)S(1)}, u32[]{:S(2)}, u32[]{:S(2)}) collective-permute-start(bf16[272,256]{1,0:T(8,128)(2,1)S(1)} %get-tuple-element.29), channel_id=1, source_target_pairs={{0,2},{1,3},{2,0},{3,1},{4,6},{5,7},{6,4},{7,5},{8,10},{9,11},{10,... | collective-permute-start | bytes 417800 | tf_op jit(solution)/shard_map/ppermute | solution.py:262
  110.2 10.1 %collective-permute-start.5 = (bf16[272,256]{1,0:T(8,128)(2,1)S(1)}, bf16[272,256]{1,0:T(8,128)(2,1)S(1)}, u32[]{:S(2)}, u32[]{:S(2)}) collective-permute-start(bf16[272,256]{1,0:T(8,128)(2,1)S(1)} %get-tuple-element.30), channel_id=1, source_target_pairs={{0,1},{1,2},{2,3},{3,0},{4,5},{5,6},{6,7},{7,4},{8,9},{9,10},{10,1... | collective-permute-start | bytes 417800 | tf_op jit(solution)/shard_map/ppermute | solution.py:262
  120.4 0.8 copy-start.4
  121.2 19.4 %all-to-all-start.1 = ((bf16[32,32,256]{2,1,0:T(8,128)(2,1)}), bf16[32,32,256]{2,1,0:T(8,128)(2,1)}, u32[]{:S(2)}, u32[]{:S(2)}) async-start(bf16[32,32,256]{2,1,0:T(8,128)(2,1)} %bitcast.15), calls=%async_computation.1 | async-start | bytes 1048576 | tf_op jit(solution)/shard_map/all_to_all | solution.py:266
  133.3 7.3 %copy-start.8 = (s32[64]{0:T(128)S(1)}, s32[64]{0:T(128)}, u32[]{:S(2)}) copy-start(s32[64]{0:T(128)} %slot_ref.3) | copy-start | bytes 772

commit v2 on v0

v2 whole, which is shorter than its diff:
```python
import functools

import jax
import jax.numpy as jnp
from jax import lax
from jax.experimental import pallas as pl
from jax.experimental.pallas import tpu as pltpu
from jax.sharding import PartitionSpec as P

VMEM_LIMIT = 32 * 1024 * 1024
REPS = 4
OWNERS = 32
LANES = 128
NN = (((1,), (0,)), ((), ()))
NT = (((1,), (1,)), ((), ()))
TN = (((0,), (0,)), ((), ()))
ANY = pl.BlockSpec(memory_space=pl.ANY)
VMEM = pl.BlockSpec(memory_space=pltpu.VMEM)
SMEM = pl.BlockSpec(memory_space=pltpu.SMEM)
BF16 = jnp.bfloat16
F32 = jnp.float32


def params():
    return pltpu.CompilerParams(vmem_limit_bytes=VMEM_LIMIT)


def cost(flops, nbytes):
    return pl.CostEstimate(flops=flops, bytes_accessed=nbytes, transcendentals=0)


def dot(a, b, dims=NN):
    return lax.dot_general(a, b, dims, preferred_element_type=F32)


def shape(dims, dtype):
    return jax.ShapeDtypeStruct(dims, dtype)


def place():
    rep = lax.axis_index("rep").astype(jnp.int32)
    core = lax.rem(lax.axis_index("fsdp").astype(jnp.int32), 2)
    return jnp.stack([rep, lax.rem(rep, 2), lax.rem(rep + 1 - 2 * core + REPS, REPS)])


def to_neighbour(x):
    pairs = []
    for owner in range(OWNERS):
        step = 1 - 2 * (owner % 2)
        for rep in range(REPS):
            pairs.append((owner * REPS + rep, owner * REPS + (rep + step) % REPS))
    return lax.ppermute(x, ("fsdp", "rep"), pairs)


def shift(x, step):
    return lax.ppermute(x, "rep", [(i, (i + step) % REPS) for i in range(REPS)])


def everyone(x):
    return lax.all_to_all(x, ("fsdp", "rep"), split_axis=0, concat_axis=0, tiled=True)


def scatter_kernel(slot_ref, grads_ref, out_ref, sem):
    def body(b, _):
        slot = slot_ref[b]
        first = (slot // 2) * REPS + lax.rem(slot, 2)
        pltpu.make_async_copy(grads_ref.at[b], out_ref.at[first], sem).start()
        pltpu.make_async_copy(grads_ref.at[b], out_ref.at[first + 2], sem).start()
        return 0

    lax.fori_loop(0, grads_ref.shape[0], body, 0, unroll=8)
    pltpu.make_async_copy(out_ref, out_ref, sem).wait()


def scatter(owner_slot, grads):
    blocks, rows, cols = grads.shape
    return pl.pallas_call(
        scatter_kernel,
        out_shape=shape((2 * blocks, rows, cols), grads.dtype),
        in_specs=[SMEM, ANY],
        out_specs=ANY,
        scratch_shapes=[pltpu.SemaphoreType.DMA],
        compiler_params=params(),
        cost_estimate=cost(0, 6 * grads.size),
        name="scatter_blocks",
    )(owner_slot, grads)


def precond_kernel(at_ref, g_ref, l0_ref, l1_ref, l2_ref, l3_ref, right_ref, out_ref, sum_ref, left, mixed):
    rep = at_ref[0]
    owners, reps, row_part, part = g_ref.shape
    size = owners * row_part
    share = l0_ref.shape[0] * l0_ref.shape[1]
    for j, ref in enumerate((l0_ref, l1_ref, l2_ref, l3_ref)):
        first = lax.rem(rep - j + REPS, REPS) * share
        left[pl.ds(pl.multiple_of(first, share), share), :] = ref[...].reshape(share, size)
    for j in range(reps):
        column = g_ref[:, j].reshape(size, part)
        mixed[:, j * part : (j + 1) * part] = dot(left[...], column).astype(BF16)
    total = jnp.zeros((8, part), F32)
    for j in range(reps):
        piece = dot(mixed[...], right_ref[0, :, j * part : (j + 1) * part])
        total += jnp.sum((piece * piece).reshape(-1, 8, part), axis=0)
        out_ref[:, j, :, :part] = piece.astype(BF16).reshape(owners, -1, part)
    sum_ref[...] = total


def precond(at, arrived, left_parts, root_right):
    owners, reps, row_part, part = arrived.shape
    size = root_right.shape[1]
    half = row_part // 2
    return pl.pallas_call(
        precond_kernel,
        grid_spec=pltpu.PrefetchScalarGridSpec(
            num_scalar_prefetch=1,
            grid=(1,),
            in_specs=[VMEM] * 5 + [pl.BlockSpec((1, size, size), lambda i, at: (at[1], 0, 0))],
            out_specs=(VMEM, VMEM),
            scratch_shapes=[pltpu.VMEM((owners * half, size), BF16), pltpu.VMEM((owners * half, size), BF16)],
        ),
        out_shape=(shape((owners, reps, half, part + LANES), BF16), shape((8, part), F32)),
        compiler_params=params(),
        cost_estimate=cost(2 * size**3, 7 * size * size),
        name="precond_rows",
    )(at, arrived, *left_parts, root_right)


def adam_kernel(at_ref, own_ref, other_ref, mom_ref, sec_ref, pre_ref, _, mom_out, sec_out, out_ref, sums, pads, sem):
    which, step = pl.program_id(0), pl.program_id(1)
    chunk, reps, row_part, part = own_ref.shape
    rows = chunk * row_part

    @pl.when((which == 0) & (step == 0))
    def _():
        sums[...] = jnp.zeros_like(sums)

    def work(ref, i):
        total = jnp.zeros((8, part), F32)
        for j in range(reps):
            cols = slice(j * part, (j + 1) * part)
            grad = ref[:, j].reshape(rows, part).astype(F32)
            first = 0.9 * mom_ref[0, :, cols] + 0.1 * grad
            second = 0.95 * sec_ref[0, :, cols] + 0.05 * grad * grad
            mom_out[0, :, cols] = first
            sec_out[0, :, cols] = second
            way = first / (jnp.sqrt(second) + 1e-08)
            total += jnp.sum((way * way).reshape(rows // 8, 8, part), axis=0)
        sums[i] += total

    @pl.when(which == 0)
    def _():
        work(own_ref, 0)

    @pl.when(which == 1)
    def _():
        work(other_ref, 1)

    @pl.when((which == 1) & (step == pl.num_programs(1) - 1))
    def _():
        own, other = jnp.sum(sums[0]), jnp.sum(sums[1])
        even = at_ref[1] == 0
        values = (jnp.where(even, own, other), jnp.where(even, other, own), jnp.sum(pre_ref[...]))
        tile = pads.shape[2:]
        row = lax.broadcasted_iota(jnp.int32, tile, 0)
        pad = jnp.zeros(tile, F32)
        for i, value in enumerate(values):
            rest = jnp.full(tile, value, F32)
            for n in range(3):
                high = rest.astype(BF16).astype(F32)
                pad = jnp.where(row == 3 * i + n, high, pad)
                rest = rest - high
        pads[...] = jnp.broadcast_to(pad.astype(BF16), pads.shape)
        copy = pltpu.make_async_copy(pads, out_ref.at[:, :, :, pl.ds(part, LANES)], sem)
        copy.start()
        copy.wait()


def adam(at, arrived, other, moment, second, pre_sq, pieces, steps=4):
    owners, reps, row_part, part = arrived.shape
    _, rows, size = moment.shape
    chunk = other.shape[0] // steps
    state = pl.BlockSpec(
        (1, rows // steps, size), lambda i, n, at: (lax.rem(at[1] + i, 2), n, 0)
    )
    own_spec = pl.BlockSpec(
        (chunk, reps, row_part, part), lambda i, n, at: (at[0] * steps + jnp.where(i == 0, n, steps - 1), 0, 0, 0)
    )
    other_spec = pl.BlockSpec((chunk, reps, row_part, part), lambda i, n, at: (jnp.where(i == 0, 0, n), 0, 0, 0))
    return pl.pallas_call(
        adam_kernel,
        grid_spec=pltpu.PrefetchScalarGridSpec(
            num_scalar_prefetch=1,
            grid=(2, steps),
            in_specs=[own_spec, other_spec, state, state, VMEM, ANY],
            out_specs=(state, state, ANY),
            scratch_shapes=[
                pltpu.VMEM((2, 8, part), F32),
                pltpu.VMEM(pieces.shape[:3] + (LANES,), BF16),
                pltpu.SemaphoreType.DMA,
            ],
        ),
        out_shape=(shape(moment.shape, F32), shape(second.shape, F32), shape(pieces.shape, BF16)),
        input_output_aliases={6: 2},
        compiler_params=params(),
        cost_estimate=cost(30 * rows * size, 40 * rows * size),
        name="adam_rows",
    )(at, arrived, other, moment, second, pre_sq, pieces)


def left_kernel(at_ref, g_ref, stat_ref, new_ref, part_ref, whole, lhs):
    owners, reps, row_part, part = g_ref.shape
    size = owners * row_part
    rows = stat_ref.shape[1]
    blocks = rows // row_part
    for j in range(reps):
        cols = slice(j * part, (j + 1) * part)
        whole[:, cols] = g_ref[:, j].reshape(size, part)
        for i, index in enumerate((at_ref[0], at_ref[2])):
            lhs[i * rows : (i + 1) * rows, cols] = g_ref[pl.ds(index * blocks, blocks), j].reshape(rows, part)
    for j in range(reps):
        cols = slice(j * part, (j + 1) * part)
        term = 0.05 * dot(lhs[...], whole[cols, :], NT)
        new_ref[0, :, cols] = 0.95 * stat_ref[0, :, cols] + term[:rows]
        part_ref[:, cols] = term[rows:].astype(BF16)


def right_kernel(at_ref, g_ref, stat_ref, new_ref, part_ref, lhs):
    owners, reps, row_part, part = g_ref.shape
    size = owners * row_part
    rows = stat_ref.shape[1]
    for i, index in enumerate((at_ref[0], at_ref[2])):
        lhs[:, i * rows : (i + 1) * rows] = g_ref[:, pl.ds(index, 1)].reshape(size, part)
    for j in range(reps):
        cols = slice(j * part, (j + 1) * part)
        term = 0.05 * dot(lhs[...], g_ref[:, j].reshape(size, part), TN)
        new_ref[0, :, cols] = 0.95 * stat_ref[0, :, cols] + term[:rows]
        part_ref[:, cols] = term[rows:].astype(BF16)


def gram(kernel, scratch, at, arrived, stat):
    _, rows, size = stat.shape
    state = pl.BlockSpec((1, rows, size), lambda i, at: (at[1], 0, 0))
    return pl.pallas_call(
        kernel,
        grid_spec=pltpu.PrefetchScalarGridSpec(
            num_scalar_prefetch=1,
            grid=(1,),
            in_specs=[VMEM, state],
            out_specs=(state, VMEM),
            scratch_shapes=scratch,
        ),
        out_shape=(shape(stat.shape, F32), shape((rows, size), BF16)),
        compiler_params=params(),
        cost_estimate=cost(4 * rows * size * size, 12 * rows * size + 2 * size * size),
        name=kernel.__name__,
    )(at, arrived, stat)


def add_kernel(at_ref, left_part, right_part, left_ref, right_ref, _, __, left_out, right_out):
    left_out[0] = 0.95 * left_ref[0] + left_part[...].astype(F32)
    right_out[0] = 0.95 * right_ref[0] + right_part[...].astype(F32)


def add(at, left_part, right_part, gram_left, gram_right, left_new, right_new, steps=4):
    _, rows, size = gram_left.shape
    state = pl.BlockSpec((1, rows // steps, size), lambda n, at: (1 - at[1], n, 0))
    term = pl.BlockSpec((rows // steps, size), lambda n, at: (n, 0))
    return pl.pallas_call(
        add_kernel,
        grid_spec=pltpu.PrefetchScalarGridSpec(
            num_scalar_prefetch=1,
            grid=(steps,),
            in_specs=[term, term, state, state, ANY, ANY],
            out_specs=(state, state),
        ),
        out_shape=(shape(gram_left.shape, F32), shape(gram_right.shape, F32)),
        input_output_aliases={5: 0, 6: 1},
        compiler_params=params(),
        cost_estimate=cost(4 * rows * size, 20 * rows * size),
        name="add_terms",
    )(at, left_part, right_part, gram_left, gram_right, left_new, right_new)


def finish_kernel(cells, slot_ref, in_ref, out_ref, ratios):
    owners = in_ref.shape[0] // REPS
    half = in_ref.shape[1]
    part = in_ref.shape[2] - LANES

    def ratio(owner, _):
        sums = in_ref[pl.ds(owner * REPS, REPS), :, part:].astype(F32)
        adam_sums = jnp.sum(sums, axis=0)
        for k in range(2):
            pre_sums = sums[k] + sums[k + 2]
            adam_all = adam_sums[3 * k : 3 * k + 1] + adam_sums[3 * k + 1 : 3 * k + 2] + adam_sums[3 * k + 2 : 3 * k + 3]
            pre_all = pre_sums[6:7] + pre_sums[7:8] + pre_sums[8:9]
            value = jnp.sqrt(adam_all / cells + 1e-06) / jnp.sqrt(pre_all / cells + 1e-06)
            ratios[2 * owner + k] = jnp.broadcast_to(value, ratios.shape[1:])
        return 0

    lax.fori_loop(0, owners, ratio, 0, unroll=4)

    def place_block(b, _):
        slot = slot_ref[b]
        first = (slot // 2) * REPS + lax.rem(slot, 2)
        by = ratios[slot]
        by = jnp.concatenate([by] * (half // by.shape[0]), axis=0)
        by = jnp.concatenate([by] * (part // LANES), axis=1)
        for n in range(2):
            piece = in_ref[first + 2 * n, :, :part].astype(F32) * by
            out_ref[b, n * half : (n + 1) * half, :] = piece.astype(BF16)
        return 0

    lax.fori_loop(0, out_ref.shape[0], place_block, 0, unroll=4)


def finish(owner_slot, pieces, size):
    count, half, wide = pieces.shape
    blocks = owner_slot.shape[0]
    part = wide - LANES
    return pl.pallas_call(
        functools.partial(finish_kernel, float(size * size)),
        out_shape=shape((blocks, 2 * half, part), BF16),
        in_specs=[SMEM, VMEM],
        out_specs=VMEM,
        scratch_shapes=[pltpu.VMEM((blocks, 8, LANES), F32)],
        compiler_params=params(),
        cost_estimate=cost(4 * blocks * half * part, 10 * blocks * half * part),
        name="finish_updates",
    )(owner_slot, pieces)


def per_device(grads, owner_slot, gram_left, gram_right, root_left, root_right, moment, second):
    blocks, row_part, part = grads.shape
    _, rows, size = root_left.shape
    at = place()
    arrived = everyone(scatter(owner_slot, grads)).reshape(OWNERS, REPS, row_part, part)

    dealt = root_left.reshape(2, rows // row_part, 2, row_part // 2, size)
    dealt = jnp.transpose(dealt, (2, 0, 1, 3, 4)).reshape(REPS, rows // row_part, row_part // 2, size)
    own_parts = [
        lax.dynamic_index_in_dim(dealt, lax.rem(at[0] + j, REPS), 0, keepdims=False) for j in range(REPS)
    ]
    left_parts = own_parts[:1] + [shift(own_parts[j], j) for j in range(1, REPS)]

    count = rows // row_part
    other = to_neighbour(lax.dynamic_slice_in_dim(arrived, at[2] * count, count, 0))
    pieces, pre_sq = precond(at, arrived, left_parts, root_right)
    left_new, left_term = gram(
        left_kernel,
        [pltpu.VMEM((size, size), BF16), pltpu.VMEM((2 * rows, size), BF16)],
        at,
        arrived,
        gram_left,
    )
    left_term = to_neighbour(left_term)
    moment_new, second_new, pieces = adam(at, arrived, other, moment, second, pre_sq, pieces)
    homed = everyone(pieces.reshape(OWNERS * REPS, row_part // 2, part + LANES))
    right_new, right_term = gram(
        right_kernel, [pltpu.VMEM((size, 2 * rows), BF16)], at, arrived, gram_right
    )
    right_term = to_neighbour(right_term)
    left_new, right_new = add(at, left_term, right_term, gram_left, gram_right, left_new, right_new)
    updates = finish(owner_slot, homed, size)
    return (updates, left_new, right_new, moment_new, second_new)


def solution(mesh):
    return jax.shard_map(
        per_device,
        mesh=mesh,
        in_specs=(
            P(None, "fsdp", "rep"),
            P(),
            P("fsdp", "rep", None),
            P("fsdp", "rep", None),
            P("fsdp", "rep", None),
            P("fsdp", None, None),
            P("fsdp", "rep", None),
            P("fsdp", "rep", None),
        ),
        out_specs=(
            P(None, "fsdp", "rep"),
            P("fsdp", "rep", None),
            P("fsdp", "rep", None),
            P("fsdp", "rep", None),
            P("fsdp", "rep", None),
        ),
        check_vma=False,
    )
```

time: 164 us -> 127 us (0.77)
  Pallas kernels: 0 us -> 24.5 us
  matrix products: 19.8 us -> 0 us
  local copies, waits for them, and re-layouts: 31.1 us -> 12.1 us
  waiting for transfers between devices: 72.8 us -> 63.4 us
  other arithmetic: 7.97 us -> 0.08 us
  blocking collectives: 6.36 us -> 0 us
    all_to_all x3 -> x2, waiting for transfers between devices: 72.8 us -> 29.9 us  [everyone(): lax.all_to_all(x, ('fsdp', 'rep'), split_axis=0, concat_axis=0, tiled=True)]
    ppermute x0 -> x6, waiting for transfers between devices: none -> 33.5 us  [the longest x3 19.3 us: to_neighbour(): return lax.ppermute(x, ('fsdp', 'rep'), pairs)]
    pallas_call x0 -> x7, Pallas kernels: none -> 24.5 us  [the longest x2 5.52 us: gram(): pl.pallas_call(kernel, grid_spec=pltpu.PrefetchScalarGridSpec(num_scalar_...]
    dot_general x3 -> x0, matrix products: 19.8 us -> none  [the longest x1 11 us: per_device(): jnp.einsum('nik,nkj->nij', root_left, product, preferred_element_type=jnp...]
    transpose x1, local copies, waits for them, and re-layouts: 12.5 us -> 1.05 us  [per_device(): jnp.transpose(dealt, (2, 0, 1, 3, 4))]
    unnamed x10 -> x22, local copies, waits for them, and re-layouts: 0.03 us -> 8.11 us
    reshape x1 -> x0, local copies, waits for them, and re-layouts: 7.71 us -> none  [per_device(): jnp.transpose(arrived, (0, 1, 3, 2, 4))]
    ppermute x0 -> x6, starting transfers between devices: none -> 6.55 us  [the longest x3 3.3 us: to_neighbour(): return lax.ppermute(x, ('fsdp', 'rep'), pairs)]
  transfers between devices with their start and end apart: 3 -> 8, of which waited for: 3 -> 5; matrix products, arithmetic and copies ran while one was open for 5% -> 3% of each run, Pallas kernels for 0% -> 10%
where the time goes in v2:
time: 127 us; the launch traced here: 126 us
  waiting for transfers between devices  63.4 us (50%)
  starting transfers between devices  25.1 us (20%)
  Pallas kernels  24.5 us (19%)
  local copies, waits for them, and re-layouts  12.1 us (10%)
    all_to_all x2, waiting for transfers between devices, everyone(): lax.all_to_all(x, ('fsdp', 'rep'), split_axis=0, concat_axis=0, tiled=True)  29.9 us
    ppermute x3, waiting for transfers between devices, to_neighbour(): return lax.ppermute(x, ('fsdp', 'rep'), pairs)  19.3 us
    all_to_all x2, starting transfers between devices, everyone(): lax.all_to_all(x, ('fsdp', 'rep'), split_axis=0, concat_axis=0, tiled=True)  18.5 us
    ppermute x3, waiting for transfers between devices, shift(): return lax.ppermute(x, 'rep', [(i, (i + step) % REPS) for i in range(REPS)])  14.1 us
    unnamed x22, local copies, waits for them, and re-layouts  8.11 us
    pallas_call x2, Pallas kernels, gram(): pl.pallas_call(kernel, grid_spec=pltpu.PrefetchScalarGridSpec(num_scalar_...  5.52 us
    pallas_call x1, Pallas kernels, adam(): pl.pallas_call(adam_kernel, grid_spec=pltpu.PrefetchScalarGridSpec(num_sc...  5.08 us
    pallas_call x1, Pallas kernels, precond(): pl.pallas_call(precond_kernel, grid_spec=pltpu.PrefetchScalarGridSpec(num...  4.11 us
  transfers between devices with their start and end apart: 8, of which 5 were waited for; matrix products, arithmetic and copies ran while one was open for 3% of the time, Pallas kernels for 10%

profile of v2, /device:TPU:1, one launch (start us, length us, event | category | flops | bytes accessed | tf_op | source)
XLA Modules:
  0.0 125.8 jit_solution(10657612680149448448)
XLA Ops:
  0.6 1.2 copy-done.6
  1.9 0.7 copy-done.7
  2.5 4.0 %scatter_blocks.1 = bf16[128,32,256]{2,1,0:T(8,128)(2,1)S(1)} custom-call(s32[64]{0:T(128)S(1)} %copy-done.7, bf16[64,32,256]{2,1,0:T(8,128)(2,1)S(1)} %copy-done.6), custom_call_target="tpu_custom_call" | custom-call | bytes 3145728 | tf_op jit(solution)/shard_map/scatter_blocks/pallas_call | solution.py:77
  6.5 0.0 copy-start.2
  6.5 1.3 %copy-done.2 = bf16[128,32,256]{2,1,0:T(8,128)(2,1)} copy-done((bf16[128,32,256]{2,1,0:T(8,128)(2,1)}, bf16[128,32,256]{2,1,0:T(8,128)(2,1)S(1)}, u32[]{:S(2)}) %copy-start.2) | copy-done | bytes 2097176
  7.9 11.5 %all-to-all-start = ((bf16[128,32,256]{2,1,0:T(8,128)(2,1)}), bf16[128,32,256]{2,1,0:T(8,128)(2,1)S(1)}, u32[]{:S(2)}, u32[]{:S(2)}) async-start(bf16[128,32,256]{2,1,0:T(8,128)(2,1)} %copy-done.2), calls=%async_computation | async-start | bytes 4194304 | tf_op jit(solution)/shard_map/all_to_all | solution.py:60
  19.4 1.0 copy.16
  20.5 29.9 %all-to-all-done = bf16[128,32,256]{2,1,0:T(8,128)(2,1)S(1)} async-done(((bf16[128,32,256]{2,1,0:T(8,128)(2,1)}), bf16[128,32,256]{2,1,0:T(8,128)(2,1)S(1)}, u32[]{:S(2)}, u32[]{:S(2)}) %all-to-all-start) | async-done | bytes 2097184 | tf_op jit(solution)/shard_map/all_to_all | solution.py:60
  50.4 0.8 constant_dynamic-slice_fusion
  51.2 2.1 %dynamic-slice_bitcast_fusion = (bf16[8,16,1024]{2,1,0:T(8,128)(2,1)}, bf16[8,16,1024]{2,1,0:T(8,128)(2,1)}, bf16[8,16,1024]{2,1,0:T(8,128)(2,1)}, bf16[8,16,1024]{2,1,0:T(8,128)(2,1)S(1)}) fusion(bf16[4,8,16,1024]{3,2,1,0:T(8,128)(2,1)} %bitcast.23, s32[]{:T(128)S(6)} %select_n.20, s32[]{:T(128)S(6)} %select_n.19, s32[]{:T(128)S(6)} %select_n.18, s32[]{:T(128)S(6)} %select_n.17), kind=kLoop, calls=%fused_computation | loop fusion | bytes 2097168 | tf_op jit(solution)/shard_map/jit(dynamic_index_in_dim)/squeeze | solution.py:341
  53.3 0.1 collective-permute-start.3
  53.4 3.1 %collective-permute-start.2 = (bf16[8,16,1024]{2,1,0:T(8,128)(2,1)}, bf16[8,16,1024]{2,1,0:T(8,128)(2,1)S(1)}, u32[]{:S(2)}, u32[]{:S(2)}) collective-permute-start(bf16[8,16,1024]{2,1,0:T(8,128)(2,1)} %get-tuple-element.28), channel_id=1, source_target_pairs={{0,2},{1,3},{2,0},{3,1},{4,6},{5,7},{6,4},{7,5},{8,10},{9,11},{10,... | collective-permute-start | bytes 786440 | tf_op jit(solution)/shard_map/ppermute | solution.py:56
  56.5 0.1 pad_add_fusion.at_ref
  56.6 10.9 %collective-permute-done.3.l3_ref = bf16[8,16,1024]{2,1,0:T(8,128)(2,1)S(1)} collective-permute-done((bf16[8,16,1024]{2,1,0:T(8,128)(2,1)}, bf16[8,16,1024]{2,1,0:T(8,128)(2,1)S(1)}, u32[]{:S(2)}, u32[]{:S(2)}) %collective-permute-start.3) | collective-permute-done | bytes 262176 | tf_op jit(solution)/shard_map/ppermute | solution.py:56
  67.5 0.0 collective-permute-done.2.l2_ref
  67.5 3.3 %collective-permute-done.1.l1_ref = bf16[8,16,1024]{2,1,0:T(8,128)(2,1)} collective-permute-done((bf16[8,16,1024]{2,1,0:T(8,128)(2,1)}, bf16[8,16,1024]{2,1,0:T(8,128)(2,1)}, u32[]{:S(2)}, u32[]{:S(2)}) %collective-permute-start.1) | collective-permute-done | bytes 262176 | tf_op jit(solution)/shard_map/ppermute | solution.py:56
  70.7 2.2 %copy-done.9 = bf16[2,1024,1024]{2,1,0:T(8,128)(2,1)S(1)} copy-done((bf16[2,1024,1024]{2,1,0:T(8,128)(2,1)S(1)}, bf16[2,1024,1024]{2,1,0:T(8,128)(2,1)}, u32[]{:S(2)}) %copy-start.9) | copy-done | bytes 4194328
  72.9 4.1 %precond_rows.1 = (bf16[32,4,16,384]{3,2,1,0:T(8,128)(2,1)S(1)}, f32[8,256]{1,0:T(8,128)S(1)}) custom-call(s32[3]{0:T(128)S(1)} %pad_add_fusion.at_ref, bf16[32,4,32,256]{3,2,1,0:T(8,128)(2,1)S(1)} %bitcast.18, bf16[8,16,1024]{2,1,0:T(8,128)(2,1)S(1)} %get-tuple-element.30.l0_ref, bf16[8,16,1024]{2,1,0:T(8,128)(2,1)} %collective-permute-done.1.l1_ref, ...), custom_call_target="tpu_custom_call" | custom-call | flops 2147483648 | bytes 7340032 | tf_op jit(solution)/shard_map/precond_rows/pallas_call | solution.py:112
  77.1 0.0 collective-permute-done.other_ref
  77.1 5.1 %adam_rows.1 = (f32[2,256,1024]{2,1,0:T(8,128)}, f32[2,256,1024]{2,1,0:T(8,128)}, bf16[32,4,16,384]{3,2,1,0:T(8,128)(2,1)S(1)}) custom-call(s32[3]{0:T(128)S(1)} %pad_add_fusion.at_ref, bf16[32,4,32,256]{3,2,1,0:T(8,128)(2,1)S(1)} %bitcast.19, bf16[8,4,32,256]{3,2,1,0:T(8,128)(2,1)S(1)} %collective-permute-done.other_ref, ...), custom_call_target="tpu_custom_call", output_to_operand_aliasing={{2}: (6, {})} | custom-call | flops 7864320 | bytes 10485760 | tf_op jit(solution)/shard_map/adam_rows/pallas_call | solution.py:189
  82.2 1.1 copy-done.3
  83.3 7.0 %all-to-all-start.1 = ((bf16[128,16,384]{2,1,0:T(8,128)(2,1)}), bf16[128,16,384]{2,1,0:T(8,128)(2,1)}, u32[]{:S(2)}, u32[]{:S(2)}) async-start(bf16[128,16,384]{2,1,0:T(8,128)(2,1)} %bitcast.22), calls=%async_computation.1 | async-start | bytes 3145728 | tf_op jit(solution)/shard_map/all_to_all | solution.py:60
  90.4 0.0 copy-start.1
  90.4 1.6 %copy-done.1 = f32[2,256,1024]{2,1,0:T(8,128)S(1)} copy-done((f32[2,256,1024]{2,1,0:T(8,128)S(1)}, f32[2,256,1024]{2,1,0:T(8,128)}, u32[]{:S(2)}) %copy-start.1) | copy-done | bytes 2097176
  92.0 2.8 %right_kernel.1 = (f32[2,256,1024]{2,1,0:T(8,128)}, bf16[256,1024]{1,0:T(8,128)(2,1)S(1)}) custom-call(s32[3]{0:T(128)S(1)} %pad_add_fusion.at_ref, bf16[32,4,32,256]{3,2,1,0:T(8,128)(2,1)S(1)} %bitcast.20, f32[2,256,1024]{2,1,0:T(8,128)S(1)} %copy-done.1), custom_call_target="tpu_custom_call" | custom-call | flops 1073741824 | bytes 5242880 | tf_op jit(solution)/shard_map/right_kernel/pallas_call | solution.py:243
  94.7 2.8 %collective-permute-start.5 = (bf16[256,1024]{1,0:T(8,128)(2,1)S(1)}, bf16[256,1024]{1,0:T(8,128)(2,1)S(1)}, u32[]{:S(2)}, u32[]{:S(2)}) collective-permute-start(bf16[256,1024]{1,0:T(8,128)(2,1)S(1)} %get-tuple-element.20), channel_id=1, source_target_pairs={{0,1},{1,2},{2,3},{3,0},{4,7},{5,4},{6,5},{7,6},{8,9},{9,10},{10,1... | collective-permute-start | bytes 1572872 | tf_op jit(solution)/shard_map/ppermute | solution.py:52
  97.5 2.7 %left_kernel.1 = (f32[2,256,1024]{2,1,0:T(8,128)}, bf16[256,1024]{1,0:T(8,128)(2,1)S(1)}) custom-call(s32[3]{0:T(128)S(1)} %pad_add_fusion.at_ref, bf16[32,4,32,256]{3,2,1,0:T(8,128)(2,1)S(1)} %bitcast.21, f32[2,256,1024]{2,1,0:T(8,128)S(1)} %copy-done), custom_call_target="tpu_custom_call" | custom-call | flops 1073741824 | bytes 5242880 | tf_op jit(solution)/shard_map/left_kernel/pallas_call | solution.py:243
  100.3 0.5 collective-permute-start.4
  100.8 13.8 %collective-permute-done.5.right_part = bf16[256,1024]{1,0:T(8,128)(2,1)S(1)} collective-permute-done((bf16[256,1024]{1,0:T(8,128)(2,1)S(1)}, bf16[256,1024]{1,0:T(8,128)(2,1)S(1)}, u32[]{:S(2)}, u32[]{:S(2)}) %collective-permute-start.5) | collective-permute-done | bytes 524320 | tf_op jit(solution)/shard_map/ppermute | solution.py:52
  114.6 5.5 %collective-permute-done.4.left_part = bf16[256,1024]{1,0:T(8,128)(2,1)S(1)} collective-permute-done((bf16[256,1024]{1,0:T(8,128)(2,1)S(1)}, bf16[256,1024]{1,0:T(8,128)(2,1)S(1)}, u32[]{:S(2)}, u32[]{:S(2)}) %collective-permute-start.4) | collective-permute-done | bytes 524320 | tf_op jit(solution)/shard_map/ppermute | solution.py:52
  120.1 2.4 %add_terms.1 = (f32[2,256,1024]{2,1,0:T(8,128)}, f32[2,256,1024]{2,1,0:T(8,128)}) custom-call(s32[3]{0:T(128)S(1)} %pad_add_fusion.at_ref, bf16[256,1024]{1,0:T(8,128)(2,1)S(1)} %collective-permute-done.4.left_part, bf16[256,1024]{1,0:T(8,128)(2,1)S(1)} %collective-permute-done.5.right_part, ...), custom_call_target="tpu_custom_call", output_to_operand_aliasing={{0}: (5, {}), {1}: (6, {})} | custom-call | flops 1048576 | bytes 5242880 | tf_op jit(solution)/shard_map/add_terms/pallas_call | solution.py:268
  122.5 3.3 %finish_updates.1 = bf16[64,32,256]{2,1,0:T(8,128)(2,1)} custom-call(s32[64]{0:T(128)S(1)} %copy-done.8, bf16[128,16,384]{2,1,0:T(8,128)(2,1)} %all-to-all-done.1.in_ref), custom_call_target="tpu_custom_call" | custom-call | flops 1048576 | bytes 2621440 | tf_op jit(solution)/shard_map/finish_updates/pallas_call | solution.py:320
  (17 shorter events, 0.0 us)
Async XLA Ops:
  0.6 1.2 copy-start.6
  1.9 0.7 copy-start.7
  6.5 1.3 %copy-start.2 = (bf16[128,32,256]{2,1,0:T(8,128)(2,1)}, bf16[128,32,256]{2,1,0:T(8,128)(2,1)S(1)}, u32[]{:S(2)}) copy-start(bf16[128,32,256]{2,1,0:T(8,128)(2,1)S(1)} %scatter_blocks.1) | copy-start | bytes 6291460
  7.9 11.5 %copy-start.10 = (bf16[2,256,1024]{2,1,0:T(8,128)(2,1)S(1)}, bf16[2,256,1024]{2,1,0:T(8,128)(2,1)}, u32[]{:S(2)}) copy-start(bf16[2,256,1024]{2,1,0:T(8,128)(2,1)} %param.12) | copy-start | bytes 3145732
  7.9 42.5 %all-to-all-start = ((bf16[128,32,256]{2,1,0:T(8,128)(2,1)}), bf16[128,32,256]{2,1,0:T(8,128)(2,1)S(1)}, u32[]{:S(2)}, u32[]{:S(2)}) async-start(bf16[128,32,256]{2,1,0:T(8,128)(2,1)} %copy-done.2), calls=%async_computation | async-start | bytes 4194304 | tf_op jit(solution)/shard_map/all_to_all | solution.py:60
  51.2 25.9 %collective-permute-start = (bf16[8,4,32,256]{3,2,1,0:T(8,128)(2,1)}, bf16[8,4,32,256]{3,2,1,0:T(8,128)(2,1)S(1)}, u32[]{:S(2)}, u32[]{:S(2)}) collective-permute-start(bf16[8,4,32,256]{3,2,1,0:T(8,128)(2,1)} %constant_dynamic-slice_fusion), channel_id=1, source_target_pairs={{0,1},{1,2},{2,3},{3,0},{4,7},{5,4},{6,5},{7,6},{8,9},{9,10},{10,1... | collective-permute-start | bytes 1572872 | tf_op jit(solution)/shard_map/ppermute | solution.py:52
  53.3 14.2 %collective-permute-start.3 = (bf16[8,16,1024]{2,1,0:T(8,128)(2,1)}, bf16[8,16,1024]{2,1,0:T(8,128)(2,1)S(1)}, u32[]{:S(2)}, u32[]{:S(2)}) collective-permute-start(bf16[8,16,1024]{2,1,0:T(8,128)(2,1)} %get-tuple-element.27), channel_id=1, source_target_pairs={{0,3},{1,0},{2,1},{3,2},{4,7},{5,4},{6,5},{7,6},{8,11},{9,8},{10,9... | collective-permute-start | bytes 786440 | tf_op jit(solution)/shard_map/ppermute | solution.py:56
  53.4 14.1 %collective-permute-start.2 = (bf16[8,16,1024]{2,1,0:T(8,128)(2,1)}, bf16[8,16,1024]{2,1,0:T(8,128)(2,1)S(1)}, u32[]{:S(2)}, u32[]{:S(2)}) collective-permute-start(bf16[8,16,1024]{2,1,0:T(8,128)(2,1)} %get-tuple-element.28), channel_id=1, source_target_pairs={{0,2},{1,3},{2,0},{3,1},{4,6},{5,7},{6,4},{7,5},{8,10},{9,11},{10,... | collective-permute-start | bytes 786440 | tf_op jit(solution)/shard_map/ppermute | solution.py:56
  56.5 14.2 %collective-permute-start.1 = (bf16[8,16,1024]{2,1,0:T(8,128)(2,1)}, bf16[8,16,1024]{2,1,0:T(8,128)(2,1)}, u32[]{:S(2)}, u32[]{:S(2)}) collective-permute-start(bf16[8,16,1024]{2,1,0:T(8,128)(2,1)} %get-tuple-element.29), channel_id=1, source_target_pairs={{0,1},{1,2},{2,3},{3,0},{4,5},{5,6},{6,7},{7,4},{8,9},{9,10},{10,1... | collective-permute-start | bytes 786440 | tf_op jit(solution)/shard_map/ppermute | solution.py:56
  70.7 2.2 %copy-start.9 = (bf16[2,1024,1024]{2,1,0:T(8,128)(2,1)S(1)}, bf16[2,1024,1024]{2,1,0:T(8,128)(2,1)}, u32[]{:S(2)}) copy-start(bf16[2,1024,1024]{2,1,0:T(8,128)(2,1)} %right_ref.2) | copy-start | bytes 12582916
  72.9 4.1 %copy-start.4 = (f32[2,256,1024]{2,1,0:T(8,128)S(1)}, f32[2,256,1024]{2,1,0:T(8,128)}, u32[]{:S(2)}) copy-start(f32[2,256,1024]{2,1,0:T(8,128)} %mom_ref.1) | copy-start | bytes 6291460
  72.9 4.1 %copy-start.5 = (f32[2,256,1024]{2,1,0:T(8,128)S(1)}, f32[2,256,1024]{2,1,0:T(8,128)}, u32[]{:S(2)}) copy-start(f32[2,256,1024]{2,1,0:T(8,128)} %sec_ref.1) | copy-start | bytes 6291460
  82.2 1.1 copy-start.3
  83.3 39.2 %all-to-all-start.1 = ((bf16[128,16,384]{2,1,0:T(8,128)(2,1)}), bf16[128,16,384]{2,1,0:T(8,128)(2,1)}, u32[]{:S(2)}, u32[]{:S(2)}) async-start(bf16[128,16,384]{2,1,0:T(8,128)(2,1)} %bitcast.22), calls=%async_computation.1 | async-start | bytes 3145728 | tf_op jit(solution)/shard_map/all_to_all | solution.py:60
  90.4 1.6 %copy-start.1 = (f32[2,256,1024]{2,1,0:T(8,128)S(1)}, f32[2,256,1024]{2,1,0:T(8,128)}, u32[]{:S(2)}) copy-start(f32[2,256,1024]{2,1,0:T(8,128)} %right_ref.3) | copy-start | bytes 6291460
  92.0 5.6 %copy-start = (f32[2,256,1024]{2,1,0:T(8,128)S(1)}, f32[2,256,1024]{2,1,0:T(8,128)}, u32[]{:S(2)}) copy-start(f32[2,256,1024]{2,1,0:T(8,128)} %left_ref.1) | copy-start | bytes 6291460
  94.7 19.8 %collective-permute-start.5 = (bf16[256,1024]{1,0:T(8,128)(2,1)S(1)}, bf16[256,1024]{1,0:T(8,128)(2,1)S(1)}, u32[]{:S(2)}, u32[]{:S(2)}) collective-permute-start(bf16[256,1024]{1,0:T(8,128)(2,1)S(1)} %get-tuple-element.20), channel_id=1, source_target_pairs={{0,1},{1,2},{2,3},{3,0},{4,7},{5,4},{6,5},{7,6},{8,9},{9,10},{10,1... | collective-permute-start | bytes 1572872 | tf_op jit(solution)/shard_map/ppermute | solution.py:52
  100.3 19.8 %collective-permute-start.4 = (bf16[256,1024]{1,0:T(8,128)(2,1)S(1)}, bf16[256,1024]{1,0:T(8,128)(2,1)S(1)}, u32[]{:S(2)}, u32[]{:S(2)}) collective-permute-start(bf16[256,1024]{1,0:T(8,128)(2,1)S(1)} %get-tuple-element.19), channel_id=1, source_target_pairs={{0,1},{1,2},{2,3},{3,0},{4,7},{5,4},{6,5},{7,6},{8,9},{9,10},{10,1... | collective-permute-start | bytes 1572872 | tf_op jit(solution)/shard_map/ppermute | solution.py:52
  120.1 2.4 %copy-start.8 = (s32[64]{0:T(128)S(1)}, s32[64]{0:T(128)}, u32[]{:S(2)}) copy-start(s32[64]{0:T(128)} %slot_ref.3) | copy-start | bytes 772

commit v3 on v0

v3 whole, which is shorter than its diff:
```python
import functools

import jax
import jax.numpy as jnp
from jax import lax
from jax.experimental import pallas as pl
from jax.experimental.pallas import tpu as pltpu
from jax.sharding import PartitionSpec as P

VMEM_LIMIT = 32 * 1024 * 1024
MID_LIMIT = 60 * 1024 * 1024
LATE_LIMIT = 60 * 1024 * 1024
REPS = 4
OWNERS = 32
LANES = 128
NN = (((1,), (0,)), ((), ()))
NT = (((1,), (1,)), ((), ()))
TN = (((0,), (0,)), ((), ()))
ANY = pl.BlockSpec(memory_space=pl.ANY)
VMEM = pl.BlockSpec(memory_space=pltpu.VMEM)
SMEM = pl.BlockSpec(memory_space=pltpu.SMEM)
BF16 = jnp.bfloat16
F32 = jnp.float32


def params(limit=VMEM_LIMIT):
    return pltpu.CompilerParams(vmem_limit_bytes=limit)


def cost(flops, nbytes):
    return pl.CostEstimate(flops=flops, bytes_accessed=nbytes, transcendentals=0)


def dot(a, b, dims=NN):
    return lax.dot_general(a, b, dims, preferred_element_type=F32)


def shape(dims, dtype):
    return jax.ShapeDtypeStruct(dims, dtype)


GRAM_COST = cost(1, 1)
MID_COST = cost(10**11, 10**6)


def place():
    rep = lax.axis_index("rep").astype(jnp.int32)
    core = lax.rem(lax.axis_index("fsdp").astype(jnp.int32), 2)
    step = 1 - 2 * core
    return jnp.stack([rep, lax.rem(rep, 2), lax.rem(rep + step + REPS, REPS), step])


def to_neighbour(x, far=1):
    pairs = []
    for owner in range(OWNERS):
        step = far * (1 - 2 * (owner % 2))
        for rep in range(REPS):
            pairs.append((owner * REPS + rep, owner * REPS + (rep + step) % REPS))
    return lax.ppermute(x, ("fsdp", "rep"), pairs)


def everyone(x):
    return lax.all_to_all(x, ("fsdp", "rep"), split_axis=0, concat_axis=0, tiled=True)


def deal_kernel(at_ref, slot_ref, grads_ref, left_ref, out_ref, keep_ref, ahead_ref, across_ref, back_ref):
    def share(j):
        to = lax.rem(at_ref[0] + j * at_ref[3] + REPS, REPS)
        return left_ref[lax.rem(to, 2), :, to // 2]

    keep_ref[...] = share(0)
    ahead_ref[...] = share(1)
    across_ref[...] = share(2)
    back_ref[...] = share(-1)

    def body(b, _):
        slot = slot_ref[b]
        first = (slot // 2) * REPS + lax.rem(slot, 2)
        block = grads_ref[b]
        out_ref[first] = block
        out_ref[first + 2] = block
        return 0

    lax.fori_loop(0, grads_ref.shape[0], body, 0, unroll=8)


def deal(at, owner_slot, grads, root_left):
    blocks, row_part, part = grads.shape
    _, rows, size = root_left.shape
    count, half = rows // row_part, row_part // 2
    return pl.pallas_call(
        deal_kernel,
        out_shape=(
            shape((2 * blocks, row_part, part), BF16),
        )
        + (shape((count, half, size), BF16),) * REPS,
        in_specs=[SMEM, SMEM, VMEM, VMEM],
        out_specs=(VMEM,) * (1 + REPS),
        compiler_params=params(60 * 1024 * 1024),
        cost_estimate=cost(0, 6 * grads.size + 4 * root_left.size),
        name="deal_blocks",
    )(at, owner_slot, grads, root_left.reshape(2, count, 2, half, size))


def load(src, dst, sem):
    copy = pltpu.make_async_copy(src, dst, sem)
    copy.start()
    return copy


def load_columns(arrived, whole, sems):
    part = arrived.shape[3]
    return [
        load(arrived.at[:, j], whole.at[:, :, pl.ds(j * part, part)], sems.at[j]) for j in range(arrived.shape[1])
    ]


def gram_kernel(
    at_ref, arrived, stat_left, stat_right, left_out, right_out, left_term, right_term, whole, lhs, gl, gr, sems, out_sems
):
    rep, k, near = at_ref[0], at_ref[1], at_ref[2]
    _, row_part, size = whole.shape
    part = size // REPS
    rows = gl.shape[0]
    columns = load_columns(arrived, whole, sems)
    get_gr = load(stat_right.at[k], gr, sems.at[REPS])
    get_gl = load(stat_left.at[k], gl, sems.at[REPS + 1])
    for copy in columns:
        copy.wait()

    grad = whole[...].reshape(size, size)
    for i, index in enumerate((rep, near)):
        cols = whole[:, :, pl.ds(pl.multiple_of(index * part, part), part)].reshape(size, part)
        term = 0.05 * dot(cols, grad, TN)
        if i == 0:
            get_gr.wait()
            gr[...] = 0.95 * gr[...] + term
            put_right = load(gr, right_out.at[k], out_sems.at[0])
        else:
            right_term[...] = term.astype(BF16)
    for i, index in enumerate((rep, near)):
        from_row = pl.ds(index * (rows // row_part), rows // row_part)
        lhs[i * rows : (i + 1) * rows, :] = whole[from_row].reshape(rows, size)
    term = 0.05 * dot(lhs[...], grad, NT)
    get_gl.wait()
    gl[...] = 0.95 * gl[...] + term[:rows]
    put_left = load(gl, left_out.at[k], out_sems.at[1])
    left_term[...] = term[rows:].astype(BF16)
    put_left.wait()
    put_right.wait()


def grams(at, arrived, gram_left, gram_right):
    owners, reps, row_part, part = arrived.shape
    _, rows, size = gram_left.shape
    state = shape(gram_left.shape, F32)
    return pl.pallas_call(
        gram_kernel,
        in_specs=[SMEM] + [ANY] * 3,
        out_specs=(ANY,) * 2 + (VMEM,) * 2,
        scratch_shapes=[
            pltpu.VMEM((owners, row_part, size), BF16),
            pltpu.VMEM((2 * rows, size), BF16),
            pltpu.VMEM((rows, size), F32),
            pltpu.VMEM((rows, size), F32),
            pltpu.SemaphoreType.DMA((REPS + 2,)),
            pltpu.SemaphoreType.DMA((2,)),
        ],
        out_shape=(state,) * 2 + (shape((rows, size), BF16),) * 2,
        compiler_params=params(MID_LIMIT),
        cost_estimate=GRAM_COST,
        name="own_grams",
    )(at, arrived, gram_left, gram_right)


def mid_kernel(
    at_ref,
    arrived,
    l0_ref,
    l1_ref,
    l2_ref,
    l3_ref,
    right_ref,
    mom_ref,
    sec_ref,
    mom_out,
    sec_out,
    pieces,
    pre_sum,
    own_sum,
    whole,
    left,
    right,
    mixed,
    mom,
    sec,
    sems,
    out_sems,
):
    rep, k, step = at_ref[0], at_ref[1], at_ref[3]
    owners, row_part, size = whole.shape
    part = size // REPS
    rows = mom.shape[0]
    share = l0_ref.shape[0]
    columns = load_columns(arrived, whole, sems)
    get_mom = load(mom_ref.at[k], mom, sems.at[REPS])
    get_sec = load(sec_ref.at[k], sec, sems.at[REPS + 1])
    get_left = []
    for j, ref in enumerate((l0_ref, l1_ref, l2_ref, l3_ref)):
        first = lax.rem(rep - j * step + REPS * REPS, REPS) * share
        get_left.append(load(ref, left.at[pl.ds(first, share)], sems.at[REPS + 2 + j]))
    get_right = load(right_ref.at[k], right, sems.at[2 * REPS + 2])
    for copy in columns + get_left:
        copy.wait()
    grad = whole[...].reshape(size, size)
    mixed[...] = dot(left[...].reshape(mixed.shape), grad).astype(BF16)

    get_mom.wait()
    get_sec.wait()
    own = whole[pl.ds(rep * (rows // row_part), rows // row_part)].reshape(rows, size).astype(F32)
    first = 0.9 * mom[...] + 0.1 * own
    second = 0.95 * sec[...] + 0.05 * own * own
    mom[...] = first
    sec[...] = second
    put_mom = load(mom, mom_out.at[k], out_sems.at[0])
    put_sec = load(sec, sec_out.at[k], out_sems.at[1])
    way = first / (jnp.sqrt(second) + 1e-08)
    own_sum[...] = jnp.sum((way * way).reshape(rows // 8, 8, size), axis=0)

    get_right.wait()
    total = jnp.zeros((8, part), F32)
    for j in range(REPS):
        piece = dot(mixed[...], right[:, j * part : (j + 1) * part])
        total += jnp.sum((piece * piece).reshape(-1, 8, part), axis=0)
        halves = piece.reshape(owners, 2, 8, part)
        for i in range(2):
            pieces[:, j, :, i * part : (i + 1) * part] = halves[:, i].astype(BF16)
    pre_sum[...] = total
    put_mom.wait()
    put_sec.wait()


def mid(at, arrived, left_parts, root_right, moment, second):
    owners, reps, row_part, part = arrived.shape
    _, rows, size = moment.shape
    half = row_part // 2
    state = shape(moment.shape, F32)
    return pl.pallas_call(
        mid_kernel,
        in_specs=[SMEM] + [ANY] * 8,
        out_specs=(ANY,) * 2 + (VMEM,) * 3,
        scratch_shapes=[
            pltpu.VMEM((owners, row_part, size), BF16),
            pltpu.VMEM((owners, half, size), BF16),
            pltpu.VMEM((size, size), BF16),
            pltpu.VMEM((owners * half, size), BF16),
            pltpu.VMEM((rows, size), F32),
            pltpu.VMEM((rows, size), F32),
            pltpu.SemaphoreType.DMA((2 * REPS + 3,)),
            pltpu.SemaphoreType.DMA((2,)),
        ],
        out_shape=(state,) * 2
        + (
            shape((owners, reps, half // 2, 2 * part + LANES), BF16),
            shape((8, part), F32),
            shape((8, size), F32),
        ),
        compiler_params=params(MID_LIMIT),
        cost_estimate=MID_COST,
        name="own_slot",
    )(at, arrived, *left_parts, root_right, moment, second)


def late_kernel(
    at_ref, grad_ref, mom_ref, sec_ref, own_ref, pre_ref, _, __, ___, mom_out, sec_out, pieces, mom, sec, pads, sems, out_sems
):
    k = 1 - at_ref[1]
    count, reps, row_part, part = grad_ref.shape
    rows = count * row_part
    steps = mom.shape[0]
    chunk = count // steps
    size = reps * part

    def block(ref, n):
        return ref.at[k, pl.ds(n * chunk * row_part, chunk * row_part)]

    loads = []
    for n in range(steps):
        for i, (src, dst) in enumerate(((mom_ref, mom), (sec_ref, sec))):
            copy = pltpu.make_async_copy(block(src, n), dst.at[n], sems.at[2 * n + i])
            copy.start()
            loads.append(copy)
    stores = []
    total = jnp.zeros((8, part), F32)
    for n in range(steps):
        loads[2 * n].wait()
        loads[2 * n + 1].wait()
        for j in range(reps):
            cols = slice(j * part, (j + 1) * part)
            grad = grad_ref[n * chunk : (n + 1) * chunk, j].reshape(chunk * row_part, part).astype(F32)
            first = 0.9 * mom[n, :, cols] + 0.1 * grad
            second = 0.95 * sec[n, :, cols] + 0.05 * grad * grad
            mom[n, :, cols] = first
            sec[n, :, cols] = second
            way = first / (jnp.sqrt(second) + 1e-08)
            total += jnp.sum((way * way).reshape(-1, 8, part), axis=0)
        for i, (src, dst) in enumerate(((mom, mom_out), (sec, sec_out))):
            copy = pltpu.make_async_copy(src.at[n], block(dst, n), out_sems.at[2 * n + i])
            copy.start()
            stores.append(copy)
    own, other = jnp.sum(own_ref[...]), jnp.sum(total)
    even = at_ref[1] == 0
    values = (jnp.where(even, own, other), jnp.where(even, other, own), jnp.sum(pre_ref[...]))
    tile = pads.shape[2:]
    row = lax.broadcasted_iota(jnp.int32, tile, 0)
    pad = jnp.zeros(tile, F32)
    for i, value in enumerate(values):
        rest = jnp.full(tile, value, F32)
        for n in range(3):
            high = rest.astype(BF16).astype(F32)
            pad = jnp.where(row == 3 * i + n, high, pad)
            rest = rest - high
    pads[...] = jnp.broadcast_to(pad.astype(BF16), pads.shape)
    copy = pltpu.make_async_copy(pads, pieces.at[:, :, :, pl.ds(2 * part, LANES)], out_sems.at[2 * steps])
    copy.start()
    for store in stores + [copy]:
        store.wait()


def late(at, grad, moment, second, own_sq, pre_sq, moment_new, second_new, pieces, steps=4):
    _, rows, size = moment.shape
    state = shape(moment.shape, F32)
    return pl.pallas_call(
        late_kernel,
        in_specs=[SMEM, VMEM, ANY, ANY, VMEM, VMEM, ANY, ANY, ANY],
        out_specs=(ANY,) * 3,
        scratch_shapes=[
            pltpu.VMEM((steps, rows // steps, size), F32),
            pltpu.VMEM((steps, rows // steps, size), F32),
            pltpu.VMEM(pieces.shape[:3] + (LANES,), BF16),
            pltpu.SemaphoreType.DMA((2 * steps,)),
            pltpu.SemaphoreType.DMA((2 * steps + 1,)),
        ],
        out_shape=(state, state, shape(pieces.shape, BF16)),
        input_output_aliases={6: 0, 7: 1, 8: 2},
        compiler_params=params(LATE_LIMIT),
        cost_estimate=cost(15 * rows * size, 20 * rows * size),
        name="other_adam",
    )(at, grad, moment, second, own_sq, pre_sq, moment_new, second_new, pieces)


def add_kernel(at_ref, left_part, right_part, left_ref, right_ref, _, __, left_out, right_out):
    left_out[0] = 0.95 * left_ref[0] + left_part[...].astype(F32)
    right_out[0] = 0.95 * right_ref[0] + right_part[...].astype(F32)


def add(at, left_part, right_part, gram_left, gram_right, left_new, right_new, steps=4):
    _, rows, size = gram_left.shape
    state = pl.BlockSpec((1, rows // steps, size), lambda n, at: (1 - at[1], n, 0))
    term = pl.BlockSpec((rows // steps, size), lambda n, at: (n, 0))
    return pl.pallas_call(
        add_kernel,
        grid_spec=pltpu.PrefetchScalarGridSpec(
            num_scalar_prefetch=1,
            grid=(steps,),
            in_specs=[term, term, state, state, ANY, ANY],
            out_specs=(state, state),
        ),
        out_shape=(shape(gram_left.shape, F32), shape(gram_right.shape, F32)),
        input_output_aliases={5: 0, 6: 1},
        compiler_params=params(),
        cost_estimate=cost(4 * rows * size, 20 * rows * size),
        name="add_terms",
    )(at, left_part, right_part, gram_left, gram_right, left_new, right_new)


def finish_kernel(cells, slot_ref, in_ref, out_ref, ratios):
    rows = in_ref.shape[1]
    part = (in_ref.shape[2] - LANES) // 2
    sums = in_ref[:, :, 2 * part :].astype(F32).reshape(-1, REPS, rows, LANES)
    adam_sums = jnp.sum(sums, axis=1)
    for k in range(2):
        adam_all = jnp.sum(adam_sums[:, 3 * k : 3 * k + 3], axis=1, keepdims=True)
        pre_all = jnp.sum((sums[:, k] + sums[:, k + 2])[:, 6:8], axis=1, keepdims=True)
        value = jnp.sqrt(adam_all / cells + 1e-06) / jnp.sqrt(pre_all / cells + 1e-06)
        ratios[:, k] = jnp.broadcast_to(value, (value.shape[0], rows, LANES))

    def place_block(b, _):
        slot = slot_ref[b]
        owner, k = slot // 2, lax.rem(slot, 2)
        by = ratios[owner, k]
        by = jnp.concatenate([by] * (2 * part // LANES), axis=1)
        for n in range(2):
            piece = in_ref[owner * REPS + k + 2 * n, :, : 2 * part].astype(F32) * by
            piece = jnp.concatenate([piece[:, :part], piece[:, part:]], axis=0)
            out_ref[b, 2 * n * rows : 2 * (n + 1) * rows, :] = piece.astype(BF16)
        return 0

    lax.fori_loop(0, out_ref.shape[0], place_block, 0, unroll=8)


def finish(owner_slot, pieces, size):
    count, rows, wide = pieces.shape
    blocks = owner_slot.shape[0]
    part = (wide - LANES) // 2
    return pl.pallas_call(
        functools.partial(finish_kernel, float(size * size)),
        out_shape=shape((blocks, 4 * rows, part), BF16),
        in_specs=[SMEM, VMEM],
        out_specs=VMEM,
        scratch_shapes=[pltpu.VMEM((blocks // 2, 2, rows, LANES), F32)],
        compiler_params=params(),
        cost_estimate=cost(8 * blocks * rows * part, 20 * blocks * rows * part),
        name="finish_updates",
    )(owner_slot, pieces)


def per_device(grads, owner_slot, gram_left, gram_right, root_left, root_right, moment, second):
    blocks, row_part, part = grads.shape
    _, rows, size = root_left.shape
    at = place()
    sent, keep, ahead, across, back = deal(at, owner_slot, grads, root_left)
    arrived = everyone(sent).reshape(OWNERS, REPS, row_part, part)
    ahead = to_neighbour(ahead)
    across = to_neighbour(across, 2)
    back = to_neighbour(back, -1)

    count = rows // row_part
    other = to_neighbour(lax.dynamic_slice_in_dim(arrived, at[2] * count, count, 0))
    left_new, right_new, left_term, right_term = grams(at, arrived, gram_left, gram_right)
    arrived, left_term, right_term = lax.optimization_barrier((arrived, left_term, right_term))
    right_term = to_neighbour(right_term)
    left_term = to_neighbour(left_term)
    moment_new, second_new, pieces, pre_sq, own_sq = mid(
        at, arrived, (keep, ahead, across, back), root_right, moment, second
    )
    moment_new, second_new, pieces = late(
        at, other, moment, second, own_sq, pre_sq, moment_new, second_new, pieces
    )
    pieces, right_term = lax.optimization_barrier((pieces, right_term))
    homed = everyone(pieces.reshape((-1,) + pieces.shape[2:]))
    left_new, right_new = add(at, left_term, right_term, gram_left, gram_right, left_new, right_new)
    updates = finish(owner_slot, homed, size)
    return (updates, left_new, right_new, moment_new, second_new)


def solution(mesh):
    return jax.shard_map(
        per_device,
        mesh=mesh,
        in_specs=(
            P(None, "fsdp", "rep"),
            P(),
            P("fsdp", "rep", None),
            P("fsdp", "rep", None),
            P("fsdp", "rep", None),
            P("fsdp", None, None),
            P("fsdp", "rep", None),
            P("fsdp", "rep", None),
        ),
        out_specs=(
            P(None, "fsdp", "rep"),
            P("fsdp", "rep", None),
            P("fsdp", "rep", None),
            P("fsdp", "rep", None),
            P("fsdp", "rep", None),
        ),
        check_vma=False,
    )
```

time: 164 us -> 106 us (0.65)
  Pallas kernels: 0 us -> 27.3 us
  waiting for transfers between devices: 72.8 us -> 46.2 us
  local copies, waits for them, and re-layouts: 31.1 us -> 6.14 us
  matrix products: 19.8 us -> 0 us
  other arithmetic: 7.97 us -> 0.6 us
  blocking collectives: 6.36 us -> 0 us
    all_to_all x3 -> x2, waiting for transfers between devices: 72.8 us -> 27.3 us  [everyone(): lax.all_to_all(x, ('fsdp', 'rep'), split_axis=0, concat_axis=0, tiled=True)]
    pallas_call x0 -> x6, Pallas kernels: none -> 27.3 us  [the longest x1 7.58 us: mid(): pl.pallas_call(mid_kernel, in_specs=[SMEM] + [ANY] * 8, out_specs=(ANY,)...]
    dot_general x3 -> x0, matrix products: 19.8 us -> none  [the longest x1 11 us: per_device(): jnp.einsum('nik,nkj->nij', root_left, product, preferred_element_type=jnp...]
    ppermute x0 -> x6, waiting for transfers between devices: none -> 18.9 us  [to_neighbour(): return lax.ppermute(x, ('fsdp', 'rep'), pairs)]
    transpose x1 -> x0, local copies, waits for them, and re-layouts: 12.5 us -> none  [per_device(): jnp.transpose(arrived, (0, 1, 3, 2, 4))]
    reshape x1 -> x0, local copies, waits for them, and re-layouts: 7.71 us -> none  [per_device(): jnp.transpose(arrived, (0, 1, 3, 2, 4))]
    ppermute x0 -> x6, starting transfers between devices: none -> 6.69 us  [to_neighbour(): return lax.ppermute(x, ('fsdp', 'rep'), pairs)]
    all_to_all x3 -> x2, starting transfers between devices: 24.1 us -> 17.5 us  [everyone(): lax.all_to_all(x, ('fsdp', 'rep'), split_axis=0, concat_axis=0, tiled=True)]
  transfers between devices with their start and end apart: 3 -> 8, of which waited for: 3 -> 2; matrix products, arithmetic and copies ran while one was open for 5% -> 0% of each run, Pallas kernels for 0% -> 20%
where the time goes in v3:
time: 106 us; the launch traced here: 105 us
  waiting for transfers between devices  46.2 us (44%)
  Pallas kernels  27.3 us (26%)
  starting transfers between devices  24.2 us (23%)
  local copies, waits for them, and re-layouts  6.14 us (6%)
    all_to_all x2, waiting for transfers between devices, everyone(): lax.all_to_all(x, ('fsdp', 'rep'), split_axis=0, concat_axis=0, tiled=True)  27.3 us
    ppermute x6, waiting for transfers between devices, to_neighbour(): return lax.ppermute(x, ('fsdp', 'rep'), pairs)  18.9 us
    all_to_all x2, starting transfers between devices, everyone(): lax.all_to_all(x, ('fsdp', 'rep'), split_axis=0, concat_axis=0, tiled=True)  17.5 us
    pallas_call x1, Pallas kernels, mid(): pl.pallas_call(mid_kernel, in_specs=[SMEM] + [ANY] * 8, out_specs=(ANY,)...  7.58 us
    pallas_call x1, Pallas kernels, grams(): pl.pallas_call(gram_kernel, in_specs=[SMEM] + [ANY] * 3, out_specs=(ANY,)...  7.3 us
    ppermute x6, starting transfers between devices, to_neighbour(): return lax.ppermute(x, ('fsdp', 'rep'), pairs)  6.69 us
    unnamed x18, local copies, waits for them, and re-layouts  6.1 us
    pallas_call x1, Pallas kernels, late(): pl.pallas_call(late_kernel, in_specs=[SMEM, VMEM, ANY, ANY, VMEM, VMEM, A...  3.86 us
  transfers between devices with their start and end apart: 8, of which 2 were waited for; matrix products, arithmetic and copies ran while one was open for 0% of the time, Pallas kernels for 20%

profile of v3, /device:TPU:1, one launch (start us, length us, event | category | flops | bytes accessed | tf_op | source)
XLA Modules:
  0.0 105.2 jit_solution(7429777387654114454)
XLA Ops:
  0.6 0.6 pad_add_fusion.at_ref
  1.2 3.8 %deal_blocks.1 = (bf16[128,32,256]{2,1,0:T(8,128)(2,1)}, bf16[8,16,1024]{2,1,0:T(8,128)(2,1)}, bf16[8,16,1024]{2,1,0:T(8,128)(2,1)}, bf16[8,16,1024]{2,1,0:T(8,128)(2,1)}, bf16[8,16,1024]{2,1,0:T(8,128)(2,1)}) custom-call(s32[4]{0:T(128)} %pad_add_fusion.at_ref, s32[64]{0:T(128)} %slot_ref.3, bf16[64,32,256]{2,1,0:T(8,128)(2,1)} %grads_ref.1, ...), custom_call_target="tpu_custom_call" | custom-call | bytes 5242880 | tf_op jit(solution)/shard_map/deal_blocks/pallas_call | solution.py:91
  5.0 11.5 %all-to-all-start = ((bf16[128,32,256]{2,1,0:T(8,128)(2,1)}), bf16[128,32,256]{2,1,0:T(8,128)(2,1)S(1)}, u32[]{:S(2)}, u32[]{:S(2)}) async-start(bf16[128,32,256]{2,1,0:T(8,128)(2,1)} %get-tuple-element.29), calls=%async_computation | async-start | bytes 4194304 | tf_op jit(solution)/shard_map/all_to_all | solution.py:63
  16.5 2.7 %collective-permute-start.1 = (bf16[8,16,1024]{2,1,0:T(8,128)(2,1)}, bf16[8,16,1024]{2,1,0:T(8,128)(2,1)S(1)}, u32[]{:S(2)}, u32[]{:S(2)}) collective-permute-start(bf16[8,16,1024]{2,1,0:T(8,128)(2,1)} %get-tuple-element.34), channel_id=1, source_target_pairs={{0,1},{1,2},{2,3},{3,0},{4,7},{5,4},{6,5},{7,6},{8,9},{9,10},{10,1... | collective-permute-start | bytes 786440 | tf_op jit(solution)/shard_map/ppermute | solution.py:59
  19.2 0.5 collective-permute-start.2
  19.8 0.6 collective-permute-start.3
  20.3 27.3 %all-to-all-done = bf16[128,32,256]{2,1,0:T(8,128)(2,1)S(1)} async-done(((bf16[128,32,256]{2,1,0:T(8,128)(2,1)}), bf16[128,32,256]{2,1,0:T(8,128)(2,1)S(1)}, u32[]{:S(2)}, u32[]{:S(2)}) %all-to-all-start) | async-done | bytes 2097184 | tf_op jit(solution)/shard_map/all_to_all | solution.py:63
  47.7 0.1 collective-permute-start
  47.7 1.2 %copy-done.6 = bf16[128,32,256]{2,1,0:T(8,128)(2,1)} copy-done((bf16[128,32,256]{2,1,0:T(8,128)(2,1)}, bf16[128,32,256]{2,1,0:T(8,128)(2,1)S(1)}, u32[]{:S(2)}) %copy-start.6) | copy-done | bytes 2097176
  48.9 7.3 %own_grams.1 = (f32[2,256,1024]{2,1,0:T(8,128)}, f32[2,256,1024]{2,1,0:T(8,128)}, bf16[256,1024]{1,0:T(8,128)(2,1)}, bf16[256,1024]{1,0:T(8,128)(2,1)}) custom-call(s32[4]{0:T(128)} %pad_add_fusion.at_ref, bf16[32,4,32,256]{3,2,1,0:T(8,128)(2,1)} %bitcast.8, f32[2,256,1024]{2,1,0:T(8,128)} %left_ref.1, f32[2,256,1024]{2,1,0:T(8,128)} %right_ref.3), custom_call_target="tpu_custom_call" | custom-call | flops 1 | bytes 1 | tf_op jit(solution)/shard_map/own_grams/pallas_call | solution.py:157
  56.2 0.1 collective-permute-start.4
  56.3 0.0 collective-permute-done.1.l1_ref
  56.3 0.0 collective-permute-done.2.l2_ref
  56.4 0.0 collective-permute-done.3.l3_ref
  56.4 0.7 copy-done.8
  57.0 7.6 %own_slot.1 = (f32[2,256,1024]{2,1,0:T(8,128)}, f32[2,256,1024]{2,1,0:T(8,128)}, bf16[32,4,8,640]{3,2,1,0:T(8,128)(2,1)}, f32[8,256]{1,0:T(8,128)}, f32[8,1024]{1,0:T(8,128)}) custom-call(s32[4]{0:T(128)} %pad_add_fusion.at_ref, bf16[32,4,32,256]{3,2,1,0:T(8,128)(2,1)} %bitcast.9, bf16[8,16,1024]{2,1,0:T(8,128)(2,1)} %get-tuple-element.33.l0_ref, ...), custom_call_target="tpu_custom_call" | custom-call | flops 99999997952 | bytes 1000000 | tf_op jit(solution)/shard_map/own_slot/pallas_call | solution.py:248
  64.6 0.0 collective-permute-done.grad_ref
  64.6 0.0 copy-start.7
  64.7 0.8 copy-done.7
  65.4 3.9 %other_adam.1 = (f32[2,256,1024]{2,1,0:T(8,128)}, f32[2,256,1024]{2,1,0:T(8,128)}, bf16[32,4,8,640]{3,2,1,0:T(8,128)(2,1)}) custom-call(s32[4]{0:T(128)} %pad_add_fusion.at_ref, bf16[8,4,32,256]{3,2,1,0:T(8,128)(2,1)} %copy-done.7, f32[2,256,1024]{2,1,0:T(8,128)} %mom_ref.3, ...), custom_call_target="tpu_custom_call", output_to_operand_aliasing={{0}: (6, {}), {1}: (7, {}), {2}: (8, {})} | custom-call | flops 3932160 | bytes 5242880 | tf_op jit(solution)/shard_map/other_adam/pallas_call | solution.py:333
  69.3 0.0 copy-start
  69.3 0.0 collective-permute-done.4.right_part
  69.3 0.0 copy-start.2
  69.4 0.8 copy-done.2
  70.1 6.0 %all-to-all-start.1 = ((bf16[128,8,640]{2,1,0:T(8,128)(2,1)}), bf16[128,8,640]{2,1,0:T(8,128)(2,1)S(1)}, u32[]{:S(2)}, u32[]{:S(2)}) async-start(bf16[128,8,640]{2,1,0:T(8,128)(2,1)} %bitcast.10), calls=%async_computation.1 | async-start | bytes 2621440 | tf_op jit(solution)/shard_map/all_to_all | solution.py:63
  76.2 2.7 %collective-permute-start.5 = (bf16[256,1024]{1,0:T(8,128)(2,1)}, bf16[256,1024]{1,0:T(8,128)(2,1)S(1)}, u32[]{:S(2)}, u32[]{:S(2)}) collective-permute-start(bf16[256,1024]{1,0:T(8,128)(2,1)} %get-tuple-element.45), channel_id=1, source_target_pairs={{0,1},{1,2},{2,3},{3,0},{4,7},{5,4},{6,5},{7,6},{8,9},{9,10},{10,1... | collective-permute-start | bytes 1572872 | tf_op jit(solution)/shard_map/ppermute | solution.py:59
  78.9 18.9 %collective-permute-done.5.left_part = bf16[256,1024]{1,0:T(8,128)(2,1)S(1)} collective-permute-done((bf16[256,1024]{1,0:T(8,128)(2,1)}, bf16[256,1024]{1,0:T(8,128)(2,1)S(1)}, u32[]{:S(2)}, u32[]{:S(2)}) %collective-permute-start.5) | collective-permute-done | bytes 524320 | tf_op jit(solution)/shard_map/ppermute | solution.py:59
  97.8 1.6 %copy-done.1 = f32[2,256,1024]{2,1,0:T(8,128)S(1)} copy-done((f32[2,256,1024]{2,1,0:T(8,128)S(1)}, f32[2,256,1024]{2,1,0:T(8,128)}, u32[]{:S(2)}) %copy-start.1) | copy-done | bytes 2097176
  99.4 1.0 copy-done.3
  100.5 2.4 %add_terms.1 = (f32[2,256,1024]{2,1,0:T(8,128)}, f32[2,256,1024]{2,1,0:T(8,128)}) custom-call(s32[4]{0:T(128)S(1)} %copy-done.4, bf16[256,1024]{1,0:T(8,128)(2,1)S(1)} %collective-permute-done.5.left_part, bf16[256,1024]{1,0:T(8,128)(2,1)S(1)} %copy-done.3, f32[2,256,1024]{2,1,0:T(8,128)S(1)} %copy-done, ...), custom_call_target="tpu_custom_call", output_to_operand_aliasing={{0}: (5, {}), {1}: (6, {})} | custom-call | flops 1048576 | bytes 5242880 | tf_op jit(solution)/shard_map/add_terms/pallas_call | solution.py:361
  102.9 0.0 all-to-all-done.1.in_ref
  102.9 2.4 %finish_updates.1 = bf16[64,32,256]{2,1,0:T(8,128)(2,1)} custom-call(s32[64]{0:T(128)S(1)} %copy-done.5, bf16[128,8,640]{2,1,0:T(8,128)(2,1)S(1)} %all-to-all-done.1.in_ref), custom_call_target="tpu_custom_call" | custom-call | flops 1048576 | bytes 2621440 | tf_op jit(solution)/shard_map/finish_updates/pallas_call | solution.py:406
  (10 shorter events, 0.1 us)
Async XLA Ops:
  5.0 42.6 %all-to-all-start = ((bf16[128,32,256]{2,1,0:T(8,128)(2,1)}), bf16[128,32,256]{2,1,0:T(8,128)(2,1)S(1)}, u32[]{:S(2)}, u32[]{:S(2)}) async-start(bf16[128,32,256]{2,1,0:T(8,128)(2,1)} %get-tuple-element.29), calls=%async_computation | async-start | bytes 4194304 | tf_op jit(solution)/shard_map/all_to_all | solution.py:63
  16.5 39.8 %collective-permute-start.1 = (bf16[8,16,1024]{2,1,0:T(8,128)(2,1)}, bf16[8,16,1024]{2,1,0:T(8,128)(2,1)S(1)}, u32[]{:S(2)}, u32[]{:S(2)}) collective-permute-start(bf16[8,16,1024]{2,1,0:T(8,128)(2,1)} %get-tuple-element.34), channel_id=1, source_target_pairs={{0,1},{1,2},{2,3},{3,0},{4,7},{5,4},{6,5},{7,6},{8,9},{9,10},{10,1... | collective-permute-start | bytes 786440 | tf_op jit(solution)/shard_map/ppermute | solution.py:59
  19.2 37.1 %collective-permute-start.2 = (bf16[8,16,1024]{2,1,0:T(8,128)(2,1)}, bf16[8,16,1024]{2,1,0:T(8,128)(2,1)}, u32[]{:S(2)}, u32[]{:S(2)}) collective-permute-start(bf16[8,16,1024]{2,1,0:T(8,128)(2,1)} %get-tuple-element.35), channel_id=1, source_target_pairs={{0,2},{1,3},{2,0},{3,1},{4,6},{5,7},{6,4},{7,5},{8,10},{9,11},{10,... | collective-permute-start | bytes 786440 | tf_op jit(solution)/shard_map/ppermute | solution.py:59
  19.8 36.6 %collective-permute-start.3 = (bf16[8,16,1024]{2,1,0:T(8,128)(2,1)}, bf16[8,16,1024]{2,1,0:T(8,128)(2,1)}, u32[]{:S(2)}, u32[]{:S(2)}) collective-permute-start(bf16[8,16,1024]{2,1,0:T(8,128)(2,1)} %get-tuple-element.36), channel_id=1, source_target_pairs={{0,3},{1,0},{2,1},{3,2},{4,5},{5,6},{6,7},{7,4},{8,11},{9,8},{10,9... | collective-permute-start | bytes 786440 | tf_op jit(solution)/shard_map/ppermute | solution.py:59
  47.6 1.3 %copy-start.6 = (bf16[128,32,256]{2,1,0:T(8,128)(2,1)}, bf16[128,32,256]{2,1,0:T(8,128)(2,1)S(1)}, u32[]{:S(2)}) copy-start(bf16[128,32,256]{2,1,0:T(8,128)(2,1)S(1)} %all-to-all-done) | copy-start | bytes 6291460
  47.7 17.0 %collective-permute-start = (bf16[8,4,32,256]{3,2,1,0:T(8,128)(2,1)S(1)}, bf16[8,4,32,256]{3,2,1,0:T(8,128)(2,1)S(1)}, u32[]{:S(2)}, u32[]{:S(2)}) collective-permute-start(bf16[8,4,32,256]{3,2,1,0:T(8,128)(2,1)S(1)} %constant_dynamic-slice_fusion), channel_id=1, source_target_pairs={{0,1},{1,2},{2,3},{3,0},{4,7},{5,4},{6,5},{7,6},{8,9},{9,10},{10,1... | collective-permute-start | bytes 1572872 | tf_op jit(solution)/shard_map/ppermute | solution.py:59
  56.2 13.1 %collective-permute-start.4 = (bf16[256,1024]{1,0:T(8,128)(2,1)}, bf16[256,1024]{1,0:T(8,128)(2,1)S(1)}, u32[]{:S(2)}, u32[]{:S(2)}) collective-permute-start(bf16[256,1024]{1,0:T(8,128)(2,1)} %get-tuple-element.43), channel_id=1, source_target_pairs={{0,1},{1,2},{2,3},{3,0},{4,7},{5,4},{6,5},{7,6},{8,9},{9,10},{10,1... | collective-permute-start | bytes 1572872 | tf_op jit(solution)/shard_map/ppermute | solution.py:59
  56.3 0.7 copy-start.8
  64.6 0.8 copy-start.7
  69.3 28.5 %copy-start = (f32[2,256,1024]{2,1,0:T(8,128)S(1)}, f32[2,256,1024]{2,1,0:T(8,128)}, u32[]{:S(2)}) copy-start(f32[2,256,1024]{2,1,0:T(8,128)} %left_ref.1) | copy-start | bytes 6291460
  69.3 28.5 %copy-start.4 = (s32[4]{0:T(128)S(1)}, s32[4]{0:T(128)}, u32[]{:S(2)}) copy-start(s32[4]{0:T(128)} %pad_add_fusion.at_ref) | copy-start | bytes 52
  69.3 0.8 copy-start.2
  70.1 32.7 %all-to-all-start.1 = ((bf16[128,8,640]{2,1,0:T(8,128)(2,1)}), bf16[128,8,640]{2,1,0:T(8,128)(2,1)S(1)}, u32[]{:S(2)}, u32[]{:S(2)}) async-start(bf16[128,8,640]{2,1,0:T(8,128)(2,1)} %bitcast.10), calls=%async_computation.1 | async-start | bytes 2621440 | tf_op jit(solution)/shard_map/all_to_all | solution.py:63
  76.2 21.6 %collective-permute-start.5 = (bf16[256,1024]{1,0:T(8,128)(2,1)}, bf16[256,1024]{1,0:T(8,128)(2,1)S(1)}, u32[]{:S(2)}, u32[]{:S(2)}) collective-permute-start(bf16[256,1024]{1,0:T(8,128)(2,1)} %get-tuple-element.45), channel_id=1, source_target_pairs={{0,1},{1,2},{2,3},{3,0},{4,7},{5,4},{6,5},{7,6},{8,9},{9,10},{10,1... | collective-permute-start | bytes 1572872 | tf_op jit(solution)/shard_map/ppermute | solution.py:59
  97.8 1.6 %copy-start.1 = (f32[2,256,1024]{2,1,0:T(8,128)S(1)}, f32[2,256,1024]{2,1,0:T(8,128)}, u32[]{:S(2)}) copy-start(f32[2,256,1024]{2,1,0:T(8,128)} %right_ref.3) | copy-start | bytes 6291460
  99.4 1.0 copy-start.3
  100.5 2.4 %copy-start.5 = (s32[64]{0:T(128)S(1)}, s32[64]{0:T(128)}, u32[]{:S(2)}) copy-start(s32[64]{0:T(128)} %slot_ref.3) | copy-start | bytes 772

commit v4 on v3

v4 whole, which is shorter than its diff:
```python
import functools

import jax
import jax.numpy as jnp
from jax import lax
from jax.experimental import pallas as pl
from jax.experimental.pallas import tpu as pltpu
from jax.sharding import PartitionSpec as P

VMEM_LIMIT = 32 * 1024 * 1024
MID_LIMIT = 60 * 1024 * 1024
BIG_LIMIT = 60 * 1024 * 1024
DEALS = 4
LATE_LIMIT = 60 * 1024 * 1024
REPS = 4
OWNERS = 32
LANES = 128
NN = (((1,), (0,)), ((), ()))
NT = (((1,), (1,)), ((), ()))
TN = (((0,), (0,)), ((), ()))
ANY = pl.BlockSpec(memory_space=pl.ANY)
VMEM = pl.BlockSpec(memory_space=pltpu.VMEM)
SMEM = pl.BlockSpec(memory_space=pltpu.SMEM)
BF16 = jnp.bfloat16
F32 = jnp.float32


def params(limit=VMEM_LIMIT):
    return pltpu.CompilerParams(vmem_limit_bytes=limit)


def cost(flops, nbytes):
    return pl.CostEstimate(flops=flops, bytes_accessed=nbytes, transcendentals=0)


def dot(a, b, dims=NN):
    return lax.dot_general(a, b, dims, preferred_element_type=F32)


def shape(dims, dtype):
    return jax.ShapeDtypeStruct(dims, dtype)


GRAM_COST = cost(1, 1)
MID_COST = cost(10**11, 10**6)


def place():
    rep = lax.axis_index("rep").astype(jnp.int32)
    core = lax.rem(lax.axis_index("fsdp").astype(jnp.int32), 2)
    step = 1 - 2 * core
    return jnp.stack([rep, lax.rem(rep, 2), lax.rem(rep + step + REPS, REPS), step])


def to_neighbour(x, far=1):
    pairs = []
    for owner in range(OWNERS):
        step = far * (1 - 2 * (owner % 2))
        for rep in range(REPS):
            pairs.append((owner * REPS + rep, owner * REPS + (rep + step) % REPS))
    return lax.ppermute(x, ("fsdp", "rep"), pairs)


def everyone(x):
    return lax.all_to_all(x, ("fsdp", "rep"), split_axis=0, concat_axis=0, tiled=True)


def load(src, dst, sem):
    copy = pltpu.make_async_copy(src, dst, sem)
    copy.start()
    return copy


def load_columns(arrived, whole, sems):
    part = arrived.shape[3]
    return [
        load(arrived.at[:, j], whole.at[:, :, pl.ds(j * part, part)], sems.at[j]) for j in range(arrived.shape[1])
    ]


def deal_kernel(slot_ref, grads_ref, out_ref, grads, out, block_of, sems):
    blocks = grads.shape[0]
    chunk = blocks // DEALS
    gets, puts = [], []
    for n in range(DEALS):
        part_of = pl.ds(n * chunk, chunk)
        gets.append(load(grads_ref.at[part_of], grads.at[part_of], sems.at[n]))

    def note(b, _):
        block_of[slot_ref[b]] = b
        return 0

    lax.fori_loop(0, blocks, note, 0, unroll=8)
    for copy in gets:
        copy.wait()

    def place_owner(owner, _):
        for k in range(2):
            block = grads[block_of[2 * owner + k]]
            out[owner * REPS + k] = block
            out[owner * REPS + k + 2] = block
        return 0

    step = blocks // 2 // DEALS
    for n in range(DEALS):
        lax.fori_loop(n * step, (n + 1) * step, place_owner, 0, unroll=4)
        part_of = pl.ds(n * step * REPS, step * REPS)
        puts.append(load(out.at[part_of], out_ref.at[part_of], sems.at[DEALS + n]))
    for copy in puts:
        copy.wait()


def deal(owner_slot, grads):
    blocks, row_part, part = grads.shape
    return pl.pallas_call(
        deal_kernel,
        out_shape=shape((2 * blocks, row_part, part), BF16),
        in_specs=[SMEM, ANY],
        out_specs=ANY,
        scratch_shapes=[
            pltpu.VMEM(grads.shape, BF16),
            pltpu.VMEM((2 * blocks, row_part, part), BF16),
            pltpu.SMEM((blocks,), jnp.int32),
            pltpu.SemaphoreType.DMA((2 * DEALS,)),
        ],
        compiler_params=params(BIG_LIMIT),
        cost_estimate=cost(0, 6 * grads.size),
        name="deal_blocks",
    )(owner_slot, grads)


def share_kernel(at_ref, left_ref, keep_ref, ahead_ref, across_ref, back_ref, left, sems):
    get = load(left_ref, left, sems.at[0])
    get.wait()
    puts = []
    for j, ref in ((1, ahead_ref), (2, across_ref), (-1, back_ref), (0, keep_ref)):
        to = lax.rem(at_ref[0] + j * at_ref[3] + REPS, REPS)
        puts.append(load(left.at[lax.rem(to, 2), :, to // 2], ref, sems.at[1 + len(puts)]))
    for copy in puts:
        copy.wait()


def share_rows(at, root_left, row_part):
    _, rows, size = root_left.shape
    count, half = rows // row_part, row_part // 2
    return pl.pallas_call(
        share_kernel,
        out_shape=(shape((count, half, size), BF16),) * REPS,
        in_specs=[SMEM, ANY],
        out_specs=(ANY,) * REPS,
        scratch_shapes=[pltpu.VMEM((2, count, 2, half, size), BF16), pltpu.SemaphoreType.DMA((1 + REPS,))],
        compiler_params=params(BIG_LIMIT),
        cost_estimate=cost(0, 4 * root_left.size),
        name="share_rows",
    )(at, root_left.reshape(2, count, 2, half, size))


def gram_kernel(
    at_ref, arrived, stat_left, stat_right, left_out, right_out, left_term, right_term,
    whole, lhs, gl, gr, lt, rt, sems, out_sems,
):
    rep, k, near = at_ref[0], at_ref[1], at_ref[2]
    _, row_part, size = whole.shape
    part = size // REPS
    rows = gl.shape[0]
    columns = load_columns(arrived, whole, sems)
    get_gr = load(stat_right.at[k], gr, sems.at[REPS])
    get_gl = load(stat_left.at[k], gl, sems.at[REPS + 1])
    for copy in columns:
        copy.wait()
    puts = []

    def emit(j, term, stat, terms, new_ref, term_ref):
        cols = pl.ds(j * part, part)
        stat[:, cols] = 0.95 * stat[:, cols] + term[:rows]
        terms[:, cols] = term[rows:].astype(BF16)
        for src, dst in ((stat, new_ref.at[k]), (terms, term_ref)):
            puts.append(load(src.at[:, cols], dst.at[:, cols], out_sems.at[len(puts)]))

    for i, index in enumerate((rep, near)):
        cols = whole[:, :, pl.ds(pl.multiple_of(index * part, part), part)].reshape(size, part)
        lhs[i * rows : (i + 1) * rows, :] = cols.T
    get_gr.wait()
    for j in range(REPS):
        grad = whole[:, :, j * part : (j + 1) * part].reshape(size, part)
        emit(j, 0.05 * dot(lhs[...], grad), gr, rt, right_out, right_term)
    for i, index in enumerate((rep, near)):
        from_row = pl.ds(index * (rows // row_part), rows // row_part)
        lhs[i * rows : (i + 1) * rows, :] = whole[from_row].reshape(rows, size)
    get_gl.wait()
    blocks = part // row_part
    for j in range(REPS):
        grad = whole[j * blocks : (j + 1) * blocks].reshape(part, size)
        emit(j, 0.05 * dot(lhs[...], grad, NT), gl, lt, left_out, left_term)
    for copy in puts:
        copy.wait()


def grams(at, arrived, gram_left, gram_right):
    owners, reps, row_part, part = arrived.shape
    _, rows, size = gram_left.shape
    state = shape(gram_left.shape, F32)
    return pl.pallas_call(
        gram_kernel,
        in_specs=[SMEM] + [ANY] * 3,
        out_specs=(ANY,) * 4,
        scratch_shapes=[
            pltpu.VMEM((owners, row_part, size), BF16),
            pltpu.VMEM((2 * rows, size), BF16),
            pltpu.VMEM((rows, size), F32),
            pltpu.VMEM((rows, size), F32),
            pltpu.VMEM((rows, size), BF16),
            pltpu.VMEM((rows, size), BF16),
            pltpu.SemaphoreType.DMA((REPS + 2,)),
            pltpu.SemaphoreType.DMA((4 * REPS,)),
        ],
        out_shape=(state,) * 2 + (shape((rows, size), BF16),) * 2,
        compiler_params=params(MID_LIMIT),
        cost_estimate=GRAM_COST,
        name="own_grams",
    )(at, arrived, gram_left, gram_right)


def mid_kernel(
    at_ref, arrived, l0_ref, l1_ref, l2_ref, l3_ref, right_ref, mom_ref, sec_ref, mom_out, sec_out, pieces, sum_ref,
    whole, left, right, mixed, mom, sec, out, sems, out_sems,
):
    rep, k, step = at_ref[0], at_ref[1], at_ref[3]
    owners, row_part, size = whole.shape
    part = size // REPS
    rows = mom.shape[0]
    share = l0_ref.shape[0]
    get_left = []
    for j, ref in enumerate((l0_ref, l1_ref, l2_ref, l3_ref)):
        first = lax.rem(rep - j * step + REPS * REPS, REPS) * share
        get_left.append(load(ref, left.at[pl.ds(first, share)], sems.at[REPS + 2 + j]))
    columns = load_columns(arrived, whole, sems)
    get_mom = load(mom_ref.at[k], mom, sems.at[REPS])
    get_sec = load(sec_ref.at[k], sec, sems.at[REPS + 1])
    half = size // 2
    get_right = [
        load(right_ref.at[k, :, pl.ds(i * half, half)], right.at[:, pl.ds(i * half, half)], sems.at[2 * REPS + 2 + i])
        for i in range(2)
    ]
    for copy in get_left + columns:
        copy.wait()
    for j in range(REPS):
        grad = whole[:, :, j * part : (j + 1) * part].reshape(size, part)
        mixed[:, j * part : (j + 1) * part] = dot(left[...].reshape(mixed.shape), grad).astype(BF16)

    get_mom.wait()
    get_sec.wait()
    own_total = jnp.zeros((8, part), F32)
    puts = []
    for j in range(REPS):
        cols = pl.ds(j * part, part)
        own = whole[pl.ds(rep * (rows // row_part), rows // row_part), :, cols].reshape(rows, part).astype(F32)
        first = 0.9 * mom[:, cols] + 0.1 * own
        second = 0.95 * sec[:, cols] + 0.05 * own * own
        mom[:, cols] = first
        sec[:, cols] = second
        way = first / (jnp.sqrt(second) + 1e-08)
        own_total += jnp.sum((way * way).reshape(rows // 8, 8, part), axis=0)
        for src, dst in ((mom, mom_out), (sec, sec_out)):
            puts.append(load(src.at[:, cols], dst.at[k, :, cols], out_sems.at[len(puts)]))
    sum_ref[0] = own_total

    for copy in get_right:
        copy.wait()
    total = jnp.zeros((8, part), F32)
    for j in range(REPS):
        piece = dot(mixed[...], right[:, j * part : (j + 1) * part])
        total += jnp.sum((piece * piece).reshape(-1, 8, part), axis=0)
        halves = piece.reshape(owners, 2, 8, part)
        for i in range(2):
            out[:, j, :, i * part : (i + 1) * part] = halves[:, i].astype(BF16)
        puts.append(load(out.at[:, j], pieces.at[:, j, :, pl.ds(0, 2 * part)], out_sems.at[len(puts)]))
    sum_ref[1] = total
    for copy in puts:
        copy.wait()


def mid(at, arrived, left_parts, root_right, moment, second):
    owners, reps, row_part, part = arrived.shape
    _, rows, size = moment.shape
    half = row_part // 2
    state = shape(moment.shape, F32)
    return pl.pallas_call(
        mid_kernel,
        in_specs=[SMEM] + [ANY] * 8,
        out_specs=(ANY,) * 3 + (VMEM,),
        scratch_shapes=[
            pltpu.VMEM((owners, row_part, size), BF16),
            pltpu.VMEM((owners, half, size), BF16),
            pltpu.VMEM((size, size), BF16),
            pltpu.VMEM((owners * half, size), BF16),
            pltpu.VMEM((rows, size), F32),
            pltpu.VMEM((rows, size), F32),
            pltpu.VMEM((owners, reps, half // 2, 2 * part), BF16),
            pltpu.SemaphoreType.DMA((2 * REPS + 4,)),
            pltpu.SemaphoreType.DMA((3 * REPS,)),
        ],
        out_shape=(state,) * 2
        + (shape((owners, reps, half // 2, 2 * part + LANES), BF16), shape((2, 8, part), F32)),
        compiler_params=params(MID_LIMIT),
        cost_estimate=MID_COST,
        name="own_slot",
    )(at, arrived, *left_parts, root_right, moment, second)


def late_kernel(
    at_ref, grad_hbm, mom_ref, sec_ref, sum_ref, _, __, ___, mom_out, sec_out, pieces, grad_ref, mom, sec, pads, sems, out_sems
):
    k = 1 - at_ref[1]
    count, reps, row_part, part = grad_ref.shape
    rows = count * row_part
    steps = mom.shape[0]
    chunk = count // steps
    size = reps * part

    def block(ref, n):
        return ref.at[k, pl.ds(n * chunk * row_part, chunk * row_part)]

    get_grad = load(grad_hbm, grad_ref, sems.at[2 * steps])
    loads = []
    for n in range(steps):
        for i, (src, dst) in enumerate(((mom_ref, mom), (sec_ref, sec))):
            copy = pltpu.make_async_copy(block(src, n), dst.at[n], sems.at[2 * n + i])
            copy.start()
            loads.append(copy)
    stores = []
    total = jnp.zeros((8, part), F32)
    get_grad.wait()
    for n in range(steps):
        loads[2 * n].wait()
        loads[2 * n + 1].wait()
        for j in range(reps):
            cols = slice(j * part, (j + 1) * part)
            grad = grad_ref[n * chunk : (n + 1) * chunk, j].reshape(chunk * row_part, part).astype(F32)
            first = 0.9 * mom[n, :, cols] + 0.1 * grad
            second = 0.95 * sec[n, :, cols] + 0.05 * grad * grad
            mom[n, :, cols] = first
            sec[n, :, cols] = second
            way = first / (jnp.sqrt(second) + 1e-08)
            total += jnp.sum((way * way).reshape(-1, 8, part), axis=0)
        for i, (src, dst) in enumerate(((mom, mom_out), (sec, sec_out))):
            copy = pltpu.make_async_copy(src.at[n], block(dst, n), out_sems.at[2 * n + i])
            copy.start()
            stores.append(copy)
    own, other = jnp.sum(sum_ref[0]), jnp.sum(total)
    even = at_ref[1] == 0
    values = (jnp.where(even, own, other), jnp.where(even, other, own), jnp.sum(sum_ref[1]))
    tile = pads.shape[2:]
    row = lax.broadcasted_iota(jnp.int32, tile, 0)
    pad = jnp.zeros(tile, F32)
    for i, value in enumerate(values):
        rest = jnp.full(tile, value, F32)
        for n in range(3):
            high = rest.astype(BF16).astype(F32)
            pad = jnp.where(row == 3 * i + n, high, pad)
            rest = rest - high
    pads[...] = jnp.broadcast_to(pad.astype(BF16), pads.shape)
    copy = pltpu.make_async_copy(pads, pieces.at[:, :, :, pl.ds(2 * part, LANES)], out_sems.at[2 * steps])
    copy.start()
    for store in stores + [copy]:
        store.wait()


def late(at, grad, moment, second, sums, moment_new, second_new, pieces, steps=4):
    _, rows, size = moment.shape
    state = shape(moment.shape, F32)
    return pl.pallas_call(
        late_kernel,
        in_specs=[SMEM, ANY, ANY, ANY, VMEM, ANY, ANY, ANY],
        out_specs=(ANY,) * 3,
        scratch_shapes=[
            pltpu.VMEM(grad.shape, BF16),
            pltpu.VMEM((steps, rows // steps, size), F32),
            pltpu.VMEM((steps, rows // steps, size), F32),
            pltpu.VMEM(pieces.shape[:3] + (LANES,), BF16),
            pltpu.SemaphoreType.DMA((2 * steps + 1,)),
            pltpu.SemaphoreType.DMA((2 * steps + 1,)),
        ],
        out_shape=(state, state, shape(pieces.shape, BF16)),
        input_output_aliases={5: 0, 6: 1, 7: 2},
        compiler_params=params(LATE_LIMIT),
        cost_estimate=cost(15 * rows * size, 20 * rows * size),
        name="other_adam",
    )(at, grad, moment, second, sums, moment_new, second_new, pieces)


def add_kernel(at_ref, term_ref, stat_ref, _, new_ref, term, stat, sems, out_sems):
    k = 1 - at_ref[1]
    steps = stat.shape[0]
    rows = stat.shape[1]
    gets = [
        (load(stat_ref.at[k, pl.ds(n * rows, rows)], stat.at[n], sems.at[n]), load(term_ref.at[pl.ds(n * rows, rows)], term.at[n], sems.at[steps + n]))
        for n in range(steps)
    ]
    puts = []
    for n in range(steps):
        for copy in gets[n]:
            copy.wait()
        stat[n] = 0.95 * stat[n] + term[n].astype(F32)
        puts.append(load(stat.at[n], new_ref.at[k, pl.ds(n * rows, rows)], out_sems.at[n]))
    for copy in puts:
        copy.wait()


def add(at, term, stat, new, estimate, steps=4):
    _, rows, size = stat.shape
    return pl.pallas_call(
        add_kernel,
        in_specs=[SMEM, ANY, ANY, ANY],
        out_specs=ANY,
        out_shape=shape(stat.shape, F32),
        scratch_shapes=[
            pltpu.VMEM((steps, rows // steps, size), BF16),
            pltpu.VMEM((steps, rows // steps, size), F32),
            pltpu.SemaphoreType.DMA((2 * steps,)),
            pltpu.SemaphoreType.DMA((steps,)),
        ],
        input_output_aliases={3: 0},
        compiler_params=params(BIG_LIMIT),
        cost_estimate=estimate,
        name="add_term",
    )(at, term, stat, new)


def finish_kernel(cells, slot_ref, in_ref, out_hbm, ratios, out_ref, sems):
    rows = in_ref.shape[1]
    part = (in_ref.shape[2] - LANES) // 2
    sums = in_ref[:, :, 2 * part :].astype(F32).reshape(-1, REPS, rows, LANES)
    adam_sums = jnp.sum(sums, axis=1)
    for k in range(2):
        adam_all = jnp.sum(adam_sums[:, 3 * k : 3 * k + 3], axis=1, keepdims=True)
        pre_all = jnp.sum((sums[:, k] + sums[:, k + 2])[:, 6:8], axis=1, keepdims=True)
        value = jnp.sqrt(adam_all / cells + 1e-06) / jnp.sqrt(pre_all / cells + 1e-06)
        ratios[:, k] = jnp.broadcast_to(value, (value.shape[0], rows, LANES))

    def place_block(b, _):
        slot = slot_ref[b]
        owner, k = slot // 2, lax.rem(slot, 2)
        by = ratios[owner, k]
        by = jnp.concatenate([by] * (2 * part // LANES), axis=1)
        for n in range(2):
            piece = in_ref[owner * REPS + k + 2 * n, :, : 2 * part].astype(F32) * by
            piece = jnp.concatenate([piece[:, :part], piece[:, part:]], axis=0)
            out_ref[b, 2 * n * rows : 2 * (n + 1) * rows, :] = piece.astype(BF16)
        return 0

    chunk = out_ref.shape[0] // DEALS
    puts = []
    for n in range(DEALS):
        lax.fori_loop(n * chunk, (n + 1) * chunk, place_block, 0, unroll=8)
        part_of = pl.ds(n * chunk, chunk)
        puts.append(load(out_ref.at[part_of], out_hbm.at[part_of], sems.at[n]))
    for copy in puts:
        copy.wait()


def finish(owner_slot, pieces, size):
    count, rows, wide = pieces.shape
    blocks = owner_slot.shape[0]
    part = (wide - LANES) // 2
    return pl.pallas_call(
        functools.partial(finish_kernel, float(size * size)),
        out_shape=shape((blocks, 4 * rows, part), BF16),
        in_specs=[SMEM, VMEM],
        out_specs=ANY,
        scratch_shapes=[
            pltpu.VMEM((blocks // 2, 2, rows, LANES), F32),
            pltpu.VMEM((blocks, 4 * rows, part), BF16),
            pltpu.SemaphoreType.DMA((DEALS,)),
        ],
        compiler_params=params(),
        cost_estimate=cost(8 * blocks * rows * part, 20 * blocks * rows * part),
        name="finish_updates",
    )(owner_slot, pieces)


def per_device(grads, owner_slot, gram_left, gram_right, root_left, root_right, moment, second):
    blocks, row_part, part = grads.shape
    _, rows, size = root_left.shape
    at = place()
    sent = deal(owner_slot, grads)
    keep, ahead, across, back = share_rows(at, root_left, row_part)
    arrived = everyone(sent).reshape(OWNERS, REPS, row_part, part)
    ahead = to_neighbour(ahead)
    across = to_neighbour(across, 2)
    back = to_neighbour(back, -1)

    count = rows // row_part
    other = to_neighbour(lax.dynamic_slice_in_dim(arrived, at[2] * count, count, 0))
    left_new, right_new, left_term, right_term = grams(at, arrived, gram_left, gram_right)
    arrived, left_term, right_term = lax.optimization_barrier((arrived, left_term, right_term))
    right_term = to_neighbour(right_term)
    left_term = to_neighbour(left_term)
    moment_new, second_new, pieces, sums = mid(
        at, arrived, (keep, ahead, across, back), root_right, moment, second
    )
    moment_new, second_new, pieces = late(
        at, other, moment, second, sums, moment_new, second_new, pieces
    )
    pieces, right_term = lax.optimization_barrier((pieces, right_term))
    homed = everyone(pieces.reshape((-1,) + pieces.shape[2:]))
    right_new = add(at, right_term, gram_right, right_new, MID_COST)
    right_new, left_new = lax.optimization_barrier((right_new, left_new))
    left_new = add(at, left_term, gram_left, left_new, GRAM_COST)
    updates = finish(owner_slot, homed, size)
    return (updates, left_new, right_new, moment_new, second_new)


def solution(mesh):
    return jax.shard_map(
        per_device,
        mesh=mesh,
        in_specs=(
            P(None, "fsdp", "rep"),
            P(),
            P("fsdp", "rep", None),
            P("fsdp", "rep", None),
            P("fsdp", "rep", None),
            P("fsdp", None, None),
            P("fsdp", "rep", None),
            P("fsdp", "rep", None),
        ),
        out_specs=(
            P(None, "fsdp", "rep"),
            P("fsdp", "rep", None),
            P("fsdp", "rep", None),
            P("fsdp", "rep", None),
            P("fsdp", "rep", None),
        ),
        check_vma=False,
    )
```

time: 106 us -> 99.9 us (0.942)
  waiting for transfers between devices: 46.2 us -> 40.5 us
  Pallas kernels: 27.3 us -> 31.5 us
  local copies, waits for them, and re-layouts: 6.14 us -> 2.85 us
  starting transfers between devices: 24.2 us -> 23.1 us
    ppermute x6, waiting for transfers between devices: 18.9 us -> 0.02 us  [to_neighbour(): return lax.ppermute(x, ('fsdp', 'rep'), pairs)]
    all_to_all x2, waiting for transfers between devices: 27.3 us -> 40.5 us  [everyone(): lax.all_to_all(x, ('fsdp', 'rep'), split_axis=0, concat_axis=0, tiled=True)]
    pallas_call x3 -> x5, Pallas kernels: 10 us -> 15.6 us  [the longest x2 5.73 us: add(): pl.pallas_call(add_kernel, in_specs=[SMEM, ANY, ANY, ANY], out_specs=ANY,...]
    unnamed x18 -> x14, local copies, waits for them, and re-layouts: 6.1 us -> 2.81 us
    ppermute x6, starting transfers between devices: 6.69 us -> 5.04 us  [to_neighbour(): return lax.ppermute(x, ('fsdp', 'rep'), pairs)]
  transfers between devices with their start and end apart: 8 -> 8, of which waited for: 2 -> 2; matrix products, arithmetic and copies ran while one was open for 0% -> 1% of each run, Pallas kernels for 20% -> 26%
where the time goes in v4:
time: 99.9 us; the launch traced here: 99.4 us
  waiting for transfers between devices  40.5 us (41%)
  Pallas kernels  31.5 us (32%)
  starting transfers between devices  23.1 us (23%)
  local copies, waits for them, and re-layouts  2.85 us (3%)
    all_to_all x2, waiting for transfers between devices, everyone(): lax.all_to_all(x, ('fsdp', 'rep'), split_axis=0, concat_axis=0, tiled=True)  40.5 us
    all_to_all x2, starting transfers between devices, everyone(): lax.all_to_all(x, ('fsdp', 'rep'), split_axis=0, concat_axis=0, tiled=True)  18 us
    pallas_call x1, Pallas kernels, mid(): pl.pallas_call(mid_kernel, in_specs=[SMEM] + [ANY] * 8, out_specs=(ANY,)...  7.44 us
    pallas_call x1, Pallas kernels, grams(): pl.pallas_call(gram_kernel, in_specs=[SMEM] + [ANY] * 3, out_specs=(ANY,)...  6.34 us
    pallas_call x2, Pallas kernels, add(): pl.pallas_call(add_kernel, in_specs=[SMEM, ANY, ANY, ANY], out_specs=ANY,...  5.73 us
    ppermute x6, starting transfers between devices, to_neighbour(): return lax.ppermute(x, ('fsdp', 'rep'), pairs)  5.04 us
    pallas_call x1, Pallas kernels, late(): pl.pallas_call(late_kernel, in_specs=[SMEM, ANY, ANY, ANY, VMEM, ANY, ANY...  3.7 us
    pallas_call x1, Pallas kernels, deal(): pl.pallas_call(deal_kernel, out_shape=shape((2 * blocks, row_part, part),...  3.27 us
  transfers between devices with their start and end apart: 8, of which 2 were waited for; matrix products, arithmetic and copies ran while one was open for 1% of the time, Pallas kernels for 26%

profile of v4, /device:TPU:1, one launch (start us, length us, event | category | flops | bytes accessed | tf_op | source)
XLA Modules:
  0.0 99.4 jit_solution(3975740731291969246)
XLA Ops:
  0.6 3.3 %deal_blocks.1 = bf16[128,32,256]{2,1,0:T(8,128)(2,1)} custom-call(s32[64]{0:T(128)} %slot_ref.3, bf16[64,32,256]{2,1,0:T(8,128)(2,1)} %grads_ref.1), custom_call_target="tpu_custom_call" | custom-call | bytes 3145728 | tf_op jit(solution)/shard_map/deal_blocks/pallas_call | solution.py:115
  3.9 11.5 %all-to-all-start = ((bf16[128,32,256]{2,1,0:T(8,128)(2,1)}), bf16[128,32,256]{2,1,0:T(8,128)(2,1)S(1)}, u32[]{:S(2)}, u32[]{:S(2)}) async-start(bf16[128,32,256]{2,1,0:T(8,128)(2,1)} %deal_blocks.1), calls=%async_computation | async-start | bytes 4194304 | tf_op jit(solution)/shard_map/all_to_all | solution.py:65
  15.4 0.7 pad_add_fusion.at_ref
  16.1 2.9 %share_rows.1 = (bf16[8,16,1024]{2,1,0:T(8,128)(2,1)}, bf16[8,16,1024]{2,1,0:T(8,128)(2,1)}, bf16[8,16,1024]{2,1,0:T(8,128)(2,1)}, bf16[8,16,1024]{2,1,0:T(8,128)(2,1)}) custom-call(s32[4]{0:T(128)} %pad_add_fusion.at_ref, bf16[2,8,2,16,1024]{4,3,2,1,0:T(8,128)(2,1)} %bitcast.11), custom_call_target="tpu_custom_call" | custom-call | bytes 2097152 | tf_op jit(solution)/shard_map/share_rows/pallas_call | solution.py:146
  19.0 2.7 %collective-permute-start.1 = (bf16[8,16,1024]{2,1,0:T(8,128)(2,1)}, bf16[8,16,1024]{2,1,0:T(8,128)(2,1)S(1)}, u32[]{:S(2)}, u32[]{:S(2)}) collective-permute-start(bf16[8,16,1024]{2,1,0:T(8,128)(2,1)} %get-tuple-element.31), channel_id=1, source_target_pairs={{0,1},{1,2},{2,3},{3,0},{4,7},{5,4},{6,5},{7,6},{8,9},{9,10},{10,1... | collective-permute-start | bytes 786440 | tf_op jit(solution)/shard_map/ppermute | solution.py:61
  21.7 0.5 collective-permute-start.2
  22.2 0.6 collective-permute-start.3
  22.8 23.7 %all-to-all-done = bf16[128,32,256]{2,1,0:T(8,128)(2,1)S(1)} async-done(((bf16[128,32,256]{2,1,0:T(8,128)(2,1)}), bf16[128,32,256]{2,1,0:T(8,128)(2,1)S(1)}, u32[]{:S(2)}, u32[]{:S(2)}) %all-to-all-start) | async-done | bytes 2097184 | tf_op jit(solution)/shard_map/all_to_all | solution.py:65
  46.6 0.1 collective-permute-start
  46.6 1.2 %copy-done.1 = bf16[128,32,256]{2,1,0:T(8,128)(2,1)} copy-done((bf16[128,32,256]{2,1,0:T(8,128)(2,1)}, bf16[128,32,256]{2,1,0:T(8,128)(2,1)S(1)}, u32[]{:S(2)}) %copy-start.1) | copy-done | bytes 2097176
  47.9 6.3 %own_grams.1 = (f32[2,256,1024]{2,1,0:T(8,128)}, f32[2,256,1024]{2,1,0:T(8,128)}, bf16[256,1024]{1,0:T(8,128)(2,1)}, bf16[256,1024]{1,0:T(8,128)(2,1)}) custom-call(s32[4]{0:T(128)} %pad_add_fusion.at_ref, bf16[32,4,32,256]{3,2,1,0:T(8,128)(2,1)} %bitcast.8, f32[2,256,1024]{2,1,0:T(8,128)} %stat_ref.3, f32[2,256,1024]{2,1,0:T(8,128)} %stat_ref.2), custom_call_target="tpu_custom_call" | custom-call | flops 1 | bytes 1 | tf_op jit(solution)/shard_map/own_grams/pallas_call | solution.py:203
  54.2 0.1 collective-permute-start.4
  54.3 0.0 collective-permute-done.1.l1_ref
  54.3 1.1 %collective-permute-start.5 = (bf16[256,1024]{1,0:T(8,128)(2,1)}, bf16[256,1024]{1,0:T(8,128)(2,1)}, u32[]{:S(2)}, u32[]{:S(2)}) collective-permute-start(bf16[256,1024]{1,0:T(8,128)(2,1)} %get-tuple-element.41), channel_id=1, source_target_pairs={{0,1},{1,2},{2,3},{3,0},{4,7},{5,4},{6,5},{7,6},{8,9},{9,10},{10,1... | collective-permute-start | bytes 1572872 | tf_op jit(solution)/shard_map/ppermute | solution.py:61
  55.4 0.0 collective-permute-done.2.l2_ref
  55.4 0.0 collective-permute-done.3.l3_ref
  55.4 0.7 copy-done.5
  56.1 0.1 copy-done.6
  56.2 7.4 %own_slot.1 = (f32[2,256,1024]{2,1,0:T(8,128)}, f32[2,256,1024]{2,1,0:T(8,128)}, bf16[32,4,8,640]{3,2,1,0:T(8,128)(2,1)}, f32[2,8,256]{2,1,0:T(8,128)}) custom-call(s32[4]{0:T(128)} %pad_add_fusion.at_ref, bf16[32,4,32,256]{3,2,1,0:T(8,128)(2,1)} %bitcast.9, bf16[8,16,1024]{2,1,0:T(8,128)(2,1)} %get-tuple-element.30.l0_ref, bf16[8,16,1024]{2,1,0:T(8,128)(2,1)} %copy-done.4, ...), custom_call_target="tpu_custom_call" | custom-call | flops 99999997952 | bytes 1000000 | tf_op jit(solution)/shard_map/own_slot/pallas_call | solution.py:288
  63.6 0.0 collective-permute-done.grad_hbm
  63.7 0.0 copy-start.2
  63.7 0.8 copy-done.2
  64.5 3.7 %other_adam.1 = (f32[2,256,1024]{2,1,0:T(8,128)}, f32[2,256,1024]{2,1,0:T(8,128)}, bf16[32,4,8,640]{3,2,1,0:T(8,128)(2,1)}) custom-call(s32[4]{0:T(128)} %pad_add_fusion.at_ref, bf16[8,4,32,256]{3,2,1,0:T(8,128)(2,1)} %copy-done.2, f32[2,256,1024]{2,1,0:T(8,128)} %mom_ref.3, ...), custom_call_target="tpu_custom_call", output_to_operand_aliasing={{0}: (5, {}), {1}: (6, {}), {2}: (7, {})} | custom-call | flops 3932160 | bytes 5242880 | tf_op jit(solution)/shard_map/other_adam/pallas_call | solution.py:372
  68.2 0.0 collective-permute-done.4.term_ref
  68.2 0.0 copy-start.3
  68.2 6.5 %all-to-all-start.1 = ((bf16[128,8,640]{2,1,0:T(8,128)(2,1)}), bf16[128,8,640]{2,1,0:T(8,128)(2,1)S(1)}, u32[]{:S(2)}, u32[]{:S(2)}) async-start(bf16[128,8,640]{2,1,0:T(8,128)(2,1)} %bitcast.10), calls=%async_computation.1 | async-start | bytes 2621440 | tf_op jit(solution)/shard_map/all_to_all | solution.py:65
  74.7 2.9 %add_term.2 = f32[2,256,1024]{2,1,0:T(8,128)} custom-call(s32[4]{0:T(128)} %pad_add_fusion.at_ref, bf16[256,1024]{1,0:T(8,128)(2,1)} %copy-done.3, f32[2,256,1024]{2,1,0:T(8,128)} %stat_ref.2, f32[2,256,1024]{2,1,0:T(8,128)} %get-tuple-element.43._), custom_call_target="tpu_custom_call", output_to_operand_aliasing={{}: (3, {})} | custom-call | flops 99999997952 | bytes 1000000 | tf_op jit(solution)/shard_map/add_term/pallas_call | solution.py:412
  77.6 0.0 copy-start
  77.6 0.0 collective-permute-done.5.term_ref
  77.6 2.9 %add_term.3 = f32[2,256,1024]{2,1,0:T(8,128)} custom-call(s32[4]{0:T(128)} %pad_add_fusion.at_ref, bf16[256,1024]{1,0:T(8,128)(2,1)} %collective-permute-done.5.term_ref, f32[2,256,1024]{2,1,0:T(8,128)} %stat_ref.3, f32[2,256,1024]{2,1,0:T(8,128)} %get-tuple-element.45._), custom_call_target="tpu_custom_call", output_to_operand_aliasing={{}: (3, {})} | custom-call | flops 1 | bytes 1 | tf_op jit(solution)/shard_map/add_term/pallas_call | solution.py:412
  80.5 16.8 %all-to-all-done.1.in_ref = bf16[128,8,640]{2,1,0:T(8,128)(2,1)S(1)} async-done(((bf16[128,8,640]{2,1,0:T(8,128)(2,1)}), bf16[128,8,640]{2,1,0:T(8,128)(2,1)S(1)}, u32[]{:S(2)}, u32[]{:S(2)}) %all-to-all-start.1) | async-done | bytes 1310752 | tf_op jit(solution)/shard_map/all_to_all | solution.py:65
  97.3 2.1 %finish_updates.1 = bf16[64,32,256]{2,1,0:T(8,128)(2,1)} custom-call(s32[64]{0:T(128)S(1)} %copy-done, bf16[128,8,640]{2,1,0:T(8,128)(2,1)S(1)} %all-to-all-done.1.in_ref), custom_call_target="tpu_custom_call" | custom-call | flops 1048576 | bytes 2621440 | tf_op jit(solution)/shard_map/finish_updates/pallas_call | solution.py:466
  (8 shorter events, 0.0 us)
Async XLA Ops:
  3.9 42.6 %all-to-all-start = ((bf16[128,32,256]{2,1,0:T(8,128)(2,1)}), bf16[128,32,256]{2,1,0:T(8,128)(2,1)S(1)}, u32[]{:S(2)}, u32[]{:S(2)}) async-start(bf16[128,32,256]{2,1,0:T(8,128)(2,1)} %deal_blocks.1), calls=%async_computation | async-start | bytes 4194304 | tf_op jit(solution)/shard_map/all_to_all | solution.py:65
  19.0 35.3 %collective-permute-start.1 = (bf16[8,16,1024]{2,1,0:T(8,128)(2,1)}, bf16[8,16,1024]{2,1,0:T(8,128)(2,1)S(1)}, u32[]{:S(2)}, u32[]{:S(2)}) collective-permute-start(bf16[8,16,1024]{2,1,0:T(8,128)(2,1)} %get-tuple-element.31), channel_id=1, source_target_pairs={{0,1},{1,2},{2,3},{3,0},{4,7},{5,4},{6,5},{7,6},{8,9},{9,10},{10,1... | collective-permute-start | bytes 786440 | tf_op jit(solution)/shard_map/ppermute | solution.py:61
  21.7 33.7 %collective-permute-start.2 = (bf16[8,16,1024]{2,1,0:T(8,128)(2,1)}, bf16[8,16,1024]{2,1,0:T(8,128)(2,1)S(1)}, u32[]{:S(2)}, u32[]{:S(2)}) collective-permute-start(bf16[8,16,1024]{2,1,0:T(8,128)(2,1)} %get-tuple-element.32), channel_id=1, source_target_pairs={{0,2},{1,3},{2,0},{3,1},{4,6},{5,7},{6,4},{7,5},{8,10},{9,11},{10,... | collective-permute-start | bytes 786440 | tf_op jit(solution)/shard_map/ppermute | solution.py:61
  22.2 33.1 %collective-permute-start.3 = (bf16[8,16,1024]{2,1,0:T(8,128)(2,1)}, bf16[8,16,1024]{2,1,0:T(8,128)(2,1)S(1)}, u32[]{:S(2)}, u32[]{:S(2)}) collective-permute-start(bf16[8,16,1024]{2,1,0:T(8,128)(2,1)} %get-tuple-element.33), channel_id=1, source_target_pairs={{0,3},{1,0},{2,1},{3,2},{4,5},{5,6},{6,7},{7,4},{8,11},{9,8},{10,9... | collective-permute-start | bytes 786440 | tf_op jit(solution)/shard_map/ppermute | solution.py:61
  46.5 1.3 %copy-start.1 = (bf16[128,32,256]{2,1,0:T(8,128)(2,1)}, bf16[128,32,256]{2,1,0:T(8,128)(2,1)S(1)}, u32[]{:S(2)}) copy-start(bf16[128,32,256]{2,1,0:T(8,128)(2,1)S(1)} %all-to-all-done) | copy-start | bytes 6291460
  46.6 17.1 %collective-permute-start = (bf16[8,4,32,256]{3,2,1,0:T(8,128)(2,1)S(1)}, bf16[8,4,32,256]{3,2,1,0:T(8,128)(2,1)S(1)}, u32[]{:S(2)}, u32[]{:S(2)}) collective-permute-start(bf16[8,4,32,256]{3,2,1,0:T(8,128)(2,1)S(1)} %constant_dynamic-slice_fusion), channel_id=1, source_target_pairs={{0,1},{1,2},{2,3},{3,0},{4,7},{5,4},{6,5},{7,6},{8,9},{9,10},{10,1... | collective-permute-start | bytes 1572872 | tf_op jit(solution)/shard_map/ppermute | solution.py:61
  54.2 14.0 %collective-permute-start.4 = (bf16[256,1024]{1,0:T(8,128)(2,1)}, bf16[256,1024]{1,0:T(8,128)(2,1)S(1)}, u32[]{:S(2)}, u32[]{:S(2)}) collective-permute-start(bf16[256,1024]{1,0:T(8,128)(2,1)} %get-tuple-element.39), channel_id=1, source_target_pairs={{0,1},{1,2},{2,3},{3,0},{4,7},{5,4},{6,5},{7,6},{8,9},{9,10},{10,1... | collective-permute-start | bytes 1572872 | tf_op jit(solution)/shard_map/ppermute | solution.py:61
  54.3 1.1 %copy-start.4 = (bf16[8,16,1024]{2,1,0:T(8,128)(2,1)}, bf16[8,16,1024]{2,1,0:T(8,128)(2,1)S(1)}, u32[]{:S(2)}) copy-start(bf16[8,16,1024]{2,1,0:T(8,128)(2,1)S(1)} %collective-permute-done.1.l1_ref) | copy-start | bytes 786436
  54.3 23.3 %collective-permute-start.5 = (bf16[256,1024]{1,0:T(8,128)(2,1)}, bf16[256,1024]{1,0:T(8,128)(2,1)}, u32[]{:S(2)}, u32[]{:S(2)}) collective-permute-start(bf16[256,1024]{1,0:T(8,128)(2,1)} %get-tuple-element.41), channel_id=1, source_target_pairs={{0,1},{1,2},{2,3},{3,0},{4,7},{5,4},{6,5},{7,6},{8,9},{9,10},{10,1... | collective-permute-start | bytes 1572872 | tf_op jit(solution)/shard_map/ppermute | solution.py:61
  55.4 0.7 copy-start.5
  55.4 0.8 copy-start.6
  63.7 0.8 copy-start.2
  68.2 6.5 %copy-start.3 = (bf16[256,1024]{1,0:T(8,128)(2,1)}, bf16[256,1024]{1,0:T(8,128)(2,1)S(1)}, u32[]{:S(2)}) copy-start(bf16[256,1024]{1,0:T(8,128)(2,1)S(1)} %collective-permute-done.4.term_ref) | copy-start | bytes 1572868
  68.2 29.1 %all-to-all-start.1 = ((bf16[128,8,640]{2,1,0:T(8,128)(2,1)}), bf16[128,8,640]{2,1,0:T(8,128)(2,1)S(1)}, u32[]{:S(2)}, u32[]{:S(2)}) async-start(bf16[128,8,640]{2,1,0:T(8,128)(2,1)} %bitcast.10), calls=%async_computation.1 | async-start | bytes 2621440 | tf_op jit(solution)/shard_map/all_to_all | solution.py:65
  77.6 19.7 %copy-start = (s32[64]{0:T(128)S(1)}, s32[64]{0:T(128)}, u32[]{:S(2)}) copy-start(s32[64]{0:T(128)} %slot_ref.3) | copy-start | bytes 772

commit v5 on v4

--- a/solution.py
+++ b/solution.py
@@ -8,10 +8,11 @@
 from jax.sharding import PartitionSpec as P
 
 VMEM_LIMIT = 32 * 1024 * 1024
-MID_LIMIT = 60 * 1024 * 1024
+GRAM_LIMIT = 50 * 1024 * 1024
+MID_LIMIT = 46 * 1024 * 1024
 BIG_LIMIT = 60 * 1024 * 1024
 DEALS = 4
-LATE_LIMIT = 60 * 1024 * 1024
+LATE_LIMIT = 46 * 1024 * 1024
 REPS = 4
 OWNERS = 32
 LANES = 128
@@ -71,13 +72,6 @@
     return copy
 
 
-def load_columns(arrived, whole, sems):
-    part = arrived.shape[3]
-    return [
-        load(arrived.at[:, j], whole.at[:, :, pl.ds(j * part, part)], sems.at[j]) for j in range(arrived.shape[1])
-    ]
-
-
 def deal_kernel(slot_ref, grads_ref, out_ref, grads, out, block_of, sems):
     blocks = grads.shape[0]
     chunk = blocks // DEALS
@@ -155,161 +149,188 @@
     )(at, root_left.reshape(2, count, 2, half, size))
 
 
-def gram_kernel(
-    at_ref, arrived, stat_left, stat_right, left_out, right_out, left_term, right_term,
-    whole, lhs, gl, gr, lt, rt, sems, out_sems,
+def near_kernel(
+    at_ref, g_ref, mom_ref, sec_ref, terms_ref, mom_out, sec_out, sum_ref,
+    whole, lhs, terms, mom, sec, sems, out_sems,
 ):
     rep, k, near = at_ref[0], at_ref[1], at_ref[2]
-    _, row_part, size = whole.shape
-    part = size // REPS
-    rows = gl.shape[0]
-    columns = load_columns(arrived, whole, sems)
-    get_gr = load(stat_right.at[k], gr, sems.at[REPS])
-    get_gl = load(stat_left.at[k], gl, sems.at[REPS + 1])
-    for copy in columns:
-        copy.wait()
+    owners, reps, row_part, part = g_ref.shape
+    size = owners * row_part
+    rows = mom.shape[0]
+    blocks = rows // row_part
+    get_mom = load(mom_ref.at[k], mom, sems.at[0])
+    get_sec = load(sec_ref.at[k], sec, sems.at[1])
     puts = []
 
-    def emit(j, term, stat, terms, new_ref, term_ref):
+    def put(src, dst):
+        puts.append(load(src, dst, out_sems.at[len(puts)]))
+
+    lhs[...] = g_ref[:, pl.ds(near, 1)].reshape(size, part).T
+    for j in range(reps):
         cols = pl.ds(j * part, part)
-        stat[:, cols] = 0.95 * stat[:, cols] + term[:rows]
-        terms[:, cols] = term[rows:].astype(BF16)
-        for src, dst in ((stat, new_ref.at[k]), (terms, term_ref)):
-            puts.append(load(src.at[:, cols], dst.at[:, cols], out_sems.at[len(puts)]))
-
-    for i, index in enumerate((rep, near)):
-        cols = whole[:, :, pl.ds(pl.multiple_of(index * part, part), part)].reshape(size, part)
-        lhs[i * rows : (i + 1) * rows, :] = cols.T
-    get_gr.wait()
-    for j in range(REPS):
-        grad = whole[:, :, j * part : (j + 1) * part].reshape(size, part)
-        emit(j, 0.05 * dot(lhs[...], grad), gr, rt, right_out, right_term)
-    for i, index in enumerate((rep, near)):
-        from_row = pl.ds(index * (rows // row_part), rows // row_part)
-        lhs[i * rows : (i + 1) * rows, :] = whole[from_row].reshape(rows, size)
-    get_gl.wait()
-    blocks = part // row_part
-    for j in range(REPS):
-        grad = whole[j * blocks : (j + 1) * blocks].reshape(part, size)
-        emit(j, 0.05 * dot(lhs[...], grad, NT), gl, lt, left_out, left_term)
-    for copy in puts:
-        copy.wait()
-
-
-def grams(at, arrived, gram_left, gram_right):
-    owners, reps, row_part, part = arrived.shape
-    _, rows, size = gram_left.shape
-    state = shape(gram_left.shape, F32)
-    return pl.pallas_call(
-        gram_kernel,
-        in_specs=[SMEM] + [ANY] * 3,
-        out_specs=(ANY,) * 4,
-        scratch_shapes=[
-            pltpu.VMEM((owners, row_part, size), BF16),
-            pltpu.VMEM((2 * rows, size), BF16),
-            pltpu.VMEM((rows, size), F32),
-            pltpu.VMEM((rows, size), F32),
-            pltpu.VMEM((rows, size), BF16),
-            pltpu.VMEM((rows, size), BF16),
-            pltpu.SemaphoreType.DMA((REPS + 2,)),
-            pltpu.SemaphoreType.DMA((4 * REPS,)),
-        ],
-        out_shape=(state,) * 2 + (shape((rows, size), BF16),) * 2,
-        compiler_params=params(MID_LIMIT),
-        cost_estimate=GRAM_COST,
-        name="own_grams",
-    )(at, arrived, gram_left, gram_right)
-
-
-def mid_kernel(
-    at_ref, arrived, l0_ref, l1_ref, l2_ref, l3_ref, right_ref, mom_ref, sec_ref, mom_out, sec_out, pieces, sum_ref,
-    whole, left, right, mixed, mom, sec, out, sems, out_sems,
-):
-    rep, k, step = at_ref[0], at_ref[1], at_ref[3]
-    owners, row_part, size = whole.shape
-    part = size // REPS
-    rows = mom.shape[0]
-    share = l0_ref.shape[0]
-    get_left = []
-    for j, ref in enumerate((l0_ref, l1_ref, l2_ref, l3_ref)):
-        first = lax.rem(rep - j * step + REPS * REPS, REPS) * share
-        get_left.append(load(ref, left.at[pl.ds(first, share)], sems.at[REPS + 2 + j]))
-    columns = load_columns(arrived, whole, sems)
-    get_mom = load(mom_ref.at[k], mom, sems.at[REPS])
-    get_sec = load(sec_ref.at[k], sec, sems.at[REPS + 1])
-    half = size // 2
-    get_right = [
-        load(right_ref.at[k, :, pl.ds(i * half, half)], right.at[:, pl.ds(i * half, half)], sems.at[2 * REPS + 2 + i])
-        for i in range(2)
-    ]
-    for copy in get_left + columns:
-        copy.wait()
-    for j in range(REPS):
-        grad = whole[:, :, j * part : (j + 1) * part].reshape(size, part)
-        mixed[:, j * part : (j + 1) * part] = dot(left[...].reshape(mixed.shape), grad).astype(BF16)
-
+        terms[0, :, cols] = (0.05 * dot(lhs[...], g_ref[:, j].reshape(size, part))).astype(BF16)
+        put(terms.at[0, :, cols], terms_ref.at[0, :, cols])
+    for j in range(reps):
+        cols = slice(j * part, (j + 1) * part)
+        whole[:, cols] = g_ref[:, j].reshape(size, part)
+    rows_near = whole[pl.ds(pl.multiple_of(near * rows, rows), rows), :]
+    for j in range(reps):
+        cols = pl.ds(j * part, part)
+        terms[1, :, cols] = (0.05 * dot(rows_near, whole[j * part : (j + 1) * part, :], NT)).astype(BF16)
+        put(terms.at[1, :, cols], terms_ref.at[1, :, cols])
     get_mom.wait()
     get_sec.wait()
-    own_total = jnp.zeros((8, part), F32)
-    puts = []
-    for j in range(REPS):
+    total = jnp.zeros((8, part), F32)
+    for j in range(reps):
         cols = pl.ds(j * part, part)
-        own = whole[pl.ds(rep * (rows // row_part), rows // row_part), :, cols].reshape(rows, part).astype(F32)
+        own = g_ref[pl.ds(rep * blocks, blocks), j].reshape(rows, part).astype(F32)
         first = 0.9 * mom[:, cols] + 0.1 * own
         second = 0.95 * sec[:, cols] + 0.05 * own * own
         mom[:, cols] = first
         sec[:, cols] = second
         way = first / (jnp.sqrt(second) + 1e-08)
-        own_total += jnp.sum((way * way).reshape(rows // 8, 8, part), axis=0)
-        for src, dst in ((mom, mom_out), (sec, sec_out)):
-            puts.append(load(src.at[:, cols], dst.at[k, :, cols], out_sems.at[len(puts)]))
-    sum_ref[0] = own_total
-
+        total += jnp.sum((way * way).reshape(rows // 8, 8, part), axis=0)
+        put(mom.at[:, cols], mom_out.at[k, :, cols])
+        put(sec.at[:, cols], sec_out.at[k, :, cols])
+    sum_ref[...] = total
+    for copy in puts:
+        copy.wait()
+
+
+def near_terms(at, arrived, moment, second):
+    _, reps, _, part = arrived.shape
+    _, rows, size = moment.shape
+    state = shape(moment.shape, F32)
+    return pl.pallas_call(
+        near_kernel,
+        in_specs=[SMEM, VMEM, ANY, ANY],
+        out_specs=(ANY,) * 3 + (VMEM,),
+        scratch_shapes=[
+            pltpu.VMEM((size, size), BF16),
+            pltpu.VMEM((rows, size), BF16),
+            pltpu.VMEM((2, rows, size), BF16),
+            pltpu.VMEM((rows, size), F32),
+            pltpu.VMEM((rows, size), F32),
+            pltpu.SemaphoreType.DMA((2,)),
+            pltpu.SemaphoreType.DMA((4 * reps,)),
+        ],
+        out_shape=(shape((2, rows, size), BF16), state, state, shape((8, part), F32)),
+        compiler_params=params(GRAM_LIMIT),
+        cost_estimate=GRAM_COST,
+        name="near_terms",
+    )(at, arrived, moment, second)
+
+
+def precond_kernel(
+    at_ref, g_ref, l0_ref, l1_ref, l2_ref, l3_ref, right_ref, pieces, sum_ref, left, right, mixed, out, sems, out_sems
+):
+    rep, k, step = at_ref[0], at_ref[1], at_ref[3]
+    owners, reps, row_part, part = g_ref.shape
+    size = owners * row_part
+    share = l0_ref.shape[0]
+    get_left = []
+    for j, ref in enumerate((l0_ref, l1_ref, l2_ref, l3_ref)):
+        first = lax.rem(rep - j * step + REPS * REPS, REPS) * share
+        get_left.append(load(ref, left.at[pl.ds(first, share)], sems.at[j]))
+    half = size // 2
+    get_right = [
+        load(right_ref.at[k, :, pl.ds(i * half, half)], right.at[:, pl.ds(i * half, half)], sems.at[REPS + i])
+        for i in range(2)
+    ]
+    for copy in get_left:
+        copy.wait()
+    for j in range(reps):
+        grad = g_ref[:, j].reshape(size, part)
+        mixed[:, j * part : (j + 1) * part] = dot(left[...].reshape(mixed.shape), grad).astype(BF16)
     for copy in get_right:
         copy.wait()
     total = jnp.zeros((8, part), F32)
-    for j in range(REPS):
+    puts = []
+    for j in range(reps):
         piece = dot(mixed[...], right[:, j * part : (j + 1) * part])
         total += jnp.sum((piece * piece).reshape(-1, 8, part), axis=0)
         halves = piece.reshape(owners, 2, 8, part)
         for i in range(2):
             out[:, j, :, i * part : (i + 1) * part] = halves[:, i].astype(BF16)
-        puts.append(load(out.at[:, j], pieces.at[:, j, :, pl.ds(0, 2 * part)], out_sems.at[len(puts)]))
-    sum_ref[1] = total
+        puts.append(load(out.at[:, j], pieces.at[:, j, :, pl.ds(0, 2 * part)], out_sems.at[j]))
+    sum_ref[...] = total
     for copy in puts:
         copy.wait()
 
 
-def mid(at, arrived, left_parts, root_right, moment, second):
+def precond(at, arrived, left_parts, root_right):
     owners, reps, row_part, part = arrived.shape
-    _, rows, size = moment.shape
+    size = root_right.shape[1]
     half = row_part // 2
-    state = shape(moment.shape, F32)
-    return pl.pallas_call(
-        mid_kernel,
-        in_specs=[SMEM] + [ANY] * 8,
-        out_specs=(ANY,) * 3 + (VMEM,),
-        scratch_shapes=[
-            pltpu.VMEM((owners, row_part, size), BF16),
+    return pl.pallas_call(
+        precond_kernel,
+        in_specs=[SMEM, VMEM] + [ANY] * 5,
+        out_specs=(ANY, VMEM),
+        scratch_shapes=[
             pltpu.VMEM((owners, half, size), BF16),
             pltpu.VMEM((size, size), BF16),
             pltpu.VMEM((owners * half, size), BF16),
+            pltpu.VMEM((owners, reps, half // 2, 2 * part), BF16),
+            pltpu.SemaphoreType.DMA((REPS + 2,)),
+            pltpu.SemaphoreType.DMA((reps,)),
+        ],
+        out_shape=(shape((owners, reps, half // 2, 2 * part + LANES), BF16), shape((8, part), F32)),
+        compiler_params=params(MID_LIMIT),
+        cost_estimate=MID_COST,
+        name="precond_rows",
+    )(at, arrived, *left_parts, root_right)
+
+
+def gram_kernel(at_ref, arrived, stat_left, stat_right, left_out, right_out, whole, gl, gr, sems, out_sems):
+    rep, k = at_ref[0], at_ref[1]
+    _, row_part, size = whole.shape
+    part = size // REPS
+    rows = gl.shape[0]
+    blocks = rows // row_part
+    columns = [load(arrived.at[:, j], whole.at[:, :, pl.ds(j * part, part)], sems.at[j]) for j in range(REPS)]
+    get_gr = load(stat_right.at[k], gr, sems.at[REPS])
+    get_gl = load(stat_left.at[k], gl, sems.at[REPS + 1])
+    for copy in columns:
+        copy.wait()
+    grad = whole[...].reshape(size, size)
+    own = whole[:, :, pl.ds(pl.multiple_of(rep * part, part), part)].reshape(size, part)
+    term = 0.05 * dot(own, grad, TN)
+    get_gr.wait()
+    gr[...] = 0.95 * gr[...] + term
+    put_right = load(gr, right_out.at[k], out_sems.at[0])
+    own = whole[pl.ds(rep * blocks, blocks)].reshape(rows, size)
+    term = 0.05 * dot(own, grad, NT)
+    get_gl.wait()
+    gl[...] = 0.95 * gl[...] + term
+    put_left = load(gl, left_out.at[k], out_sems.at[1])
+    put_right.wait()
+    put_left.wait()
+
+
+def grams(at, arrived, gram_left, gram_right):
+    owners, _, row_part, _ = arrived.shape
+    _, rows, size = gram_left.shape
+    state = shape(gram_left.shape, F32)
+    return pl.pallas_call(
+        gram_kernel,
+        in_specs=[SMEM] + [ANY] * 3,
+        out_specs=(ANY,) * 2,
+        scratch_shapes=[
+            pltpu.VMEM((owners, row_part, size), BF16),
             pltpu.VMEM((rows, size), F32),
             pltpu.VMEM((rows, size), F32),
-            pltpu.VMEM((owners, reps, half // 2, 2 * part), BF16),
-            pltpu.SemaphoreType.DMA((2 * REPS + 4,)),
-            pltpu.SemaphoreType.DMA((3 * REPS,)),
-        ],
-        out_shape=(state,) * 2
-        + (shape((owners, reps, half // 2, 2 * part + LANES), BF16), shape((2, 8, part), F32)),
-        compiler_params=params(MID_LIMIT),
+            pltpu.SemaphoreType.DMA((REPS + 2,)),
+            pltpu.SemaphoreType.DMA((2,)),
+        ],
+        out_shape=(state,) * 2,
+        compiler_params=params(BIG_LIMIT),
         cost_estimate=MID_COST,
-        name="own_slot",
-    )(at, arrived, *left_parts, root_right, moment, second)
+        name="own_grams",
+    )(at, arrived, gram_left, gram_right)
 
 
 def late_kernel(
-    at_ref, grad_hbm, mom_ref, sec_ref, sum_ref, _, __, ___, mom_out, sec_out, pieces, grad_ref, mom, sec, pads, sems, out_sems
+    at_ref, grad_hbm, mom_ref, sec_ref, own_ref, pre_ref, _, __, ___, mom_out, sec_out, pieces, grad_ref, mom, sec, pads, sems, out_sems
 ):
     k = 1 - at_ref[1]
     count, reps, row_part, part = grad_ref.shape
@@ -347,9 +368,9 @@
             copy = pltpu.make_async_copy(src.at[n], block(dst, n), out_sems.at[2 * n + i])
             copy.start()
             stores.append(copy)
-    own, other = jnp.sum(sum_ref[0]), jnp.sum(total)
+    own, other = jnp.sum(own_ref[...]), jnp.sum(total)
     even = at_ref[1] == 0
-    values = (jnp.where(even, own, other), jnp.where(even, other, own), jnp.sum(sum_ref[1]))
+    values = (jnp.where(even, own, other), jnp.where(even, other, own), jnp.sum(pre_ref[...]))
     tile = pads.shape[2:]
     row = lax.broadcasted_iota(jnp.int32, tile, 0)
     pad = jnp.zeros(tile, F32)
@@ -366,12 +387,12 @@
         store.wait()
 
 
-def late(at, grad, moment, second, sums, moment_new, second_new, pieces, steps=4):
+def late(at, grad, moment, second, own_sq, pre_sq, moment_new, second_new, pieces, steps=4):
     _, rows, size = moment.shape
     state = shape(moment.shape, F32)
     return pl.pallas_call(
         late_kernel,
-        in_specs=[SMEM, ANY, ANY, ANY, VMEM, ANY, ANY, ANY],
+        in_specs=[SMEM, ANY, ANY, ANY, VMEM, VMEM, ANY, ANY, ANY],
         out_specs=(ANY,) * 3,
         scratch_shapes=[
             pltpu.VMEM(grad.shape, BF16),
@@ -382,49 +403,45 @@
             pltpu.SemaphoreType.DMA((2 * steps + 1,)),
         ],
         out_shape=(state, state, shape(pieces.shape, BF16)),
-        input_output_aliases={5: 0, 6: 1, 7: 2},
+        input_output_aliases={6: 0, 7: 1, 8: 2},
         compiler_params=params(LATE_LIMIT),
         cost_estimate=cost(15 * rows * size, 20 * rows * size),
         name="other_adam",
-    )(at, grad, moment, second, sums, moment_new, second_new, pieces)
-
-
-def add_kernel(at_ref, term_ref, stat_ref, _, new_ref, term, stat, sems, out_sems):
+    )(at, grad, moment, second, own_sq, pre_sq, moment_new, second_new, pieces)
+
+
+def add_kernel(at_ref, terms_ref, right_ref, left_ref, _, __, right_out, left_out, terms, stat, sems, out_sems):
     k = 1 - at_ref[1]
-    steps = stat.shape[0]
-    rows = stat.shape[1]
-    gets = [
-        (load(stat_ref.at[k, pl.ds(n * rows, rows)], stat.at[n], sems.at[n]), load(term_ref.at[pl.ds(n * rows, rows)], term.at[n], sems.at[steps + n]))
-        for n in range(steps)
-    ]
+    gets = [load(ref.at[k], stat.at[i], sems.at[i]) for i, ref in enumerate((right_ref, left_ref))]
+    load(terms_ref, terms, sems.at[2]).wait()
     puts = []
-    for n in range(steps):
-        for copy in gets[n]:
-            copy.wait()
-        stat[n] = 0.95 * stat[n] + term[n].astype(F32)
-        puts.append(load(stat.at[n], new_ref.at[k, pl.ds(n * rows, rows)], out_sems.at[n]))
+    for i, ref in enumerate((right_out, left_out)):
+        gets[i].wait()
+        stat[i] = 0.95 * stat[i] + terms[i].astype(F32)
+        puts.append(load(stat.at[i], ref.at[k], out_sems.at[i]))
     for copy in puts:
         copy.wait()
 
 
-def add(at, term, stat, new, estimate, steps=4):
-    _, rows, size = stat.shape
+def add(at, terms, gram_right, gram_left, right_new, left_new):
+    _, rows, size = gram_left.shape
+    state = shape(gram_left.shape, F32)
     return pl.pallas_call(
         add_kernel,
-        in_specs=[SMEM, ANY, ANY, ANY],
-        out_specs=ANY,
-        out_shape=shape(stat.shape, F32),
-        scratch_shapes=[
-            pltpu.VMEM((steps, rows // steps, size), BF16),
-            pltpu.VMEM((steps, rows // steps, size), F32),
-            pltpu.SemaphoreType.DMA((2 * steps,)),
-            pltpu.SemaphoreType.DMA((steps,)),
-        ],
-        input_output_aliases={3: 0},
+        in_specs=[SMEM] + [ANY] * 5,
+        out_specs=(ANY, ANY),
+        out_shape=(state, state),
+        scratch_shapes=[
+            pltpu.VMEM((2, rows, size), BF16),
+            pltpu.VMEM((2, rows, size), F32),
+            pltpu.SemaphoreType.DMA((3,)),
+            pltpu.SemaphoreType.DMA((2,)),
+        ],
+        input_output_aliases={4: 0, 5: 1},
         compiler_params=params(BIG_LIMIT),
-        cost_estimate=estimate,
-        name="add_term",
-    )(at, term, stat, new)
+        cost_estimate=GRAM_COST,
+        name="add_terms",
+    )(at, terms, gram_right, gram_left, right_new, left_new)
 
 
 def finish_kernel(cells, slot_ref, in_ref, out_hbm, ratios, out_ref, sems):
@@ -492,21 +509,17 @@
 
     count = rows // row_part
     other = to_neighbour(lax.dynamic_slice_in_dim(arrived, at[2] * count, count, 0))
-    left_new, right_new, left_term, right_term = grams(at, arrived, gram_left, gram_right)
-    arrived, left_term, right_term = lax.optimization_barrier((arrived, left_term, right_term))
-    right_term = to_neighbour(right_term)
-    left_term = to_neighbour(left_term)
-    moment_new, second_new, pieces, sums = mid(
-        at, arrived, (keep, ahead, across, back), root_right, moment, second
+    terms, moment_new, second_new, own_sq = near_terms(at, arrived, moment, second)
+    arrived, terms = lax.optimization_barrier((arrived, terms))
+    terms = to_neighbour(terms)
+    pieces, pre_sq = precond(at, arrived, (keep, ahead, across, back), root_right)
+    moment_new, second_new, pieces = late(
+        at, other, moment, second, own_sq, pre_sq, moment_new, second_new, pieces
     )
-    moment_new, second_new, pieces = late(
-        at, other, moment, second, sums, moment_new, second_new, pieces
-    )
-    pieces, right_term = lax.optimization_barrier((pieces, right_term))
+    arrived, pieces = lax.optimization_barrier((arrived, pieces))
     homed = everyone(pieces.reshape((-1,) + pieces.shape[2:]))
-    right_new = add(at, right_term, gram_right, right_new, MID_COST)
-    right_new, left_new = lax.optimization_barrier((right_new, left_new))
-    left_new = add(at, left_term, gram_left, left_new, GRAM_COST)
+    left_new, right_new = grams(at, arrived, gram_left, gram_right)
+    right_new, left_new = add(at, terms, gram_right, gram_left, right_new, left_new)
     updates = finish(owner_slot, homed, size)
     return (updates, left_new, right_new, moment_new, second_new)
 

time: 99.9 us -> 93.5 us (0.936)
  waiting for transfers between devices: 40.5 us -> 37.1 us
  local copies, waits for them, and re-layouts: 2.85 us -> 0.07 us
  Pallas kernels: 31.5 us -> 29.9 us
  starting transfers between devices: 23.1 us -> 24.6 us
    all_to_all x2, waiting for transfers between devices: 40.5 us -> 36.8 us  [everyone(): lax.all_to_all(x, ('fsdp', 'rep'), split_axis=0, concat_axis=0, tiled=True)]
    unnamed x14 -> x12, local copies, waits for them, and re-layouts: 2.81 us -> 0.03 us
    all_to_all x2, starting transfers between devices: 18 us -> 20.7 us  [everyone(): lax.all_to_all(x, ('fsdp', 'rep'), split_axis=0, concat_axis=0, tiled=True)]
    pallas_call x1, Pallas kernels: 6.34 us -> 5.21 us  [grams(): pl.pallas_call(gram_kernel, in_specs=[SMEM] + [ANY] * 3, out_specs=(ANY,)...]
    ppermute x6 -> x5, starting transfers between devices: 5.04 us -> 3.99 us  [to_neighbour(): return lax.ppermute(x, ('fsdp', 'rep'), pairs)]
  transfers between devices with their start and end apart: 8 -> 7, of which waited for: 2 -> 3; matrix products, arithmetic and copies ran while one was open for 1% -> 1% of each run, Pallas kernels for 26% -> 26%
where the time goes in v5:
time: 93.5 us; the launch traced here: 93.1 us
  waiting for transfers between devices  37.1 us (40%)
  Pallas kernels  29.9 us (32%)
  starting transfers between devices  24.6 us (26%)
    all_to_all x2, waiting for transfers between devices, everyone(): lax.all_to_all(x, ('fsdp', 'rep'), split_axis=0, concat_axis=0, tiled=True)  36.8 us
    all_to_all x2, starting transfers between devices, everyone(): lax.all_to_all(x, ('fsdp', 'rep'), split_axis=0, concat_axis=0, tiled=True)  20.7 us
    pallas_call x1, Pallas kernels, grams(): pl.pallas_call(gram_kernel, in_specs=[SMEM] + [ANY] * 3, out_specs=(ANY,)...  5.21 us
    pallas_call x1, Pallas kernels, near_terms(): pl.pallas_call(near_kernel, in_specs=[SMEM, VMEM, ANY, ANY], out_specs=(A...  4.88 us
    pallas_call x1, Pallas kernels, precond(): pl.pallas_call(precond_kernel, in_specs=[SMEM, VMEM] + [ANY] * 5, out_spe...  4.72 us
    pallas_call x1, Pallas kernels, add(): pl.pallas_call(add_kernel, in_specs=[SMEM] + [ANY] * 5, out_specs=(ANY, A...  4.12 us
    ppermute x5, starting transfers between devices, to_neighbour(): return lax.ppermute(x, ('fsdp', 'rep'), pairs)  3.99 us
    pallas_call x1, Pallas kernels, deal(): pl.pallas_call(deal_kernel, out_shape=shape((2 * blocks, row_part, part),...  3.27 us
  transfers between devices with their start and end apart: 7, of which 3 were waited for; matrix products, arithmetic and copies ran while one was open for 1% of the time, Pallas kernels for 26%

profile of v5, /device:TPU:1, one launch (start us, length us, event | category | flops | bytes accessed | tf_op | source)
XLA Modules:
  0.0 93.1 jit_solution(18281908844478438501)
XLA Ops:
  0.6 3.3 %deal_blocks.1 = bf16[128,32,256]{2,1,0:T(8,128)(2,1)} custom-call(s32[64]{0:T(128)} %slot_ref.3, bf16[64,32,256]{2,1,0:T(8,128)(2,1)} %grads_ref.1), custom_call_target="tpu_custom_call" | custom-call | bytes 3145728 | tf_op jit(solution)/shard_map/deal_blocks/pallas_call | solution.py:109
  3.9 11.5 %all-to-all-start = ((bf16[128,32,256]{2,1,0:T(8,128)(2,1)}), bf16[128,32,256]{2,1,0:T(8,128)(2,1)S(1)}, u32[]{:S(2)}, u32[]{:S(2)}) async-start(bf16[128,32,256]{2,1,0:T(8,128)(2,1)} %deal_blocks.1), calls=%async_computation | async-start | bytes 4194304 | tf_op jit(solution)/shard_map/all_to_all | solution.py:66
  15.4 0.6 pad_add_fusion.at_ref
  16.0 3.0 %share_rows.1 = (bf16[8,16,1024]{2,1,0:T(8,128)(2,1)}, bf16[8,16,1024]{2,1,0:T(8,128)(2,1)}, bf16[8,16,1024]{2,1,0:T(8,128)(2,1)}, bf16[8,16,1024]{2,1,0:T(8,128)(2,1)}) custom-call(s32[4]{0:T(128)} %pad_add_fusion.at_ref, bf16[2,8,2,16,1024]{4,3,2,1,0:T(8,128)(2,1)} %bitcast.11), custom_call_target="tpu_custom_call" | custom-call | bytes 2097152 | tf_op jit(solution)/shard_map/share_rows/pallas_call | solution.py:140
  19.1 2.7 %collective-permute-start.1 = (bf16[8,16,1024]{2,1,0:T(8,128)(2,1)}, bf16[8,16,1024]{2,1,0:T(8,128)(2,1)S(1)}, u32[]{:S(2)}, u32[]{:S(2)}) collective-permute-start(bf16[8,16,1024]{2,1,0:T(8,128)(2,1)} %get-tuple-element.30), channel_id=1, source_target_pairs={{0,1},{1,2},{2,3},{3,0},{4,7},{5,4},{6,5},{7,6},{8,9},{9,10},{10,1... | collective-permute-start | bytes 786440 | tf_op jit(solution)/shard_map/ppermute | solution.py:62
  21.8 0.5 collective-permute-start.2
  22.3 0.6 collective-permute-start.3
  22.9 23.6 %all-to-all-done = bf16[128,32,256]{2,1,0:T(8,128)(2,1)S(1)} async-done(((bf16[128,32,256]{2,1,0:T(8,128)(2,1)}), bf16[128,32,256]{2,1,0:T(8,128)(2,1)S(1)}, u32[]{:S(2)}, u32[]{:S(2)}) %all-to-all-start) | async-done | bytes 2097184 | tf_op jit(solution)/shard_map/all_to_all | solution.py:66
  46.6 0.0 copy-start.5
  46.6 0.1 collective-permute-start
  46.7 0.0 copy-done.3
  46.7 4.9 %near_terms.1 = (bf16[2,256,1024]{2,1,0:T(8,128)(2,1)}, f32[2,256,1024]{2,1,0:T(8,128)}, f32[2,256,1024]{2,1,0:T(8,128)}, f32[8,256]{1,0:T(8,128)S(1)}) custom-call(s32[4]{0:T(128)S(1)} %copy-done.3, bf16[32,4,32,256]{3,2,1,0:T(8,128)(2,1)S(1)} %bitcast.8, f32[2,256,1024]{2,1,0:T(8,128)} %mom_ref.3, f32[2,256,1024]{2,1,0:T(8,128)} %sec_ref.3), custom_call_target="tpu_custom_call" | custom-call | flops 1 | bytes 1 | tf_op jit(solution)/shard_map/near_terms/pallas_call | solution.py:204
  51.6 0.1 collective-permute-start.4
  51.6 0.0 collective-permute-done.1.l1_ref
  51.6 0.0 collective-permute-done.2.l2_ref
  51.7 0.0 collective-permute-done.3.l3_ref
  51.7 0.0 copy-done
  51.7 0.0 copy-done.5
  51.7 0.0 copy-start.1
  51.7 0.0 copy-start.2
  51.7 4.7 %precond_rows.1 = (bf16[32,4,8,640]{3,2,1,0:T(8,128)(2,1)}, f32[8,256]{1,0:T(8,128)S(1)}) custom-call(s32[4]{0:T(128)S(1)} %copy-done.3, bf16[32,4,32,256]{3,2,1,0:T(8,128)(2,1)S(1)} %bitcast.9, bf16[8,16,1024]{2,1,0:T(8,128)(2,1)S(1)} %copy-done.5, bf16[8,16,1024]{2,1,0:T(8,128)(2,1)S(1)} %collective-permute-done.1.l1_ref, ...), custom_call_target="tpu_custom_call" | custom-call | flops 99999997952 | bytes 1000000 | tf_op jit(solution)/shard_map/precond_rows/pallas_call | solution.py:265
  56.4 0.3 collective-permute-done.grad_hbm
  56.7 0.0 copy-done.1
  56.7 0.0 copy-done.2
  56.7 2.5 %other_adam.1 = (f32[2,256,1024]{2,1,0:T(8,128)}, f32[2,256,1024]{2,1,0:T(8,128)}, bf16[32,4,8,640]{3,2,1,0:T(8,128)(2,1)}) custom-call(s32[4]{0:T(128)S(1)} %copy-done.3, bf16[8,4,32,256]{3,2,1,0:T(8,128)(2,1)S(1)} %collective-permute-done.grad_hbm, f32[2,256,1024]{2,1,0:T(8,128)S(1)} %copy-done.1, ...), custom_call_target="tpu_custom_call", output_to_operand_aliasing={{0}: (6, {}), {1}: (7, {}), {2}: (8, {})} | custom-call | flops 3932160 | bytes 5242880 | tf_op jit(solution)/shard_map/other_adam/pallas_call | solution.py:393
  59.2 9.2 %all-to-all-start.1 = ((bf16[128,8,640]{2,1,0:T(8,128)(2,1)}), bf16[128,8,640]{2,1,0:T(8,128)(2,1)S(1)}, u32[]{:S(2)}, u32[]{:S(2)}) async-start(bf16[128,8,640]{2,1,0:T(8,128)(2,1)} %bitcast.6), calls=%async_computation.1 | async-start | bytes 2621440 | tf_op jit(solution)/shard_map/all_to_all | solution.py:66
  68.4 5.2 %own_grams.1 = (f32[2,256,1024]{2,1,0:T(8,128)}, f32[2,256,1024]{2,1,0:T(8,128)}) custom-call(s32[4]{0:T(128)} %pad_add_fusion.at_ref, bf16[32,4,32,256]{3,2,1,0:T(8,128)(2,1)} %bitcast.10, f32[2,256,1024]{2,1,0:T(8,128)} %left_ref.1, f32[2,256,1024]{2,1,0:T(8,128)} %right_ref.3), custom_call_target="tpu_custom_call" | custom-call | flops 99999997952 | bytes 1000000 | tf_op jit(solution)/shard_map/own_grams/pallas_call | solution.py:314
  73.6 0.0 collective-permute-done.4.terms_ref
  73.6 0.0 copy-start.4
  73.6 4.1 %add_terms.1 = (f32[2,256,1024]{2,1,0:T(8,128)}, f32[2,256,1024]{2,1,0:T(8,128)}) custom-call(s32[4]{0:T(128)} %pad_add_fusion.at_ref, bf16[2,256,1024]{2,1,0:T(8,128)(2,1)} %collective-permute-done.4.terms_ref, f32[2,256,1024]{2,1,0:T(8,128)} %right_ref.3, f32[2,256,1024]{2,1,0:T(8,128)} %left_ref.1, ...), custom_call_target="tpu_custom_call", output_to_operand_aliasing={{0}: (4, {}), {1}: (5, {})} | custom-call | flops 1 | bytes 1 | tf_op jit(solution)/shard_map/add_terms/pallas_call | solution.py:429
  77.8 13.2 %all-to-all-done.1.in_ref = bf16[128,8,640]{2,1,0:T(8,128)(2,1)S(1)} async-done(((bf16[128,8,640]{2,1,0:T(8,128)(2,1)}), bf16[128,8,640]{2,1,0:T(8,128)(2,1)S(1)}, u32[]{:S(2)}, u32[]{:S(2)}) %all-to-all-start.1) | async-done | bytes 1310752 | tf_op jit(solution)/shard_map/all_to_all | solution.py:66
  91.0 2.1 %finish_updates.1 = bf16[64,32,256]{2,1,0:T(8,128)(2,1)} custom-call(s32[64]{0:T(128)S(1)} %copy-done.4, bf16[128,8,640]{2,1,0:T(8,128)(2,1)S(1)} %all-to-all-done.1.in_ref), custom_call_target="tpu_custom_call" | custom-call | flops 1048576 | bytes 2621440 | tf_op jit(solution)/shard_map/finish_updates/pallas_call | solution.py:483
  (4 shorter events, 0.0 us)
Async XLA Ops:
  3.9 42.6 %all-to-all-start = ((bf16[128,32,256]{2,1,0:T(8,128)(2,1)}), bf16[128,32,256]{2,1,0:T(8,128)(2,1)S(1)}, u32[]{:S(2)}, u32[]{:S(2)}) async-start(bf16[128,32,256]{2,1,0:T(8,128)(2,1)} %deal_blocks.1), calls=%async_computation | async-start | bytes 4194304 | tf_op jit(solution)/shard_map/all_to_all | solution.py:66
  16.0 30.6 %copy-start.3 = (s32[4]{0:T(128)S(1)}, s32[4]{0:T(128)}, u32[]{:S(2)}) copy-start(s32[4]{0:T(128)} %pad_add_fusion.at_ref) | copy-start | bytes 52
  19.1 32.6 %collective-permute-start.1 = (bf16[8,16,1024]{2,1,0:T(8,128)(2,1)}, bf16[8,16,1024]{2,1,0:T(8,128)(2,1)S(1)}, u32[]{:S(2)}, u32[]{:S(2)}) collective-permute-start(bf16[8,16,1024]{2,1,0:T(8,128)(2,1)} %get-tuple-element.30), channel_id=1, source_target_pairs={{0,1},{1,2},{2,3},{3,0},{4,7},{5,4},{6,5},{7,6},{8,9},{9,10},{10,1... | collective-permute-start | bytes 786440 | tf_op jit(solution)/shard_map/ppermute | solution.py:62
  21.8 29.9 %collective-permute-start.2 = (bf16[8,16,1024]{2,1,0:T(8,128)(2,1)}, bf16[8,16,1024]{2,1,0:T(8,128)(2,1)S(1)}, u32[]{:S(2)}, u32[]{:S(2)}) collective-permute-start(bf16[8,16,1024]{2,1,0:T(8,128)(2,1)} %get-tuple-element.31), channel_id=1, source_target_pairs={{0,2},{1,3},{2,0},{3,1},{4,6},{5,7},{6,4},{7,5},{8,10},{9,11},{10,... | collective-permute-start | bytes 786440 | tf_op jit(solution)/shard_map/ppermute | solution.py:62
  22.3 29.4 %collective-permute-start.3 = (bf16[8,16,1024]{2,1,0:T(8,128)(2,1)}, bf16[8,16,1024]{2,1,0:T(8,128)(2,1)S(1)}, u32[]{:S(2)}, u32[]{:S(2)}) collective-permute-start(bf16[8,16,1024]{2,1,0:T(8,128)(2,1)} %get-tuple-element.32), channel_id=1, source_target_pairs={{0,3},{1,0},{2,1},{3,2},{4,5},{5,6},{6,7},{7,4},{8,11},{9,8},{10,9... | collective-permute-start | bytes 786440 | tf_op jit(solution)/shard_map/ppermute | solution.py:62
  46.5 5.2 %copy-start = (bf16[128,32,256]{2,1,0:T(8,128)(2,1)}, bf16[128,32,256]{2,1,0:T(8,128)(2,1)S(1)}, u32[]{:S(2)}) copy-start(bf16[128,32,256]{2,1,0:T(8,128)(2,1)S(1)} %all-to-all-done) | copy-start | bytes 6291460
  46.6 5.1 %copy-start.5 = (bf16[8,16,1024]{2,1,0:T(8,128)(2,1)S(1)}, bf16[8,16,1024]{2,1,0:T(8,128)(2,1)}, u32[]{:S(2)}) copy-start(bf16[8,16,1024]{2,1,0:T(8,128)(2,1)} %get-tuple-element.29.l0_ref) | copy-start | bytes 786436
  46.6 10.1 %collective-permute-start = (bf16[8,4,32,256]{3,2,1,0:T(8,128)(2,1)S(1)}, bf16[8,4,32,256]{3,2,1,0:T(8,128)(2,1)S(1)}, u32[]{:S(2)}, u32[]{:S(2)}) collective-permute-start(bf16[8,4,32,256]{3,2,1,0:T(8,128)(2,1)S(1)} %constant_dynamic-slice_fusion), channel_id=1, source_target_pairs={{0,1},{1,2},{2,3},{3,0},{4,7},{5,4},{6,5},{7,6},{8,9},{9,10},{10,1... | collective-permute-start | bytes 1572872 | tf_op jit(solution)/shard_map/ppermute | solution.py:62
  51.6 22.1 %collective-permute-start.4 = (bf16[2,256,1024]{2,1,0:T(8,128)(2,1)}, bf16[2,256,1024]{2,1,0:T(8,128)(2,1)}, u32[]{:S(2)}, u32[]{:S(2)}) collective-permute-start(bf16[2,256,1024]{2,1,0:T(8,128)(2,1)} %get-tuple-element.39), channel_id=1, source_target_pairs={{0,1},{1,2},{2,3},{3,0},{4,7},{5,4},{6,5},{7,6},{8,9},{9,10},{10,1... | collective-permute-start | bytes 3145736 | tf_op jit(solution)/shard_map/ppermute | solution.py:62
  51.7 5.0 %copy-start.1 = (f32[2,256,1024]{2,1,0:T(8,128)S(1)}, f32[2,256,1024]{2,1,0:T(8,128)}, u32[]{:S(2)}) copy-start(f32[2,256,1024]{2,1,0:T(8,128)} %mom_ref.3) | copy-start | bytes 6291460
  51.7 5.0 %copy-start.2 = (f32[2,256,1024]{2,1,0:T(8,128)S(1)}, f32[2,256,1024]{2,1,0:T(8,128)}, u32[]{:S(2)}) copy-start(f32[2,256,1024]{2,1,0:T(8,128)} %sec_ref.3) | copy-start | bytes 6291460
  59.2 31.7 %all-to-all-start.1 = ((bf16[128,8,640]{2,1,0:T(8,128)(2,1)}), bf16[128,8,640]{2,1,0:T(8,128)(2,1)S(1)}, u32[]{:S(2)}, u32[]{:S(2)}) async-start(bf16[128,8,640]{2,1,0:T(8,128)(2,1)} %bitcast.6), calls=%async_computation.1 | async-start | bytes 2621440 | tf_op jit(solution)/shard_map/all_to_all | solution.py:66
  73.6 17.3 %copy-start.4 = (s32[64]{0:T(128)S(1)}, s32[64]{0:T(128)}, u32[]{:S(2)}) copy-start(s32[64]{0:T(128)} %slot_ref.3) | copy-start | bytes 772

commit v6 on v5

--- a/solution.py
+++ b/solution.py
@@ -48,9 +48,8 @@
 
 def place():
     rep = lax.axis_index("rep").astype(jnp.int32)
-    core = lax.rem(lax.axis_index("fsdp").astype(jnp.int32), 2)
-    step = 1 - 2 * core
-    return jnp.stack([rep, lax.rem(rep, 2), lax.rem(rep + step + REPS, REPS), step])
+    step = 1 - 2 * lax.rem(lax.axis_index("fsdp").astype(jnp.int32), 2)
+    return rep, lax.rem(rep, 2), lax.rem(rep + step + REPS, REPS), step
 
 
 def to_neighbour(x, far=1):
@@ -72,10 +71,11 @@
     return copy
 
 
-def deal_kernel(slot_ref, grads_ref, out_ref, grads, out, block_of, sems):
+def deal_kernel(slot_hbm, grads_ref, out_ref, grads, out, slot_ref, block_of, sems):
     blocks = grads.shape[0]
     chunk = blocks // DEALS
     gets, puts = [], []
+    get_slots = load(slot_hbm, slot_ref, sems.at[2 * DEALS])
     for n in range(DEALS):
         part_of = pl.ds(n * chunk, chunk)
         gets.append(load(grads_ref.at[part_of], grads.at[part_of], sems.at[n]))
@@ -84,6 +84,7 @@
         block_of[slot_ref[b]] = b
         return 0
 
+    get_slots.wait()
     lax.fori_loop(0, blocks, note, 0, unroll=8)
     for copy in gets:
         copy.wait()
@@ -109,13 +110,14 @@
     return pl.pallas_call(
         deal_kernel,
         out_shape=shape((2 * blocks, row_part, part), BF16),
-        in_specs=[SMEM, ANY],
+        in_specs=[ANY, ANY],
         out_specs=ANY,
         scratch_shapes=[
             pltpu.VMEM(grads.shape, BF16),
             pltpu.VMEM((2 * blocks, row_part, part), BF16),
             pltpu.SMEM((blocks,), jnp.int32),
-            pltpu.SemaphoreType.DMA((2 * DEALS,)),
+            pltpu.SMEM((blocks,), jnp.int32),
+            pltpu.SemaphoreType.DMA((2 * DEALS + 1,)),
         ],
         compiler_params=params(BIG_LIMIT),
         cost_estimate=cost(0, 6 * grads.size),
@@ -123,37 +125,45 @@
     )(owner_slot, grads)
 
 
-def share_kernel(at_ref, left_ref, keep_ref, ahead_ref, across_ref, back_ref, left, sems):
-    get = load(left_ref, left, sems.at[0])
-    get.wait()
-    puts = []
-    for j, ref in ((1, ahead_ref), (2, across_ref), (-1, back_ref), (0, keep_ref)):
-        to = lax.rem(at_ref[0] + j * at_ref[3] + REPS, REPS)
-        puts.append(load(left.at[lax.rem(to, 2), :, to // 2], ref, sems.at[1 + len(puts)]))
+def share_kernel(left_ref, ahead_ref, across_ref, back_ref, left, sems, out_sems):
+    here = place()
+    outs = ((1, ahead_ref), (2, across_ref), (-1, back_ref))
+    gets, puts = [], []
+    for i, (j, _) in enumerate(outs):
+        to = lax.rem(here[0] + j * here[3] + REPS, REPS)
+        gets.append(load(left_ref.at[lax.rem(to, 2), :, to // 2], left.at[i], sems.at[i]))
+    for i, (_, ref) in enumerate(outs):
+        gets[i].wait()
+        puts.append(load(left.at[i], ref, out_sems.at[i]))
     for copy in puts:
         copy.wait()
 
 
-def share_rows(at, root_left, row_part):
-    _, rows, size = root_left.shape
-    count, half = rows // row_part, row_part // 2
+def share_rows(halves):
+    _, count, _, half, size = halves.shape
+    others = REPS - 1
     return pl.pallas_call(
         share_kernel,
-        out_shape=(shape((count, half, size), BF16),) * REPS,
-        in_specs=[SMEM, ANY],
-        out_specs=(ANY,) * REPS,
-        scratch_shapes=[pltpu.VMEM((2, count, 2, half, size), BF16), pltpu.SemaphoreType.DMA((1 + REPS,))],
+        out_shape=(shape((count, half, size), BF16),) * others,
+        in_specs=[ANY],
+        out_specs=(ANY,) * others,
+        scratch_shapes=[
+            pltpu.VMEM((others, count, half, size), BF16),
+            pltpu.SemaphoreType.DMA((others,)),
+            pltpu.SemaphoreType.DMA((others,)),
+        ],
         compiler_params=params(BIG_LIMIT),
-        cost_estimate=cost(0, 4 * root_left.size),
+        cost_estimate=cost(0, 3 * halves.size),
         name="share_rows",
-    )(at, root_left.reshape(2, count, 2, half, size))
+    )(halves)
 
 
 def near_kernel(
-    at_ref, g_ref, mom_ref, sec_ref, terms_ref, mom_out, sec_out, sum_ref,
+    g_ref, mom_ref, sec_ref, terms_ref, mom_out, sec_out, sum_ref,
     whole, lhs, terms, mom, sec, sems, out_sems,
 ):
-    rep, k, near = at_ref[0], at_ref[1], at_ref[2]
+    here = place()
+    rep, k, near = here[0], here[1], here[2]
     owners, reps, row_part, part = g_ref.shape
     size = owners * row_part
     rows = mom.shape[0]
@@ -197,13 +207,13 @@
         copy.wait()
 
 
-def near_terms(at, arrived, moment, second):
+def near_terms(arrived, moment, second):
     _, reps, _, part = arrived.shape
     _, rows, size = moment.shape
     state = shape(moment.shape, F32)
     return pl.pallas_call(
         near_kernel,
-        in_specs=[SMEM, VMEM, ANY, ANY],
+        in_specs=[VMEM, ANY, ANY],
         out_specs=(ANY,) * 3 + (VMEM,),
         scratch_shapes=[
             pltpu.VMEM((size, size), BF16),
@@ -218,18 +228,19 @@
         compiler_params=params(GRAM_LIMIT),
         cost_estimate=GRAM_COST,
         name="near_terms",
-    )(at, arrived, moment, second)
+    )(arrived, moment, second)
 
 
 def precond_kernel(
-    at_ref, g_ref, l0_ref, l1_ref, l2_ref, l3_ref, right_ref, pieces, sum_ref, left, right, mixed, out, sems, out_sems
+    g_ref, l0_ref, l1_ref, l2_ref, l3_ref, right_ref, pieces, sum_ref, left, right, mixed, out, sems, out_sems
 ):
-    rep, k, step = at_ref[0], at_ref[1], at_ref[3]
+    here = place()
+    rep, k, step = here[0], here[1], here[3]
     owners, reps, row_part, part = g_ref.shape
     size = owners * row_part
-    share = l0_ref.shape[0]
+    share = l1_ref.shape[0]
     get_left = []
-    for j, ref in enumerate((l0_ref, l1_ref, l2_ref, l3_ref)):
+    for j, ref in enumerate((l0_ref.at[k, :, rep // 2], l1_ref, l2_ref, l3_ref)):
         first = lax.rem(rep - j * step + REPS * REPS, REPS) * share
         get_left.append(load(ref, left.at[pl.ds(first, share)], sems.at[j]))
     half = size // 2
@@ -258,13 +269,13 @@
         copy.wait()
 
 
-def precond(at, arrived, left_parts, root_right):
+def precond(arrived, left_parts, root_right):
     owners, reps, row_part, part = arrived.shape
     size = root_right.shape[1]
     half = row_part // 2
     return pl.pallas_call(
         precond_kernel,
-        in_specs=[SMEM, VMEM] + [ANY] * 5,
+        in_specs=[VMEM] + [ANY] * 5,
         out_specs=(ANY, VMEM),
         scratch_shapes=[
             pltpu.VMEM((owners, half, size), BF16),
@@ -278,11 +289,12 @@
         compiler_params=params(MID_LIMIT),
         cost_estimate=MID_COST,
         name="precond_rows",
-    )(at, arrived, *left_parts, root_right)
-
-
-def gram_kernel(at_ref, arrived, stat_left, stat_right, left_out, right_out, whole, gl, gr, sems, out_sems):
-    rep, k = at_ref[0], at_ref[1]
+    )(arrived, *left_parts, root_right)
+
+
+def gram_kernel(arrived, stat_left, stat_right, left_out, right_out, whole, gl, gr, sems, out_sems):
+    here = place()
+    rep, k = here[0], here[1]
     _, row_part, size = whole.shape
     part = size // REPS
     rows = gl.shape[0]
@@ -307,13 +319,13 @@
     put_left.wait()
 
 
-def grams(at, arrived, gram_left, gram_right):
+def grams(arrived, gram_left, gram_right):
     owners, _, row_part, _ = arrived.shape
     _, rows, size = gram_left.shape
     state = shape(gram_left.shape, F32)
     return pl.pallas_call(
         gram_kernel,
-        in_specs=[SMEM] + [ANY] * 3,
+        in_specs=[ANY] * 3,
         out_specs=(ANY,) * 2,
         scratch_shapes=[
             pltpu.VMEM((owners, row_part, size), BF16),
@@ -326,13 +338,14 @@
         compiler_params=params(BIG_LIMIT),
         cost_estimate=MID_COST,
         name="own_grams",
-    )(at, arrived, gram_left, gram_right)
+    )(arrived, gram_left, gram_right)
 
 
 def late_kernel(
-    at_ref, grad_hbm, mom_ref, sec_ref, own_ref, pre_ref, _, __, ___, mom_out, sec_out, pieces, grad_ref, mom, sec, pads, sems, out_sems
+    grad_hbm, mom_ref, sec_ref, own_ref, pre_ref, _, __, ___, mom_out, sec_out, pieces, grad_ref, mom, sec, pads, sems, out_sems
 ):
-    k = 1 - at_ref[1]
+    here = place()
+    k = 1 - here[1]
     count, reps, row_part, part = grad_ref.shape
     rows = count * row_part
     steps = mom.shape[0]
@@ -369,7 +382,7 @@
             copy.start()
             stores.append(copy)
     own, other = jnp.sum(own_ref[...]), jnp.sum(total)
-    even = at_ref[1] == 0
+    even = here[1] == 0
     values = (jnp.where(even, own, other), jnp.where(even, other, own), jnp.sum(pre_ref[...]))
     tile = pads.shape[2:]
     row = lax.broadcasted_iota(jnp.int32, tile, 0)
@@ -387,12 +400,12 @@
         store.wait()
 
 
-def late(at, grad, moment, second, own_sq, pre_sq, moment_new, second_new, pieces, steps=4):
+def late(grad, moment, second, own_sq, pre_sq, moment_new, second_new, pieces, steps=4):
     _, rows, size = moment.shape
     state = shape(moment.shape, F32)
     return pl.pallas_call(
         late_kernel,
-        in_specs=[SMEM, ANY, ANY, ANY, VMEM, VMEM, ANY, ANY, ANY],
+        in_specs=[ANY, ANY, ANY, VMEM, VMEM, ANY, ANY, ANY],
         out_specs=(ANY,) * 3,
         scratch_shapes=[
             pltpu.VMEM(grad.shape, BF16),
@@ -403,15 +416,16 @@
             pltpu.SemaphoreType.DMA((2 * steps + 1,)),
         ],
         out_shape=(state, state, shape(pieces.shape, BF16)),
-        input_output_aliases={6: 0, 7: 1, 8: 2},
+        input_output_aliases={5: 0, 6: 1, 7: 2},
         compiler_params=params(LATE_LIMIT),
         cost_estimate=cost(15 * rows * size, 20 * rows * size),
         name="other_adam",
-    )(at, grad, moment, second, own_sq, pre_sq, moment_new, second_new, pieces)
-
-
-def add_kernel(at_ref, terms_ref, right_ref, left_ref, _, __, right_out, left_out, terms, stat, sems, out_sems):
-    k = 1 - at_ref[1]
+    )(grad, moment, second, own_sq, pre_sq, moment_new, second_new, pieces)
+
+
+def add_kernel(terms_ref, right_ref, left_ref, _, __, right_out, left_out, terms, stat, sems, out_sems):
+    here = place()
+    k = 1 - here[1]
     gets = [load(ref.at[k], stat.at[i], sems.at[i]) for i, ref in enumerate((right_ref, left_ref))]
     load(terms_ref, terms, sems.at[2]).wait()
     puts = []
@@ -423,12 +437,12 @@
         copy.wait()
 
 
-def add(at, terms, gram_right, gram_left, right_new, left_new):
+def add(terms, gram_right, gram_left, right_new, left_new):
     _, rows, size = gram_left.shape
     state = shape(gram_left.shape, F32)
     return pl.pallas_call(
         add_kernel,
-        in_specs=[SMEM] + [ANY] * 5,
+        in_specs=[ANY] * 5,
         out_specs=(ANY, ANY),
         out_shape=(state, state),
         scratch_shapes=[
@@ -437,11 +451,11 @@
             pltpu.SemaphoreType.DMA((3,)),
             pltpu.SemaphoreType.DMA((2,)),
         ],
-        input_output_aliases={4: 0, 5: 1},
+        input_output_aliases={3: 0, 4: 1},
         compiler_params=params(BIG_LIMIT),
         cost_estimate=GRAM_COST,
         name="add_terms",
-    )(at, terms, gram_right, gram_left, right_new, left_new)
+    )(terms, gram_right, gram_left, right_new, left_new)
 
 
 def finish_kernel(cells, slot_ref, in_ref, out_hbm, ratios, out_ref, sems):
@@ -469,7 +483,7 @@
     chunk = out_ref.shape[0] // DEALS
     puts = []
     for n in range(DEALS):
-        lax.fori_loop(n * chunk, (n + 1) * chunk, place_block, 0, unroll=8)
+        lax.fori_loop(n * chunk, (n + 1) * chunk, place_block, 0, unroll=16)
         part_of = pl.ds(n * chunk, chunk)
         puts.append(load(out_ref.at[part_of], out_hbm.at[part_of], sems.at[n]))
     for copy in puts:
@@ -499,27 +513,28 @@
 def per_device(grads, owner_slot, gram_left, gram_right, root_left, root_right, moment, second):
     blocks, row_part, part = grads.shape
     _, rows, size = root_left.shape
-    at = place()
+    near = place()[2]
     sent = deal(owner_slot, grads)
-    keep, ahead, across, back = share_rows(at, root_left, row_part)
+    halves = root_left.reshape(2, rows // row_part, 2, row_part // 2, size)
+    ahead, across, back = share_rows(halves)
     arrived = everyone(sent).reshape(OWNERS, REPS, row_part, part)
     ahead = to_neighbour(ahead)
     across = to_neighbour(across, 2)
     back = to_neighbour(back, -1)
 
     count = rows // row_part
-    other = to_neighbour(lax.dynamic_slice_in_dim(arrived, at[2] * count, count, 0))
-    terms, moment_new, second_new, own_sq = near_terms(at, arrived, moment, second)
+    other = to_neighbour(lax.dynamic_slice_in_dim(arrived, near * count, count, 0))
+    terms, moment_new, second_new, own_sq = near_terms(arrived, moment, second)
     arrived, terms = lax.optimization_barrier((arrived, terms))
     terms = to_neighbour(terms)
-    pieces, pre_sq = precond(at, arrived, (keep, ahead, across, back), root_right)
+    pieces, pre_sq = precond(arrived, (halves, ahead, across, back), root_right)
     moment_new, second_new, pieces = late(
-        at, other, moment, second, own_sq, pre_sq, moment_new, second_new, pieces
+        other, moment, second, own_sq, pre_sq, moment_new, second_new, pieces
     )
     arrived, pieces = lax.optimization_barrier((arrived, pieces))
     homed = everyone(pieces.reshape((-1,) + pieces.shape[2:]))
-    left_new, right_new = grams(at, arrived, gram_left, gram_right)
-    right_new, left_new = add(at, terms, gram_right, gram_left, right_new, left_new)
+    left_new, right_new = grams(arrived, gram_left, gram_right)
+    right_new, left_new = add(terms, gram_right, gram_left, right_new, left_new)
     updates = finish(owner_slot, homed, size)
     return (updates, left_new, right_new, moment_new, second_new)
 

time: 93.5 us -> 92.2 us (0.986)
  Pallas kernels: 29.9 us -> 24.8 us
  waiting for transfers between devices: 37.1 us -> 41.5 us
    pallas_call x5, Pallas kernels: 21.4 us -> 18.3 us  [the longest x1 4.55 us: grams(): pl.pallas_call(gram_kernel, in_specs=[ANY] * 3, out_specs=(ANY,) * 2, scr...]
    all_to_all x2, waiting for transfers between devices: 36.8 us -> 40 us  [everyone(): lax.all_to_all(x, ('fsdp', 'rep'), split_axis=0, concat_axis=0, tiled=True)]
    ppermute x5, waiting for transfers between devices: 0.29 us -> 1.5 us  [to_neighbour(): return lax.ppermute(x, ('fsdp', 'rep'), pairs)]
    pallas_call x1, Pallas kernels: 3.02 us -> 1.9 us  [share_rows(): pl.pallas_call(share_kernel, out_shape=(shape((count, half, size), BF16),...]
  transfers between devices with their start and end apart: 7 -> 7, of which waited for: 3 -> 3; matrix products, arithmetic and copies ran while one was open for 1% -> 0% of each run, Pallas kernels for 26% -> 22%
where the time goes in v6:
time: 92.2 us; the launch traced here: 91.8 us
  waiting for transfers between devices  41.5 us (45%)
  Pallas kernels  24.8 us (27%)
  starting transfers between devices  24.6 us (27%)
    all_to_all x2, waiting for transfers between devices, everyone(): lax.all_to_all(x, ('fsdp', 'rep'), split_axis=0, concat_axis=0, tiled=True)  40 us
    all_to_all x2, starting transfers between devices, everyone(): lax.all_to_all(x, ('fsdp', 'rep'), split_axis=0, concat_axis=0, tiled=True)  20.7 us
    pallas_call x1, Pallas kernels, grams(): pl.pallas_call(gram_kernel, in_specs=[ANY] * 3, out_specs=(ANY,) * 2, scr...  4.55 us
    pallas_call x1, Pallas kernels, near_terms(): pl.pallas_call(near_kernel, in_specs=[VMEM, ANY, ANY], out_specs=(ANY,) *...  4.37 us
    pallas_call x1, Pallas kernels, precond(): pl.pallas_call(precond_kernel, in_specs=[VMEM] + [ANY] * 5, out_specs=(AN...  4.01 us
    ppermute x5, starting transfers between devices, to_neighbour(): return lax.ppermute(x, ('fsdp', 'rep'), pairs)  3.98 us
    pallas_call x1, Pallas kernels, add(): pl.pallas_call(add_kernel, in_specs=[ANY] * 5, out_specs=(ANY, ANY), out_...  3.33 us
    pallas_call x1, Pallas kernels, deal(): pl.pallas_call(deal_kernel, out_shape=shape((2 * blocks, row_part, part),...  2.61 us
  transfers between devices with their start and end apart: 7, of which 3 were waited for; matrix products, arithmetic and copies ran while one was open for 0% of the time, Pallas kernels for 22%

profile of v6, /device:TPU:1, one launch (start us, length us, event | category | flops | bytes accessed | tf_op | source)
XLA Modules:
  0.0 91.8 jit_solution(7838123839961891061)
XLA Ops:
  0.6 2.6 %deal_blocks.1 = bf16[128,32,256]{2,1,0:T(8,128)(2,1)} custom-call(s32[64]{0:T(128)} %slot_ref.1, bf16[64,32,256]{2,1,0:T(8,128)(2,1)} %grads_ref.1), custom_call_target="tpu_custom_call" | custom-call | bytes 3145728 | tf_op jit(solution)/shard_map/deal_blocks/pallas_call | solution.py:110
  3.3 11.5 %all-to-all-start = ((bf16[128,32,256]{2,1,0:T(8,128)(2,1)}), bf16[128,32,256]{2,1,0:T(8,128)(2,1)S(1)}, u32[]{:S(2)}, u32[]{:S(2)}) async-start(bf16[128,32,256]{2,1,0:T(8,128)(2,1)} %deal_blocks.1), calls=%async_computation | async-start | bytes 4194304 | tf_op jit(solution)/shard_map/all_to_all | solution.py:65
  14.8 1.9 %share_rows.1 = (bf16[8,16,1024]{2,1,0:T(8,128)(2,1)}, bf16[8,16,1024]{2,1,0:T(8,128)(2,1)}, bf16[8,16,1024]{2,1,0:T(8,128)(2,1)}) custom-call(bf16[2,8,2,16,1024]{4,3,2,1,0:T(8,128)(2,1)} %bitcast.7), custom_call_target="tpu_custom_call" | custom-call | bytes 1572864 | tf_op jit(solution)/shard_map/share_rows/pallas_call | solution.py:145
  16.7 2.7 %collective-permute-start.1 = (bf16[8,16,1024]{2,1,0:T(8,128)(2,1)}, bf16[8,16,1024]{2,1,0:T(8,128)(2,1)S(1)}, u32[]{:S(2)}, u32[]{:S(2)}) collective-permute-start(bf16[8,16,1024]{2,1,0:T(8,128)(2,1)} %get-tuple-element.28), channel_id=1, source_target_pairs={{0,1},{1,2},{2,3},{3,0},{4,7},{5,4},{6,5},{7,6},{8,9},{9,10},{10,1... | collective-permute-start | bytes 786440 | tf_op jit(solution)/shard_map/ppermute | solution.py:61
  19.4 0.5 collective-permute-start.2
  19.9 0.6 collective-permute-start.3
  20.5 25.4 %all-to-all-done = bf16[128,32,256]{2,1,0:T(8,128)(2,1)S(1)} async-done(((bf16[128,32,256]{2,1,0:T(8,128)(2,1)}), bf16[128,32,256]{2,1,0:T(8,128)(2,1)S(1)}, u32[]{:S(2)}, u32[]{:S(2)}) %all-to-all-start) | async-done | bytes 2097184 | tf_op jit(solution)/shard_map/all_to_all | solution.py:65
  45.9 0.0 copy-start
  45.9 0.0 copy-start.3
  45.9 0.1 collective-permute-start
  46.0 4.4 %near_terms.1 = (bf16[2,256,1024]{2,1,0:T(8,128)(2,1)}, f32[2,256,1024]{2,1,0:T(8,128)}, f32[2,256,1024]{2,1,0:T(8,128)}, f32[8,256]{1,0:T(8,128)S(1)}) custom-call(bf16[32,4,32,256]{3,2,1,0:T(8,128)(2,1)S(1)} %bitcast.4, f32[2,256,1024]{2,1,0:T(8,128)} %mom_ref.3, f32[2,256,1024]{2,1,0:T(8,128)} %sec_ref.3), custom_call_target="tpu_custom_call" | custom-call | flops 1 | bytes 1 | tf_op jit(solution)/shard_map/near_terms/pallas_call | solution.py:214
  50.4 0.0 copy-start.1
  50.4 0.0 copy-start.2
  50.4 0.1 collective-permute-start.4
  50.5 0.0 collective-permute-done.1.l1_ref
  50.5 0.0 collective-permute-done.2.l2_ref
  50.5 0.0 collective-permute-done.3.l3_ref
  50.5 0.0 copy-done
  50.5 0.0 copy-done.3
  50.6 4.0 %precond_rows.1 = (bf16[32,4,8,640]{3,2,1,0:T(8,128)(2,1)}, f32[8,256]{1,0:T(8,128)S(1)}) custom-call(bf16[32,4,32,256]{3,2,1,0:T(8,128)(2,1)S(1)} %bitcast.5, bf16[2,8,2,16,1024]{4,3,2,1,0:T(8,128)(2,1)S(1)} %bitcast.8, bf16[8,16,1024]{2,1,0:T(8,128)(2,1)S(1)} %collective-permute-done.1.l1_ref, bf16[8,16,1024]{2,1,0:T(8,128)(2,1)S(1)} %collective-permute-done.2.l2_ref, ...), custom_call_target="tpu_custom_call" | custom-call | flops 99999997952 | bytes 1000000 | tf_op jit(solution)/shard_map/precond_rows/pallas_call | solution.py:276
  54.6 1.5 %collective-permute-done.grad_hbm = bf16[8,4,32,256]{3,2,1,0:T(8,128)(2,1)S(1)} collective-permute-done((bf16[8,4,32,256]{3,2,1,0:T(8,128)(2,1)S(1)}, bf16[8,4,32,256]{3,2,1,0:T(8,128)(2,1)S(1)}, u32[]{:S(2)}, u32[]{:S(2)}) %collective-permute-start) | collective-permute-done | bytes 524320 | tf_op jit(solution)/shard_map/ppermute | solution.py:61
  56.1 0.0 copy-done.1
  56.1 0.0 copy-done.2
  56.1 2.0 %other_adam.1 = (f32[2,256,1024]{2,1,0:T(8,128)}, f32[2,256,1024]{2,1,0:T(8,128)}, bf16[32,4,8,640]{3,2,1,0:T(8,128)(2,1)}) custom-call(bf16[8,4,32,256]{3,2,1,0:T(8,128)(2,1)S(1)} %collective-permute-done.grad_hbm, f32[2,256,1024]{2,1,0:T(8,128)S(1)} %copy-done.1, ...), custom_call_target="tpu_custom_call", output_to_operand_aliasing={{0}: (5, {}), {1}: (6, {}), {2}: (7, {})} | custom-call | flops 3932160 | bytes 5242880 | tf_op jit(solution)/shard_map/other_adam/pallas_call | solution.py:406
  58.1 9.2 %all-to-all-start.1 = ((bf16[128,8,640]{2,1,0:T(8,128)(2,1)}), bf16[128,8,640]{2,1,0:T(8,128)(2,1)S(1)}, u32[]{:S(2)}, u32[]{:S(2)}) async-start(bf16[128,8,640]{2,1,0:T(8,128)(2,1)} %bitcast.2), calls=%async_computation.1 | async-start | bytes 2621440 | tf_op jit(solution)/shard_map/all_to_all | solution.py:65
  67.2 4.5 %own_grams.1 = (f32[2,256,1024]{2,1,0:T(8,128)}, f32[2,256,1024]{2,1,0:T(8,128)}) custom-call(bf16[32,4,32,256]{3,2,1,0:T(8,128)(2,1)} %bitcast.6, f32[2,256,1024]{2,1,0:T(8,128)} %left_ref.1, f32[2,256,1024]{2,1,0:T(8,128)} %right_ref.3), custom_call_target="tpu_custom_call" | custom-call | flops 99999997952 | bytes 1000000 | tf_op jit(solution)/shard_map/own_grams/pallas_call | solution.py:326
  71.8 0.0 collective-permute-done.4.terms_ref
  71.8 0.0 copy-start.4
  71.8 3.3 %add_terms.1 = (f32[2,256,1024]{2,1,0:T(8,128)}, f32[2,256,1024]{2,1,0:T(8,128)}) custom-call(bf16[2,256,1024]{2,1,0:T(8,128)(2,1)} %collective-permute-done.4.terms_ref, f32[2,256,1024]{2,1,0:T(8,128)} %right_ref.3, f32[2,256,1024]{2,1,0:T(8,128)} %left_ref.1, f32[2,256,1024]{2,1,0:T(8,128)} %get-tuple-element.39._, ...), custom_call_target="tpu_custom_call", output_to_operand_aliasing={{0}: (3, {}), {1}: (4, {})} | custom-call | flops 1 | bytes 1 | tf_op jit(solution)/shard_map/add_terms/pallas_call | solution.py:443
  75.1 14.6 %all-to-all-done.1.in_ref = bf16[128,8,640]{2,1,0:T(8,128)(2,1)S(1)} async-done(((bf16[128,8,640]{2,1,0:T(8,128)(2,1)}), bf16[128,8,640]{2,1,0:T(8,128)(2,1)S(1)}, u32[]{:S(2)}, u32[]{:S(2)}) %all-to-all-start.1) | async-done | bytes 1310752 | tf_op jit(solution)/shard_map/all_to_all | solution.py:65
  89.8 0.0 copy-done.4
  89.8 2.0 %finish_updates.1 = bf16[64,32,256]{2,1,0:T(8,128)(2,1)} custom-call(s32[64]{0:T(128)S(1)} %copy-done.4, bf16[128,8,640]{2,1,0:T(8,128)(2,1)S(1)} %all-to-all-done.1.in_ref), custom_call_target="tpu_custom_call" | custom-call | flops 1048576 | bytes 2621440 | tf_op jit(solution)/shard_map/finish_updates/pallas_call | solution.py:497
  (1 shorter events, 0.0 us)
Async XLA Ops:
  3.3 42.6 %all-to-all-start = ((bf16[128,32,256]{2,1,0:T(8,128)(2,1)}), bf16[128,32,256]{2,1,0:T(8,128)(2,1)S(1)}, u32[]{:S(2)}, u32[]{:S(2)}) async-start(bf16[128,32,256]{2,1,0:T(8,128)(2,1)} %deal_blocks.1), calls=%async_computation | async-start | bytes 4194304 | tf_op jit(solution)/shard_map/all_to_all | solution.py:65
  16.7 33.8 %collective-permute-start.1 = (bf16[8,16,1024]{2,1,0:T(8,128)(2,1)}, bf16[8,16,1024]{2,1,0:T(8,128)(2,1)S(1)}, u32[]{:S(2)}, u32[]{:S(2)}) collective-permute-start(bf16[8,16,1024]{2,1,0:T(8,128)(2,1)} %get-tuple-element.28), channel_id=1, source_target_pairs={{0,1},{1,2},{2,3},{3,0},{4,7},{5,4},{6,5},{7,6},{8,9},{9,10},{10,1... | collective-permute-start | bytes 786440 | tf_op jit(solution)/shard_map/ppermute | solution.py:61
  19.4 31.1 %collective-permute-start.2 = (bf16[8,16,1024]{2,1,0:T(8,128)(2,1)}, bf16[8,16,1024]{2,1,0:T(8,128)(2,1)S(1)}, u32[]{:S(2)}, u32[]{:S(2)}) collective-permute-start(bf16[8,16,1024]{2,1,0:T(8,128)(2,1)} %get-tuple-element.29), channel_id=1, source_target_pairs={{0,2},{1,3},{2,0},{3,1},{4,6},{5,7},{6,4},{7,5},{8,10},{9,11},{10,... | collective-permute-start | bytes 786440 | tf_op jit(solution)/shard_map/ppermute | solution.py:61
  19.9 30.6 %collective-permute-start.3 = (bf16[8,16,1024]{2,1,0:T(8,128)(2,1)}, bf16[8,16,1024]{2,1,0:T(8,128)(2,1)S(1)}, u32[]{:S(2)}, u32[]{:S(2)}) collective-permute-start(bf16[8,16,1024]{2,1,0:T(8,128)(2,1)} %get-tuple-element.30), channel_id=1, source_target_pairs={{0,3},{1,0},{2,1},{3,2},{4,5},{5,6},{6,7},{7,4},{8,11},{9,8},{10,9... | collective-permute-start | bytes 786440 | tf_op jit(solution)/shard_map/ppermute | solution.py:61
  45.9 4.7 %copy-start = (bf16[128,32,256]{2,1,0:T(8,128)(2,1)}, bf16[128,32,256]{2,1,0:T(8,128)(2,1)S(1)}, u32[]{:S(2)}) copy-start(bf16[128,32,256]{2,1,0:T(8,128)(2,1)S(1)} %all-to-all-done) | copy-start | bytes 6291460
  45.9 4.6 %copy-start.3 = (bf16[2,256,1024]{2,1,0:T(8,128)(2,1)S(1)}, bf16[2,256,1024]{2,1,0:T(8,128)(2,1)}, u32[]{:S(2)}) copy-start(bf16[2,256,1024]{2,1,0:T(8,128)(2,1)} %param.12) | copy-start | bytes 3145732
  45.9 10.1 %collective-permute-start = (bf16[8,4,32,256]{3,2,1,0:T(8,128)(2,1)S(1)}, bf16[8,4,32,256]{3,2,1,0:T(8,128)(2,1)S(1)}, u32[]{:S(2)}, u32[]{:S(2)}) collective-permute-start(bf16[8,4,32,256]{3,2,1,0:T(8,128)(2,1)S(1)} %constant_dynamic-slice_fusion), channel_id=1, source_target_pairs={{0,1},{1,2},{2,3},{3,0},{4,7},{5,4},{6,5},{7,6},{8,9},{9,10},{10,1... | collective-permute-start | bytes 1572872 | tf_op jit(solution)/shard_map/ppermute | solution.py:61
  50.4 5.7 %copy-start.1 = (f32[2,256,1024]{2,1,0:T(8,128)S(1)}, f32[2,256,1024]{2,1,0:T(8,128)}, u32[]{:S(2)}) copy-start(f32[2,256,1024]{2,1,0:T(8,128)} %mom_ref.3) | copy-start | bytes 6291460
  50.4 5.7 %copy-start.2 = (f32[2,256,1024]{2,1,0:T(8,128)S(1)}, f32[2,256,1024]{2,1,0:T(8,128)}, u32[]{:S(2)}) copy-start(f32[2,256,1024]{2,1,0:T(8,128)} %sec_ref.3) | copy-start | bytes 6291460
  50.4 21.4 %collective-permute-start.4 = (bf16[2,256,1024]{2,1,0:T(8,128)(2,1)}, bf16[2,256,1024]{2,1,0:T(8,128)(2,1)}, u32[]{:S(2)}, u32[]{:S(2)}) collective-permute-start(bf16[2,256,1024]{2,1,0:T(8,128)(2,1)} %get-tuple-element.37), channel_id=1, source_target_pairs={{0,1},{1,2},{2,3},{3,0},{4,7},{5,4},{6,5},{7,6},{8,9},{9,10},{10,1... | collective-permute-start | bytes 3145736 | tf_op jit(solution)/shard_map/ppermute | solution.py:61
  58.1 31.7 %all-to-all-start.1 = ((bf16[128,8,640]{2,1,0:T(8,128)(2,1)}), bf16[128,8,640]{2,1,0:T(8,128)(2,1)S(1)}, u32[]{:S(2)}, u32[]{:S(2)}) async-start(bf16[128,8,640]{2,1,0:T(8,128)(2,1)} %bitcast.2), calls=%async_computation.1 | async-start | bytes 2621440 | tf_op jit(solution)/shard_map/all_to_all | solution.py:65
  71.8 18.0 %copy-start.4 = (s32[64]{0:T(128)S(1)}, s32[64]{0:T(128)}, u32[]{:S(2)}) copy-start(s32[64]{0:T(128)} %slot_ref.1) | copy-start | bytes 772

commit v7 on v6

--- a/solution.py
+++ b/solution.py
@@ -8,7 +8,7 @@
 from jax.sharding import PartitionSpec as P
 
 VMEM_LIMIT = 32 * 1024 * 1024
-GRAM_LIMIT = 50 * 1024 * 1024
+GRAM_LIMIT = 46 * 1024 * 1024
 MID_LIMIT = 46 * 1024 * 1024
 BIG_LIMIT = 60 * 1024 * 1024
 DEALS = 4
@@ -160,7 +160,7 @@
 
 def near_kernel(
     g_ref, mom_ref, sec_ref, terms_ref, mom_out, sec_out, sum_ref,
-    whole, lhs, terms, mom, sec, sems, out_sems,
+    whole, lhs, terms, mom, sec, total_ref, sems, out_sems,
 ):
     here = place()
     rep, k, near = here[0], here[1], here[2]
@@ -202,7 +202,8 @@
         total += jnp.sum((way * way).reshape(rows // 8, 8, part), axis=0)
         put(mom.at[:, cols], mom_out.at[k, :, cols])
         put(sec.at[:, cols], sec_out.at[k, :, cols])
-    sum_ref[...] = total
+    total_ref[...] = total
+    put(total_ref, sum_ref)
     for copy in puts:
         copy.wait()
 
@@ -214,15 +215,16 @@
     return pl.pallas_call(
         near_kernel,
         in_specs=[VMEM, ANY, ANY],
-        out_specs=(ANY,) * 3 + (VMEM,),
+        out_specs=(ANY,) * 4,
         scratch_shapes=[
             pltpu.VMEM((size, size), BF16),
             pltpu.VMEM((rows, size), BF16),
             pltpu.VMEM((2, rows, size), BF16),
             pltpu.VMEM((rows, size), F32),
             pltpu.VMEM((rows, size), F32),
+            pltpu.VMEM((8, part), F32),
             pltpu.SemaphoreType.DMA((2,)),
-            pltpu.SemaphoreType.DMA((4 * reps,)),
+            pltpu.SemaphoreType.DMA((4 * reps + 1,)),
         ],
         out_shape=(shape((2, rows, size), BF16), state, state, shape((8, part), F32)),
         compiler_params=params(GRAM_LIMIT),
@@ -232,7 +234,7 @@
 
 
 def precond_kernel(
-    g_ref, l0_ref, l1_ref, l2_ref, l3_ref, right_ref, pieces, sum_ref, left, right, mixed, out, sems, out_sems
+    g_ref, l0_ref, l1_ref, l2_ref, l3_ref, right_ref, pieces, sum_ref, left, right, mixed, out, total_ref, sems, out_sems
 ):
     here = place()
     rep, k, step = here[0], here[1], here[3]
@@ -264,7 +266,8 @@
         for i in range(2):
             out[:, j, :, i * part : (i + 1) * part] = halves[:, i].astype(BF16)
         puts.append(load(out.at[:, j], pieces.at[:, j, :, pl.ds(0, 2 * part)], out_sems.at[j]))
-    sum_ref[...] = total
+    total_ref[...] = total
+    puts.append(load(total_ref, sum_ref, out_sems.at[reps]))
     for copy in puts:
         copy.wait()
 
@@ -276,14 +279,15 @@
     return pl.pallas_call(
         precond_kernel,
         in_specs=[VMEM] + [ANY] * 5,
-        out_specs=(ANY, VMEM),
+        out_specs=(ANY, ANY),
         scratch_shapes=[
             pltpu.VMEM((owners, half, size), BF16),
             pltpu.VMEM((size, size), BF16),
             pltpu.VMEM((owners * half, size), BF16),
             pltpu.VMEM((owners, reps, half // 2, 2 * part), BF16),
+            pltpu.VMEM((8, part), F32),
             pltpu.SemaphoreType.DMA((REPS + 2,)),
-            pltpu.SemaphoreType.DMA((reps,)),
+            pltpu.SemaphoreType.DMA((reps + 1,)),
         ],
         out_shape=(shape((owners, reps, half // 2, 2 * part + LANES), BF16), shape((8, part), F32)),
         compiler_params=params(MID_LIMIT),
@@ -342,7 +346,7 @@
 
 
 def late_kernel(
-    grad_hbm, mom_ref, sec_ref, own_ref, pre_ref, _, __, ___, mom_out, sec_out, pieces, grad_ref, mom, sec, pads, sems, out_sems
+    grad_hbm, mom_ref, sec_ref, own_hbm, pre_hbm, _, __, ___, mom_out, sec_out, pieces, grad_ref, mom, sec, pads, own_ref, pre_ref, sems, out_sems
 ):
     here = place()
     k = 1 - here[1]
@@ -356,6 +360,10 @@
         return ref.at[k, pl.ds(n * chunk * row_part, chunk * row_part)]
 
     get_grad = load(grad_hbm, grad_ref, sems.at[2 * steps])
+    get_sums = [
+        load(own_hbm, own_ref, sems.at[2 * steps + 1]),
+        load(pre_hbm, pre_ref, sems.at[2 * steps + 2]),
+    ]
     loads = []
     for n in range(steps):
         for i, (src, dst) in enumerate(((mom_ref, mom), (sec_ref, sec))):
@@ -381,6 +389,8 @@
             copy = pltpu.make_async_copy(src.at[n], block(dst, n), out_sems.at[2 * n + i])
             copy.start()
             stores.append(copy)
+    for copy in get_sums:
+        copy.wait()
     own, other = jnp.sum(own_ref[...]), jnp.sum(total)
     even = here[1] == 0
     values = (jnp.where(even, own, other), jnp.where(even, other, own), jnp.sum(pre_ref[...]))
@@ -405,14 +415,16 @@
     state = shape(moment.shape, F32)
     return pl.pallas_call(
         late_kernel,
-        in_specs=[ANY, ANY, ANY, VMEM, VMEM, ANY, ANY, ANY],
+        in_specs=[ANY] * 8,
         out_specs=(ANY,) * 3,
         scratch_shapes=[
             pltpu.VMEM(grad.shape, BF16),
             pltpu.VMEM((steps, rows // steps, size), F32),
             pltpu.VMEM((steps, rows // steps, size), F32),
             pltpu.VMEM(pieces.shape[:3] + (LANES,), BF16),
-            pltpu.SemaphoreType.DMA((2 * steps + 1,)),
+            pltpu.VMEM(own_sq.shape, F32),
+            pltpu.VMEM(pre_sq.shape, F32),
+            pltpu.SemaphoreType.DMA((2 * steps + 3,)),
             pltpu.SemaphoreType.DMA((2 * steps + 1,)),
         ],
         out_shape=(state, state, shape(pieces.shape, BF16)),
@@ -458,7 +470,8 @@
     )(terms, gram_right, gram_left, right_new, left_new)
 
 
-def finish_kernel(cells, slot_ref, in_ref, out_hbm, ratios, out_ref, sems):
+def finish_kernel(cells, slot_hbm, in_ref, out_hbm, ratios, out_ref, slot_ref, sems):
+    get_slots = load(slot_hbm, slot_ref, sems.at[DEALS])
     rows = in_ref.shape[1]
     part = (in_ref.shape[2] - LANES) // 2
     sums = in_ref[:, :, 2 * part :].astype(F32).reshape(-1, REPS, rows, LANES)
@@ -482,6 +495,7 @@
 
     chunk = out_ref.shape[0] // DEALS
     puts = []
+    get_slots.wait()
     for n in range(DEALS):
         lax.fori_loop(n * chunk, (n + 1) * chunk, place_block, 0, unroll=16)
         part_of = pl.ds(n * chunk, chunk)
@@ -497,12 +511,13 @@
     return pl.pallas_call(
         functools.partial(finish_kernel, float(size * size)),
         out_shape=shape((blocks, 4 * rows, part), BF16),
-        in_specs=[SMEM, VMEM],
+        in_specs=[ANY, VMEM],
         out_specs=ANY,
         scratch_shapes=[
             pltpu.VMEM((blocks // 2, 2, rows, LANES), F32),
             pltpu.VMEM((blocks, 4 * rows, part), BF16),
-            pltpu.SemaphoreType.DMA((DEALS,)),
+            pltpu.SMEM((blocks,), jnp.int32),
+            pltpu.SemaphoreType.DMA((DEALS + 1,)),
         ],
         compiler_params=params(),
         cost_estimate=cost(8 * blocks * rows * part, 20 * blocks * rows * part),

time: 92.2 us -> 91.9 us (level)
  local copies, waits for them, and re-layouts: 0.07 us -> 3.87 us
  Pallas kernels: 24.8 us -> 23.2 us
  waiting for transfers between devices: 41.5 us -> 40 us
  starting transfers between devices: 24.6 us -> 23.6 us
    unnamed x10 -> x12, local copies, waits for them, and re-layouts: 0.03 us -> 3.83 us
    ppermute x5, waiting for transfers between devices: 1.5 us -> 0.01 us  [to_neighbour(): return lax.ppermute(x, ('fsdp', 'rep'), pairs)]
    pallas_call x1, Pallas kernels: 4.37 us -> 3.11 us  [near_terms(): pl.pallas_call(near_kernel, in_specs=[VMEM, ANY, ANY], out_specs=(ANY,) *...]
    all_to_all x2, starting transfers between devices: 20.7 us -> 19.6 us  [everyone(): lax.all_to_all(x, ('fsdp', 'rep'), split_axis=0, concat_axis=0, tiled=True)]
  transfers between devices with their start and end apart: 7 -> 7, of which waited for: 3 -> 2; matrix products, arithmetic and copies ran while one was open for 0% -> 0% of each run, Pallas kernels for 22% -> 21%
where the time goes in v7:
time: 91.9 us; the launch traced here: 91.5 us
  waiting for transfers between devices  40 us (44%)
  starting transfers between devices  23.6 us (26%)
  Pallas kernels  23.2 us (25%)
  local copies, waits for them, and re-layouts  3.87 us (4%)
    all_to_all x2, waiting for transfers between devices, everyone(): lax.all_to_all(x, ('fsdp', 'rep'), split_axis=0, concat_axis=0, tiled=True)  40 us
    all_to_all x2, starting transfers between devices, everyone(): lax.all_to_all(x, ('fsdp', 'rep'), split_axis=0, concat_axis=0, tiled=True)  19.6 us
    pallas_call x1, Pallas kernels, grams(): pl.pallas_call(gram_kernel, in_specs=[ANY] * 3, out_specs=(ANY,) * 2, scr...  4.55 us
    pallas_call x1, Pallas kernels, precond(): pl.pallas_call(precond_kernel, in_specs=[VMEM] + [ANY] * 5, out_specs=(AN...  4 us
    ppermute x5, starting transfers between devices, to_neighbour(): return lax.ppermute(x, ('fsdp', 'rep'), pairs)  3.98 us
    unnamed x12, local copies, waits for them, and re-layouts  3.83 us
    pallas_call x1, Pallas kernels, add(): pl.pallas_call(add_kernel, in_specs=[ANY] * 5, out_specs=(ANY, ANY), out_...  3.33 us
    pallas_call x1, Pallas kernels, near_terms(): pl.pallas_call(near_kernel, in_specs=[VMEM, ANY, ANY], out_specs=(ANY,) *...  3.11 us
  transfers between devices with their start and end apart: 7, of which 2 were waited for; matrix products, arithmetic and copies ran while one was open for 0% of the time, Pallas kernels for 21%

profile of v7, /device:TPU:1, one launch (start us, length us, event | category | flops | bytes accessed | tf_op | source)
XLA Modules:
  0.0 91.5 jit_solution(9193627334378414374)
XLA Ops:
  0.6 2.6 %deal_blocks.1 = bf16[128,32,256]{2,1,0:T(8,128)(2,1)} custom-call(s32[64]{0:T(128)} %slot_hbm.3, bf16[64,32,256]{2,1,0:T(8,128)(2,1)} %grads_ref.1), custom_call_target="tpu_custom_call" | custom-call | bytes 3145728 | tf_op jit(solution)/shard_map/deal_blocks/pallas_call | solution.py:110
  3.3 11.5 %all-to-all-start = ((bf16[128,32,256]{2,1,0:T(8,128)(2,1)}), bf16[128,32,256]{2,1,0:T(8,128)(2,1)S(1)}, u32[]{:S(2)}, u32[]{:S(2)}) async-start(bf16[128,32,256]{2,1,0:T(8,128)(2,1)} %deal_blocks.1), calls=%async_computation | async-start | bytes 4194304 | tf_op jit(solution)/shard_map/all_to_all | solution.py:65
  14.8 1.9 %share_rows.1 = (bf16[8,16,1024]{2,1,0:T(8,128)(2,1)}, bf16[8,16,1024]{2,1,0:T(8,128)(2,1)}, bf16[8,16,1024]{2,1,0:T(8,128)(2,1)}) custom-call(bf16[2,8,2,16,1024]{4,3,2,1,0:T(8,128)(2,1)} %bitcast.7), custom_call_target="tpu_custom_call" | custom-call | bytes 1572864 | tf_op jit(solution)/shard_map/share_rows/pallas_call | solution.py:145
  16.7 2.7 %collective-permute-start.1 = (bf16[8,16,1024]{2,1,0:T(8,128)(2,1)}, bf16[8,16,1024]{2,1,0:T(8,128)(2,1)S(1)}, u32[]{:S(2)}, u32[]{:S(2)}) collective-permute-start(bf16[8,16,1024]{2,1,0:T(8,128)(2,1)} %get-tuple-element.28), channel_id=1, source_target_pairs={{0,1},{1,2},{2,3},{3,0},{4,7},{5,4},{6,5},{7,6},{8,9},{9,10},{10,1... | collective-permute-start | bytes 786440 | tf_op jit(solution)/shard_map/ppermute | solution.py:61
  19.4 0.5 collective-permute-start.2
  19.9 0.6 collective-permute-start.3
  20.5 25.4 %all-to-all-done = bf16[128,32,256]{2,1,0:T(8,128)(2,1)S(1)} async-done(((bf16[128,32,256]{2,1,0:T(8,128)(2,1)}), bf16[128,32,256]{2,1,0:T(8,128)(2,1)S(1)}, u32[]{:S(2)}, u32[]{:S(2)}) %all-to-all-start) | async-done | bytes 2097184 | tf_op jit(solution)/shard_map/all_to_all | solution.py:65
  45.9 0.0 copy-start
  45.9 0.1 collective-permute-start
  46.0 0.0 copy-start.1
  46.0 2.2 %copy-done.1 = f32[2,256,1024]{2,1,0:T(8,128)S(1)} copy-done((f32[2,256,1024]{2,1,0:T(8,128)S(1)}, f32[2,256,1024]{2,1,0:T(8,128)}, u32[]{:S(2)}) %copy-start.1) | copy-done | bytes 2097176
  48.2 1.6 %copy-done.2 = f32[2,256,1024]{2,1,0:T(8,128)S(1)} copy-done((f32[2,256,1024]{2,1,0:T(8,128)S(1)}, f32[2,256,1024]{2,1,0:T(8,128)}, u32[]{:S(2)}) %copy-start.2) | copy-done | bytes 2097176
  49.8 3.1 %near_terms.1 = (bf16[2,256,1024]{2,1,0:T(8,128)(2,1)}, f32[2,256,1024]{2,1,0:T(8,128)}, f32[2,256,1024]{2,1,0:T(8,128)}, f32[8,256]{1,0:T(8,128)S(1)}) custom-call(bf16[32,4,32,256]{3,2,1,0:T(8,128)(2,1)S(1)} %bitcast.4, f32[2,256,1024]{2,1,0:T(8,128)S(1)} %copy-done.1, f32[2,256,1024]{2,1,0:T(8,128)S(1)} %copy-done.2), custom_call_target="tpu_custom_call" | custom-call | flops 1 | bytes 1 | tf_op jit(solution)/shard_map/near_terms/pallas_call | solution.py:215
  52.9 0.0 copy-start.3
  53.0 0.1 collective-permute-start.4
  53.0 0.0 collective-permute-done.1.l1_ref
  53.0 0.0 collective-permute-done.2.l2_ref
  53.1 0.0 collective-permute-done.3.l3_ref
  53.1 0.0 copy-done
  53.1 0.0 copy-done.4
  53.1 4.0 %precond_rows.1 = (bf16[32,4,8,640]{3,2,1,0:T(8,128)(2,1)}, f32[8,256]{1,0:T(8,128)S(1)}) custom-call(bf16[32,4,32,256]{3,2,1,0:T(8,128)(2,1)S(1)} %bitcast.5, bf16[2,8,2,16,1024]{4,3,2,1,0:T(8,128)(2,1)S(1)} %bitcast.8, bf16[8,16,1024]{2,1,0:T(8,128)(2,1)S(1)} %collective-permute-done.1.l1_ref, bf16[8,16,1024]{2,1,0:T(8,128)(2,1)S(1)} %collective-permute-done.2.l2_ref, ...), custom_call_target="tpu_custom_call" | custom-call | flops 99999997952 | bytes 1000000 | tf_op jit(solution)/shard_map/precond_rows/pallas_call | solution.py:279
  57.1 0.0 collective-permute-done.grad_hbm
  57.1 0.0 copy-done.3
  57.1 2.0 %other_adam.1 = (f32[2,256,1024]{2,1,0:T(8,128)}, f32[2,256,1024]{2,1,0:T(8,128)}, bf16[32,4,8,640]{3,2,1,0:T(8,128)(2,1)}) custom-call(bf16[8,4,32,256]{3,2,1,0:T(8,128)(2,1)S(1)} %collective-permute-done.grad_hbm, f32[2,256,1024]{2,1,0:T(8,128)S(1)} %copy-done.1, ...), custom_call_target="tpu_custom_call", output_to_operand_aliasing={{0}: (5, {}), {1}: (6, {}), {2}: (7, {})} | custom-call | flops 3932160 | bytes 5242880 | tf_op jit(solution)/shard_map/other_adam/pallas_call | solution.py:416
  59.2 8.1 %all-to-all-start.1 = ((bf16[128,8,640]{2,1,0:T(8,128)(2,1)}), bf16[128,8,640]{2,1,0:T(8,128)(2,1)S(1)}, u32[]{:S(2)}, u32[]{:S(2)}) async-start(bf16[128,8,640]{2,1,0:T(8,128)(2,1)} %bitcast.2), calls=%async_computation.1 | async-start | bytes 2621440 | tf_op jit(solution)/shard_map/all_to_all | solution.py:65
  67.2 4.5 %own_grams.1 = (f32[2,256,1024]{2,1,0:T(8,128)}, f32[2,256,1024]{2,1,0:T(8,128)}) custom-call(bf16[32,4,32,256]{3,2,1,0:T(8,128)(2,1)} %bitcast.6, f32[2,256,1024]{2,1,0:T(8,128)} %left_ref.1, f32[2,256,1024]{2,1,0:T(8,128)} %right_ref.3), custom_call_target="tpu_custom_call" | custom-call | flops 99999997952 | bytes 1000000 | tf_op jit(solution)/shard_map/own_grams/pallas_call | solution.py:330
  71.8 0.0 collective-permute-done.4.terms_ref
  71.8 0.0 copy-start.5
  71.8 3.3 %add_terms.1 = (f32[2,256,1024]{2,1,0:T(8,128)}, f32[2,256,1024]{2,1,0:T(8,128)}) custom-call(bf16[2,256,1024]{2,1,0:T(8,128)(2,1)} %collective-permute-done.4.terms_ref, f32[2,256,1024]{2,1,0:T(8,128)} %right_ref.3, f32[2,256,1024]{2,1,0:T(8,128)} %left_ref.1, f32[2,256,1024]{2,1,0:T(8,128)} %get-tuple-element.39._, ...), custom_call_target="tpu_custom_call", output_to_operand_aliasing={{0}: (3, {}), {1}: (4, {})} | custom-call | flops 1 | bytes 1 | tf_op jit(solution)/shard_map/add_terms/pallas_call | solution.py:455
  75.2 14.6 %all-to-all-done.1.in_ref = bf16[128,8,640]{2,1,0:T(8,128)(2,1)S(1)} async-done(((bf16[128,8,640]{2,1,0:T(8,128)(2,1)}), bf16[128,8,640]{2,1,0:T(8,128)(2,1)S(1)}, u32[]{:S(2)}, u32[]{:S(2)}) %all-to-all-start.1) | async-done | bytes 1310752 | tf_op jit(solution)/shard_map/all_to_all | solution.py:65
  89.8 0.0 copy-done.5
  89.8 1.7 %finish_updates.1 = bf16[64,32,256]{2,1,0:T(8,128)(2,1)} custom-call(s32[64]{0:T(128)S(1)} %copy-done.5, bf16[128,8,640]{2,1,0:T(8,128)(2,1)S(1)} %all-to-all-done.1.in_ref), custom_call_target="tpu_custom_call" | custom-call | flops 1048576 | bytes 2621440 | tf_op jit(solution)/shard_map/finish_updates/pallas_call | solution.py:511
  (3 shorter events, 0.0 us)
Async XLA Ops:
  3.3 42.6 %all-to-all-start = ((bf16[128,32,256]{2,1,0:T(8,128)(2,1)}), bf16[128,32,256]{2,1,0:T(8,128)(2,1)S(1)}, u32[]{:S(2)}, u32[]{:S(2)}) async-start(bf16[128,32,256]{2,1,0:T(8,128)(2,1)} %deal_blocks.1), calls=%async_computation | async-start | bytes 4194304 | tf_op jit(solution)/shard_map/all_to_all | solution.py:65
  16.7 36.4 %collective-permute-start.1 = (bf16[8,16,1024]{2,1,0:T(8,128)(2,1)}, bf16[8,16,1024]{2,1,0:T(8,128)(2,1)S(1)}, u32[]{:S(2)}, u32[]{:S(2)}) collective-permute-start(bf16[8,16,1024]{2,1,0:T(8,128)(2,1)} %get-tuple-element.28), channel_id=1, source_target_pairs={{0,1},{1,2},{2,3},{3,0},{4,7},{5,4},{6,5},{7,6},{8,9},{9,10},{10,1... | collective-permute-start | bytes 786440 | tf_op jit(solution)/shard_map/ppermute | solution.py:61
  19.4 33.7 %collective-permute-start.2 = (bf16[8,16,1024]{2,1,0:T(8,128)(2,1)}, bf16[8,16,1024]{2,1,0:T(8,128)(2,1)S(1)}, u32[]{:S(2)}, u32[]{:S(2)}) collective-permute-start(bf16[8,16,1024]{2,1,0:T(8,128)(2,1)} %get-tuple-element.29), channel_id=1, source_target_pairs={{0,2},{1,3},{2,0},{3,1},{4,6},{5,7},{6,4},{7,5},{8,10},{9,11},{10,... | collective-permute-start | bytes 786440 | tf_op jit(solution)/shard_map/ppermute | solution.py:61
  19.9 33.2 %collective-permute-start.3 = (bf16[8,16,1024]{2,1,0:T(8,128)(2,1)}, bf16[8,16,1024]{2,1,0:T(8,128)(2,1)S(1)}, u32[]{:S(2)}, u32[]{:S(2)}) collective-permute-start(bf16[8,16,1024]{2,1,0:T(8,128)(2,1)} %get-tuple-element.30), channel_id=1, source_target_pairs={{0,3},{1,0},{2,1},{3,2},{4,5},{5,6},{6,7},{7,4},{8,11},{9,8},{10,9... | collective-permute-start | bytes 786440 | tf_op jit(solution)/shard_map/ppermute | solution.py:61
  45.9 7.2 %copy-start = (bf16[128,32,256]{2,1,0:T(8,128)(2,1)}, bf16[128,32,256]{2,1,0:T(8,128)(2,1)S(1)}, u32[]{:S(2)}) copy-start(bf16[128,32,256]{2,1,0:T(8,128)(2,1)S(1)} %all-to-all-done) | copy-start | bytes 6291460
  45.9 11.2 %collective-permute-start = (bf16[8,4,32,256]{3,2,1,0:T(8,128)(2,1)S(1)}, bf16[8,4,32,256]{3,2,1,0:T(8,128)(2,1)S(1)}, u32[]{:S(2)}, u32[]{:S(2)}) collective-permute-start(bf16[8,4,32,256]{3,2,1,0:T(8,128)(2,1)S(1)} %constant_dynamic-slice_fusion), channel_id=1, source_target_pairs={{0,1},{1,2},{2,3},{3,0},{4,7},{5,4},{6,5},{7,6},{8,9},{9,10},{10,1... | collective-permute-start | bytes 1572872 | tf_op jit(solution)/shard_map/ppermute | solution.py:61
  46.0 2.2 %copy-start.1 = (f32[2,256,1024]{2,1,0:T(8,128)S(1)}, f32[2,256,1024]{2,1,0:T(8,128)}, u32[]{:S(2)}) copy-start(f32[2,256,1024]{2,1,0:T(8,128)} %mom_ref.3) | copy-start | bytes 6291460
  48.2 1.6 %copy-start.2 = (f32[2,256,1024]{2,1,0:T(8,128)S(1)}, f32[2,256,1024]{2,1,0:T(8,128)}, u32[]{:S(2)}) copy-start(f32[2,256,1024]{2,1,0:T(8,128)} %sec_ref.3) | copy-start | bytes 6291460
  49.8 3.3 %copy-start.4 = (bf16[2,256,1024]{2,1,0:T(8,128)(2,1)S(1)}, bf16[2,256,1024]{2,1,0:T(8,128)(2,1)}, u32[]{:S(2)}) copy-start(bf16[2,256,1024]{2,1,0:T(8,128)(2,1)} %param.12) | copy-start | bytes 3145732
  52.9 4.2 %copy-start.3 = (f32[2,256,1024]{2,1,0:T(8,128)S(1)}, f32[2,256,1024]{2,1,0:T(8,128)}, u32[]{:S(2)}) copy-start(f32[2,256,1024]{2,1,0:T(8,128)} %sec_ref.3) | copy-start | bytes 6291460
  53.0 18.9 %collective-permute-start.4 = (bf16[2,256,1024]{2,1,0:T(8,128)(2,1)}, bf16[2,256,1024]{2,1,0:T(8,128)(2,1)}, u32[]{:S(2)}, u32[]{:S(2)}) collective-permute-start(bf16[2,256,1024]{2,1,0:T(8,128)(2,1)} %get-tuple-element.37), channel_id=1, source_target_pairs={{0,1},{1,2},{2,3},{3,0},{4,7},{5,4},{6,5},{7,6},{8,9},{9,10},{10,1... | collective-permute-start | bytes 3145736 | tf_op jit(solution)/shard_map/ppermute | solution.py:61
  59.2 30.7 %all-to-all-start.1 = ((bf16[128,8,640]{2,1,0:T(8,128)(2,1)}), bf16[128,8,640]{2,1,0:T(8,128)(2,1)S(1)}, u32[]{:S(2)}, u32[]{:S(2)}) async-start(bf16[128,8,640]{2,1,0:T(8,128)(2,1)} %bitcast.2), calls=%async_computation.1 | async-start | bytes 2621440 | tf_op jit(solution)/shard_map/all_to_all | solution.py:65
  71.8 18.0 %copy-start.5 = (s32[64]{0:T(128)S(1)}, s32[64]{0:T(128)}, u32[]{:S(2)}) copy-start(s32[64]{0:T(128)} %slot_hbm.3) | copy-start | bytes 772
